TPU v7x, 256 devices: a whole 4x4x8 slice. The times are simulated.
256 devices in a mesh: pb: 64 (over x_hi, y, z), ka: 4 (over x_lo, core).
Axes of the slice: x: 4 (x_hi: 2, x_lo: 2; x = x_hi * 2 + x_lo), y: 4, z: 8, core: 2. Of those that a mesh axis runs over, the one named last changes fastest.
Arguments:
- queries: bfloat16 [32768, 1024], P('pb'), may hold values from -9 to 9
- keys: bfloat16 [8, 4096, 128], P(None, 'ka'), may hold values from -6 to 6
- values: bfloat16 [8, 4096, 128], P(None, 'ka'), may hold values from -6 to 6
- grad_out: bfloat16 [32768, 1024], P('pb'), may hold values from -6 to 6
- query_blocks: int32 [128], P('pb'), may hold values from 0 to 15, as said below
Outputs:
- grad_queries: bfloat16 [32768, 1024], P(('pb', 'ka'))
- grad_keys: bfloat16 [8, 4096, 128], P('ka', 'pb')
- grad_values: bfloat16 [8, 4096, 128], P('ka', 'pb')
Inputs may be any that keep to these rules, and one draw needn't show every extreme that they name: `query_blocks`: for each key and value head g, the two entries at index pb = g * 8 + l are a sequence block b and its mirror 2 * 8 - 1 - b, in either order; every block appears once among the head's entries.
All inputs are finite; a program needn't handle non-finite values.
Results may differ from a plain program's by a relative error of at most 0.0059.
Values sent between devices are 32-bit elements; how exact they have to be, the bound alone decides.
No kernel may reach another device: no remote copies, remote signals or barrier semaphores. Data moves between devices by JAX's collectives and lax.ppermute only.
A program may use at most 128 MiB of HBM per device.

v0:
```python
import jax
import jax.numpy as jnp
from jax import lax
from jax.sharding import PartitionSpec as P

NEG = -1e30


def stat_update(query_part, grad_part, pos_part, key_tile, value_tile, kpos_tile, current, scale):
    run_max, run_sum, run_dot = current
    scores = (
        jnp.einsum("rd,kd->rk", query_part, key_tile, preferred_element_type=jnp.float32) * scale
    )
    visible = kpos_tile[None, :] <= pos_part[:, None]
    new_max = jnp.maximum(run_max, jnp.max(jnp.where(visible, scores, NEG), axis=1))
    factor = jnp.exp(run_max - new_max)
    weights = jnp.where(visible, jnp.exp(scores - new_max[:, None]), 0.0)
    slopes = jnp.einsum("rd,kd->rk", grad_part, value_tile, preferred_element_type=jnp.float32)
    new_sum = run_sum * factor + jnp.sum(weights, axis=1)
    new_dot = run_dot * factor + jnp.sum(weights * slopes, axis=1)
    return (new_max, new_sum, new_dot)


def grad_update(
    query_part, grad_part, pos_part, key_tile, value_tile, kpos_tile, lse_part, delta_part, scale
):
    scores = (
        jnp.einsum("rd,kd->rk", query_part, key_tile, preferred_element_type=jnp.float32) * scale
    )
    visible = kpos_tile[None, :] <= pos_part[:, None]
    probs = jnp.where(visible, jnp.exp(scores - lse_part[:, None]), 0.0)
    slopes = jnp.einsum("rd,kd->rk", grad_part, value_tile, preferred_element_type=jnp.float32)
    score_grads = (probs * (slopes - delta_part[:, None]) * scale).astype(jnp.bfloat16)
    probs_low = probs.astype(jnp.bfloat16)
    query_term = jnp.dot(score_grads, key_tile, preferred_element_type=jnp.float32)
    key_term = jnp.einsum("rk,rd->kd", score_grads, query_part, preferred_element_type=jnp.float32)
    value_term = jnp.einsum("rk,rd->kd", probs_low, grad_part, preferred_element_type=jnp.float32)
    return (query_term, key_term, value_term)


def on_device(queries, keys, values, grad_out, query_blocks):
    width = keys.shape[2]
    head_count = keys.shape[0]
    heads = queries.shape[1] // width
    query_count = queries.shape[0]
    query_block = query_count // 2
    key_count = keys.shape[1]
    key_block = key_count // 2
    scale = width ** (-0.5)
    pb_size = lax.axis_size("pb")
    per_head = pb_size // head_count
    owner = lax.axis_index("pb") // per_head
    own_keys = lax.dynamic_index_in_dim(keys, owner, 0, keepdims=False)
    own_values = lax.dynamic_index_in_dim(values, owner, 0, keepdims=False)
    ka_size = lax.axis_size("ka")
    ka_index = lax.axis_index("ka")
    query_pos = (
        query_blocks[:, None] * query_block + jnp.arange(query_block, dtype=jnp.int32)[None, :]
    ).reshape(query_count)
    key_starts = jnp.stack([ka_index, 2 * ka_size - 1 - ka_index])
    key_pos = (
        key_starts[:, None] * key_block + jnp.arange(key_block, dtype=jnp.int32)[None, :]
    ).reshape(key_count)
    groups = 1
    row_count = query_count * heads // groups
    query_rows = queries.reshape(groups, row_count, width)
    grad_rows = grad_out.reshape(groups, row_count, width)
    pos_rows = jnp.broadcast_to(query_pos[:, None], (query_count, heads)).reshape(groups, row_count)
    tile_size = 512
    per_block = key_block // tile_size
    key_tiles = own_keys.reshape(2, per_block, tile_size, width)
    value_tiles = own_values.reshape(2, per_block, tile_size, width)
    kpos_tiles = key_pos.reshape(2, per_block, tile_size)

    def stat_step(state, pieces):
        key_tile, value_tile, kpos_tile = pieces
        group = 0
        current = (state[0][group], state[1][group], state[2][group])

        def stat_active(present, group=group):
            return stat_update(
                query_rows[group],
                grad_rows[group],
                pos_rows[group],
                key_tile,
                value_tile,
                kpos_tile,
                present,
                scale,
            )

        current = stat_active(current)
        results = [current]
        stacked = tuple((jnp.stack([entry[member] for entry in results]) for member in range(3)))
        return (stacked, None)

    start_state = (
        jnp.full((groups, row_count), NEG, jnp.float32),
        jnp.zeros((groups, row_count), jnp.float32),
        jnp.zeros((groups, row_count), jnp.float32),
    )
    flat_tiles = (
        key_tiles.reshape(2 * per_block, tile_size, width),
        value_tiles.reshape(2 * per_block, tile_size, width),
        kpos_tiles.reshape(2 * per_block, tile_size),
    )
    state, _ = lax.scan(stat_step, start_state, flat_tiles)
    top = lax.pmax(state[0], "ka")
    factor = jnp.exp(state[0] - top)
    total, dotted = lax.psum((state[1] * factor, state[2] * factor), "ka")
    lse = top + jnp.log(total)
    delta = dotted / total

    def grad_step(query_acc, pieces):
        key_tile, value_tile, kpos_tile = pieces
        group = 0

        def grad_active(present, group=group):
            query_term, key_term, value_term = grad_update(
                query_rows[group],
                grad_rows[group],
                pos_rows[group],
                key_tile,
                value_tile,
                kpos_tile,
                lse[group],
                delta[group],
                scale,
            )
            return (present + query_term, key_term, value_term)

        outcome = grad_active(query_acc[group])
        new_acc = [outcome[0]]
        key_sum = outcome[1]
        value_sum = outcome[2]
        return (jnp.stack(new_acc), (key_sum, value_sum))

    query_acc = jnp.zeros((groups, row_count, width), jnp.float32)
    key_terms = []
    value_terms = []
    zero_index = jnp.int32(0)
    for block in range(2):
        query_acc, (key_part, value_part) = lax.scan(
            grad_step, query_acc, (key_tiles[block], value_tiles[block], kpos_tiles[block])
        )
        key_part = key_part.reshape(key_block, 1, width)
        value_part = value_part.reshape(key_block, 1, width)
        key_terms.append(key_part)
        value_terms.append(value_part)
    blank = jnp.zeros((2, key_block, head_count, width), jnp.float32)
    key_full = lax.dynamic_update_slice(
        blank, jnp.stack(key_terms), (zero_index, zero_index, owner, zero_index)
    ).reshape(2, key_block * head_count, width)
    value_full = lax.dynamic_update_slice(
        blank, jnp.stack(value_terms), (zero_index, zero_index, owner, zero_index)
    ).reshape(2, key_block * head_count, width)
    key_result, value_result = (
        lax.psum_scatter(key_full, "pb", scatter_dimension=1, tiled=True),
        lax.psum_scatter(value_full, "pb", scatter_dimension=1, tiled=True),
    )
    query_share = lax.psum_scatter(
        query_acc.reshape(query_count, heads * width), "ka", scatter_dimension=0, tiled=True
    )
    return (
        query_share.astype(jnp.bfloat16),
        key_result.astype(jnp.bfloat16),
        value_result.astype(jnp.bfloat16),
    )


def solution(mesh):
    placed = (P("pb", None), P(None, "ka", None), P(None, "ka", None), P("pb", None), P("pb"))
    return jax.shard_map(
        on_device,
        mesh=mesh,
        in_specs=placed,
        out_specs=(P(("pb", "ka"), None), P("ka", "pb", None), P("ka", "pb", None)),
        check_vma=False,
    )
```

profile of v0, /device:TPU:64, one launch (start us, length us, event | category | flops | bytes accessed | tf_op | source)
XLA Modules:
  0.0 845.4 jit_solution(2019157731298510534)
XLA Ops:
  7.3 1.5 squeeze_reshape.23
  8.8 1.9 squeeze_reshape.28
  10.7 1.5 squeeze_reshape.24
  12.2 2.3 squeeze_reshape.27
  15.1 1.9 constant_dynamic-slice_fusion.1
  16.9 15.9 %while.4 = (s32[]{:T(128)}, f32[1,4096]{1,0:T(1,128)S(1)}, f32[1,4096]{1,0:T(1,128)S(1)}, f32[1,4096]{1,0:T(1,128)S(1)}, s32[2,512]{1,0:T(2,128)S(1)}, /*index=5...) while((s32[]{:T(128)}, f32[1,4096]{1,0:T(1,128)S(1)}, ...), condition=%wide.wide.region_4.5_spmd.clone, body=%wide.wide.region_0.4_spmd.clone.sunk | while | flops 1105240064 | bytes 33255644 | solution.py:107
  17.3 2.3 fusion.75
  19.6 2.9 fusion.76
  22.5 2.2 fusion.78
  25.2 2.3 fusion.75
  27.6 2.9 fusion.76
  30.5 2.2 fusion.78
  32.8 11.2 %pmax.7 = f32[1,4096]{1,0:T(1,128)S(1)} all-reduce(f32[1,4096]{1,0:T(1,128)S(1)} %get-tuple-element.117), channel_id=1, replica_groups=mesh['pb'=64,'ka'=4] {'ka'}, use_global_device_ids=true, to_apply=%region_5.6 | all-reduce | flops 4096 | bytes 32768 | tf_op jit(solution)/shard_map/pmax | solution.py:108
  44.1 10.5 %all-reduce = (f32[1,4096]{1,0:T(1,128)S(1)}, f32[1,4096]{1,0:T(1,128)S(1)}) all-reduce(f32[1,4096]{1,0:T(1,128)S(1)} %get-tuple-element.195, f32[1,4096]{1,0:T(1,128)S(1)} %get-tuple-element.194), channel_id=1, replica_groups=mesh['pb'=64,'ka'=4] {'ka'}, use_global_device_ids=true, to_apply=%region_6.7 | all-reduce | flops 8192 | bytes 65536 | tf_op jit(solution)/shard_map/psum | solution.py:110
  54.6 2.9 bitcast_select_fusion.1
  57.6 3.1 bitcast_select_fusion
  60.7 2.4 fusion.18
  63.1 2.3 fusion.20
  65.4 2.4 fusion.31
  67.8 2.2 convolution_add_fusion
  70.0 1.5 reshape.93
  71.9 4.6 fusion.28
  76.5 4.6 fusion.25
  81.2 2.2 broadcast_in_dim.45.clone.1
  83.4 15.2 %dynamic_update_slice.16 = f32[2,512,8,128]{3,2,1,0:T(8,128)} dynamic-update-slice(f32[2,512,8,128]{3,2,1,0:T(8,128)} %broadcast_in_dim.45.clone.1, f32[2,512,1,128]{3,2,1,0:T(1,128)S(1)} %bitcast.137, s32[]{:T(128)} %constant.86.clone.1, s32[]{:T(128)} %constant.86.clone.1, s32[]{:T(128)S(6)} %select_n.28, s32[]{:T(128)} %constant.86.clone.1) | dynamic-update-slice | bytes 1048580 | tf_op jit(solution)/shard_map/dynamic_update_slice | solution.py:154
  98.7 3.5 convolution_bitcast_fusion
  102.1 3.5 convolution_bitcast_fusion.1
  105.7 2.2 broadcast_in_dim.45.clone
  107.9 15.1 %dynamic_update_slice.15 = f32[2,512,8,128]{3,2,1,0:T(8,128)} dynamic-update-slice(f32[2,512,8,128]{3,2,1,0:T(8,128)} %broadcast_in_dim.45.clone, f32[2,512,1,128]{3,2,1,0:T(1,128)S(1)} %bitcast.136, s32[]{:T(128)} %constant.86.clone.1, s32[]{:T(128)} %constant.86.clone.1, s32[]{:T(128)S(6)} %select_n.28, s32[]{:T(128)} %constant.86.clone.1) | dynamic-update-slice | bytes 1048580 | tf_op jit(solution)/shard_map/dynamic_update_slice | solution.py:151
  123.0 1.8 convert_element_type.27
  124.8 347.6 %reduce-scatter.8.cloned.1.call-done = f32[2,64,128]{2,1,0:T(8,128)} async-done(((f32[2,4096,128]{2,1,0:T(8,128)}), f32[2,64,128]{2,1,0:T(8,128)}) %reduce-scatter.8.cloned.1.call-update) | async-done | bytes 65552 | tf_op jit(solution)/shard_map/reduce_scatter | solution.py:159
  473.9 363.5 %reduce-scatter.6.cloned.1.call-done = f32[2,64,128]{2,1,0:T(8,128)} async-done(((f32[2,4096,128]{2,1,0:T(8,128)}), f32[2,64,128]{2,1,0:T(8,128)}) %reduce-scatter.6.cloned.1.call-update) | async-done | bytes 65552 | tf_op jit(solution)/shard_map/reduce_scatter | solution.py:158
  (62 shorter events, 4.9 us)
Async XLA Ops:
  7.2 7.4 copy-start.8
  7.2 115.8 %reduce-scatter.4.cloned.1.call-start = ((), (), s32[]{:S(2)}) async-start(), calls=%async_computation.3 | async-start | bytes 2621440 | tf_op jit(solution)/shard_map/reduce_scatter | solution.py:161
  8.8 48.8 %copy-start.4 = (bf16[4096,128]{1,0:T(8,128)(2,1)}, bf16[4096,128]{1,0:T(8,128)(2,1)S(1)}, u32[]{:S(2)}) copy-start(bf16[4096,128]{1,0:T(8,128)(2,1)S(1)} %squeeze_reshape.23) | copy-start | bytes 3145732
  17.2 2.4 copy-start.6
  17.2 2.4 copy-start.7
  25.2 2.4 copy-start.6
  25.2 2.4 copy-start.7
  57.5 5.5 copy-start
  60.7 4.8 copy-start.1
  63.0 4.8 copy-start.2
  65.4 2.4 copy-start.3
  71.6 400.8 %reduce-scatter.8.cloned.1.call-start = ((), (), s32[]{:S(2)}) async-start(), calls=%async_computation.5 | async-start | bytes 4259840 | tf_op jit(solution)/shard_map/reduce_scatter | solution.py:159
  81.1 17.5 %copy-start.5 = (bf16[4096,128]{1,0:T(8,128)(2,1)S(1)}, bf16[4096,128]{1,0:T(8,128)(2,1)}, u32[]{:S(2)}) copy-start(bf16[4096,128]{1,0:T(8,128)(2,1)} %copy-done.4) | copy-start | bytes 3145732
  98.6 738.8 %reduce-scatter.6.cloned.1.call-start = ((), (), s32[]{:S(2)}) async-start(), calls=%async_computation.4 | async-start | bytes 4259840 | tf_op jit(solution)/shard_map/reduce_scatter | solution.py:158
Sparse Core Ops, SparseCore 0:
  71.7 32.9 reduce-scatter.3
  107.4 364.9 reduce-scatter.7
  474.9 362.4 reduce-scatter.5
where the time goes:
time: 854 us; the launch traced here: 845 us
  waiting for transfers between devices  711 us (83%)
  local copies, waits for them, and re-layouts  46.3 us (5%)
  matrix products  41.9 us (5%)
  blocking collectives  21.7 us (3%)
  between operations  14 us (2%)
  other arithmetic  9.76 us (1%)
    reduce_scatter x1, waiting for transfers between devices, on_device(): lax.psum_scatter(key_full, 'pb', scatter_dimension=1, tiled=True)  364 us
    reduce_scatter x1, waiting for transfers between devices, on_device(): lax.psum_scatter(value_full, 'pb', scatter_dimension=1, tiled=True)  348 us
  transfers between devices with their start and end apart: 3, of which 2 were waited for; matrix products, arithmetic and copies ran while one was open for 6% of the time, Pallas kernels for 0%

commit v1 on v0

v1 whole, which is shorter than its diff:
```python
import functools
import math

import jax
import jax.numpy as jnp
from jax import lax
from jax.experimental import pallas as pl
from jax.experimental.pallas import tpu as pltpu
from jax.sharding import PartitionSpec as P

NEG = -1e30
HIDDEN = -2e30
TILE = 256
PAIR = 2
ZS = 8
YS = 4
F32 = jnp.float32
BF16 = jnp.bfloat16


def nt(a, b):
    return lax.dot_general(a, b, (((1,), (1,)), ((), ())), preferred_element_type=F32)


def tn(a, b):
    return lax.dot_general(a, b, (((0,), (0,)), ((), ())), preferred_element_type=F32)


def nn(a, b):
    return jnp.dot(a, b, preferred_element_type=F32)


def for_tiles(info, work):
    ka = info[2]

    def step(u, carry):
        slot = u // 4
        j = u % 4
        place = jnp.where(j < 2, 2 * ka + j, 2 * (7 - ka) + j - 2)
        block = info[slot]

        @pl.when(place < block)
        def _():
            work(slot, j, False)

        @pl.when(place == block)
        def _():
            work(slot, j, True)

        return carry

    lax.fori_loop(0, 8, step, 0)


def rows_of(index, size):
    return pl.ds(pl.multiple_of(index * size, size), size)


def visible_mask():
    shape = (TILE, TILE)
    return lax.broadcasted_iota(jnp.int32, shape, 0) <= lax.broadcasted_iota(jnp.int32, shape, 1)


def stat_kernel(width, info, q_ref, g_ref, k_ref, v_ref, out_ref, m_scr, l_scr, d_scr):
    factor = width**-0.5 * math.log2(math.e)
    heads = out_ref.shape[0] // 3
    m_scr[...] = jnp.full(m_scr.shape, NEG, F32)
    l_scr[...] = jnp.zeros(l_scr.shape, F32)
    d_scr[...] = jnp.zeros(d_scr.shape, F32)

    def work(slot, j, masked):
        keys = k_ref[0, rows_of(j, TILE), :]
        values = v_ref[0, rows_of(j, TILE), :]
        for h in range(PAIR):
            cols = slice(h * width, (h + 1) * width)
            scores = nt(keys, q_ref[rows_of(slot, TILE), cols]) * factor
            if masked:
                scores = jnp.where(visible_mask(), scores, HIDDEN)
            scores = scores.reshape(TILE // 8, 8, TILE)
            slopes = nt(values, g_ref[rows_of(slot, TILE), cols]).reshape(TILE // 8, 8, TILE)
            old = m_scr[h, slot]
            new = jnp.maximum(old, jnp.max(scores, axis=0))
            weights = jnp.exp2(scores - new[None])
            shrink = jnp.exp2(old - new)
            m_scr[h, slot] = new
            l_scr[h, slot] = l_scr[h, slot] * shrink + jnp.sum(weights, axis=0)
            d_scr[h, slot] = d_scr[h, slot] * shrink + jnp.sum(weights * slopes, axis=0)

    for_tiles(info, work)
    for h in range(PAIR):
        head = pl.program_id(0) * PAIR + h
        for slot in range(2):
            cols = slice(slot * TILE, (slot + 1) * TILE)
            m = m_scr[h, slot]
            top = jnp.max(m, axis=0, keepdims=True)
            shrink = jnp.exp2(m - top)
            out_ref[pl.ds(head, 1), cols] = top
            out_ref[pl.ds(heads + head, 1), cols] = jnp.sum(l_scr[h, slot] * shrink, axis=0, keepdims=True)
            out_ref[pl.ds(2 * heads + head, 1), cols] = jnp.sum(d_scr[h, slot] * shrink, axis=0, keepdims=True)


def grad_kernel(
    width, info, q_ref, g_ref, k_ref, v_ref, stat_ref,
    dq0, dq1, dq2, dq3, own, near_p, near_m, far_p, far_m, half_p, half_m,
    lse_scr, delta_scr, dk_scr, dv_scr, dq_scr,
):
    scale = width**-0.5
    factor = scale * math.log2(math.e)
    heads = lse_scr.shape[0]
    ka_size = stat_ref.shape[0]
    step = pl.program_id(0)

    @pl.when(step == 0)
    def _():
        top = stat_ref[0, :heads, :]
        for a in range(1, ka_size):
            top = jnp.maximum(top, stat_ref[a, :heads, :])
        total = jnp.zeros(top.shape, F32)
        dotted = jnp.zeros(top.shape, F32)
        for a in range(ka_size):
            shrink = jnp.exp2(stat_ref[a, :heads, :] - top)
            total += stat_ref[a, heads : 2 * heads, :] * shrink
            dotted += stat_ref[a, 2 * heads :, :] * shrink
        lse_scr[...] = top + jnp.log2(total)
        delta_scr[...] = dotted / total
        dk_scr[...] = jnp.zeros(dk_scr.shape, F32)
        dv_scr[...] = jnp.zeros(dv_scr.shape, F32)

    dq_scr[...] = jnp.zeros(dq_scr.shape, F32)

    def work(slot, j, masked):
        keys = k_ref[0, rows_of(j, TILE), :]
        values = v_ref[0, rows_of(j, TILE), :]
        key_sum = dk_scr[rows_of(j, TILE), :]
        value_sum = dv_scr[rows_of(j, TILE), :]
        for h in range(PAIR):
            cols = slice(h * width, (h + 1) * width)
            head = step * PAIR + h
            q = q_ref[rows_of(slot, TILE), cols]
            g = g_ref[rows_of(slot, TILE), cols]
            lse = lse_scr[pl.ds(head, 1), rows_of(slot, TILE)]
            delta = delta_scr[pl.ds(head, 1), rows_of(slot, TILE)]
            probs = jnp.exp2(nt(keys, q) * factor - lse)
            if masked:
                probs = jnp.where(visible_mask(), probs, 0.0)
            slopes = nt(values, g)
            score_grads = (probs * (slopes - delta) * scale).astype(BF16)
            value_sum += nn(probs.astype(BF16), g)
            key_sum += nn(score_grads, q)
            dq_scr[rows_of(slot, TILE), cols] += tn(score_grads, keys)
        dk_scr[rows_of(j, TILE), :] = key_sum
        dv_scr[rows_of(j, TILE), :] = value_sum

    for_tiles(info, work)

    ka = info[2]
    for rel, out in enumerate((dq0, dq1, dq2, dq3)):
        share = jnp.bitwise_xor(ka, rel)
        out[...] = dq_scr[rows_of(share, dq0.shape[0]), :]

    @pl.when(step == pl.num_programs(0) - 1)
    def _():
        z = info[4]

        def put(out, at, rel, pieces):
            for g in pieces:
                row = lax.rem(z + rel, ZS) * 8 + g * 8 * ZS
                for kv, acc in enumerate((dk_scr, dv_scr)):
                    for blk in range(2):
                        start = pl.multiple_of(row + blk * (dk_scr.shape[0] // 2), 8)
                        out[at : at + 8, :] = acc[pl.ds(start, 8), :]
                        at += 8

        every = range(8)
        put(own, 0, 0, every)
        put(near_p, 0, 1, every)
        put(near_p, 256, 3, every)
        put(near_m, 0, 7, every)
        put(near_m, 256, 5, every)
        put(far_p, 0, 2, every)
        put(far_m, 0, 6, every)
        put(half_p, 0, 4, range(4))
        put(half_m, 0, 4, range(4, 8))


def sum_kernel(info, own, near_p, near_m, far_p, far_m, mine, other):
    xh, y = info[5], info[6]
    for out, there in ((mine, xh), (other, 1 - xh)):
        for rel in range(YS):
            start = rows_of(there * YS + lax.rem(y + rel, YS), 32)
            out[rel] = (own[start, :] + near_p[start, :] + near_m[start, :]) + (far_p[start, :] + far_m[start, :])


def place_kernel(info, mine, other, from1, from2, from3, dk_ref, dv_ref, scr):
    xh, y = info[5], info[6]
    parts = [(0, mine[0], other[0])]
    parts += [(rel, ref[0], ref[1]) for rel, ref in ((1, from1), (2, from2), (3, from3))]
    for rel, near, far in parts:
        from_y = lax.rem(y + YS - rel, YS)
        for part, from_x in ((near, xh), (far, 1 - xh)):
            head = from_x * YS + from_y
            for kv in range(2):
                for blk in range(2):
                    at = (kv * 2 + blk) * 8
                    scr[kv, blk, :, pl.ds(head, 1), :] = part[at : at + 8, :].reshape(8, 1, part.shape[1])
    for kv, out in enumerate((dk_ref, dv_ref)):
        for blk in range(2):
            out[blk] = scr[kv, blk].reshape(64, out.shape[2]).astype(BF16)


def on_device(queries, keys, values, grad_out, query_blocks):
    head_count, key_count, width = keys.shape
    query_count = queries.shape[0]
    heads = queries.shape[1] // width
    pb = lax.axis_index("pb")
    ka = lax.axis_index("ka")
    pb_size = lax.axis_size("pb")
    owner = pb // ZS
    info = jnp.stack(
        [query_blocks[0], query_blocks[1], ka, owner, pb % ZS, owner // YS, owner % YS]
    ).astype(jnp.int32)
    steps = heads // PAIR

    part = pl.BlockSpec((query_count, PAIR * width), lambda i, s: (0, i))
    whole = pl.BlockSpec((1, key_count, width), lambda i, s: (s[3], 0, 0))
    params = pltpu.CompilerParams(vmem_limit_bytes=48 * 2**20)

    def fixed(shape):
        return pl.BlockSpec(shape, lambda i, s: (0,) * len(shape))

    def array(shape, dtype=F32):
        return jax.ShapeDtypeStruct(shape, dtype)

    stats = pl.pallas_call(
        functools.partial(stat_kernel, width),
        out_shape=array((3 * heads, query_count)),
        grid_spec=pltpu.PrefetchScalarGridSpec(
            num_scalar_prefetch=1,
            grid=(steps,),
            in_specs=[part, part, whole, whole],
            out_specs=fixed((3 * heads, query_count)),
            scratch_shapes=[pltpu.VMEM((PAIR, 2, 8, TILE), F32)] * 3,
        ),
        compiler_params=params,
        name="row_stats",
    )(info, queries, grad_out, keys, values)
    gathered = lax.all_gather(stats, "ka")

    share = query_count // 4
    chunk = (256, width)
    shapes = [chunk, (512, width), (512, width), chunk, chunk, (128, width), (128, width)]
    outs = pl.pallas_call(
        functools.partial(grad_kernel, width),
        out_shape=[array((share, heads * width))] * 4 + [array(s) for s in shapes],
        grid_spec=pltpu.PrefetchScalarGridSpec(
            num_scalar_prefetch=1,
            grid=(steps,),
            in_specs=[part, part, whole, whole, fixed(gathered.shape)],
            out_specs=[pl.BlockSpec((share, PAIR * width), lambda i, s: (0, i))] * 4 + [fixed(s) for s in shapes],
            scratch_shapes=[
                pltpu.VMEM((heads, query_count), F32),
                pltpu.VMEM((heads, query_count), F32),
                pltpu.VMEM((key_count, width), F32),
                pltpu.VMEM((key_count, width), F32),
                pltpu.VMEM((query_count, PAIR * width), F32),
            ],
        ),
        compiler_params=params,
        name="grads",
    )(info, queries, grad_out, keys, values, gathered)
    dq0, dq1, dq2, dq3, own, near_p, near_m, far_p, far_m, half_p, half_m = outs

    def along_z(x, by):
        return lax.ppermute(x, "pb", [(p, p // ZS * ZS + (p + by) % ZS) for p in range(pb_size)])

    def along_y(x, by):
        return lax.ppermute(
            x, "pb", [(p, (p // (ZS * YS) * YS + (p // ZS + by) % YS) * ZS + p % ZS) for p in range(pb_size)]
        )

    def across_x(x):
        return lax.ppermute(x, "pb", [(p, (p + pb_size // 2) % pb_size) for p in range(pb_size)])

    def across_ka(x, by):
        return lax.ppermute(x, "ka", [(a, a ^ by) for a in range(4)])

    got_np = along_z(near_p, 1)
    got_nm = along_z(near_m, ZS - 1)
    got_hp = along_z(half_p, 2)
    got_hm = along_z(half_m, ZS - 2)

    got3 = across_ka(dq3, 1)
    for_other = dq2 + got3
    got1 = across_ka(dq1, 1)
    got2 = across_ka(for_other, 2)

    far_p = far_p + got_np[256:] + jnp.pad(got_hp, ((0, 128), (0, 0)))
    far_m = far_m + got_nm[256:] + jnp.pad(got_hm, ((128, 0), (0, 0)))
    got_fp = along_z(far_p, 2)
    got_fm = along_z(far_m, ZS - 2)

    small = pl.BlockSpec(memory_space=pltpu.VMEM)
    scalars = pl.BlockSpec(memory_space=pltpu.SMEM)
    mine, other = pl.pallas_call(
        sum_kernel,
        out_shape=[array((YS, 32, width))] * 2,
        in_specs=[scalars] + [small] * 5,
        out_specs=[small] * 2,
        name="add_parts",
    )(info, own, got_np[:256], got_nm[:256], got_fp, got_fm)
    other = across_x(other)
    pairs = [jnp.stack([mine[k], other[k]]) for k in range(1, YS)]
    got_y = [along_y(x, k) for k, x in zip((2, 1, 3), (pairs[1], pairs[0], pairs[2]))]
    grad_keys, grad_values = pl.pallas_call(
        place_kernel,
        out_shape=[array((2, 64, width), BF16)] * 2,
        in_specs=[scalars] + [small] * 5,
        out_specs=[small] * 2,
        scratch_shapes=[pltpu.VMEM((2, 2, 8, 8, width), F32)],
        name="place_rows",
    )(info, mine, other, got_y[1], got_y[0], got_y[2])

    grad_queries = (dq0 + got1 + got2).astype(BF16)
    return grad_queries, grad_keys, grad_values


def solution(mesh):
    placed = (P("pb", None), P(None, "ka", None), P(None, "ka", None), P("pb", None), P("pb"))
    return jax.shard_map(
        on_device,
        mesh=mesh,
        in_specs=placed,
        out_specs=(P(("pb", "ka"), None), P("ka", "pb", None), P("ka", "pb", None)),
        check_vma=False,
    )
```

time: 854 us -> 90.3 us (0.11)
  waiting for transfers between devices: 711 us -> 12.4 us
  matrix products: 41.9 us -> 0 us
  local copies, waits for them, and re-layouts: 46.3 us -> 7.46 us
  starting transfers between devices: 0.34 us -> 30.7 us
  Pallas kernels: 0 us -> 28.1 us
  blocking collectives: 21.7 us -> 6.17 us
  between operations: 14 us -> 0.75 us
    reduce_scatter x3 -> x0, waiting for transfers between devices: 711 us -> none  [the longest x1 364 us: on_device(): lax.psum_scatter(key_full, 'pb', scatter_dimension=1, tiled=True)]
    dot_general x14 -> x0, matrix products: 41.9 us -> none  [the longest x2 9.25 us: grad_update(): jnp.einsum('rk,rd->kd', probs_low, grad_part, preferred_element_type=jnp....]
    ppermute x0 -> x13, starting transfers between devices: none -> 30.7 us  [the longest x6 17.3 us: along_z(): lax.ppermute(x, 'pb', [(p, p // ZS * ZS + (p + by) % ZS) for p in range(p...]
    dynamic_update_slice x2 -> x0, local copies, waits for them, and re-layouts: 30.3 us -> none  [the longest x1 15.2 us: on_device(): lax.dynamic_update_slice(blank, jnp.stack(value_terms), (zero_index, zero...]
    pallas_call x0 -> x4, Pallas kernels: none -> 28.1 us  [the longest x1 16 us: on_device(): pl.pallas_call(functools.partial(grad_kernel, width), out_shape=[array((s...]
    ppermute x0 -> x13, waiting for transfers between devices: none -> 12.4 us  [the longest x6 8.53 us: along_z(): lax.ppermute(x, 'pb', [(p, p // ZS * ZS + (p + by) % ZS) for p in range(p...]
    pmax x1 -> x0, blocking collectives: 11.2 us -> none  [on_device(): top = lax.pmax(state[0], 'ka')]
    psum x1 -> x0, blocking collectives: 10.5 us -> none  [on_device(): total, dotted = lax.psum((state[1] * factor, state[2] * factor), 'ka')]
  transfers between devices with their start and end apart: 3 -> 13, of which waited for: 2 -> 7; matrix products, arithmetic and copies ran while one was open for 6% -> 3% of each run, Pallas kernels for 0% -> 4%
where the time goes in v1:
time: 90.3 us; the launch traced here: 88.7 us
  starting transfers between devices  30.7 us (34%)
  Pallas kernels  28.1 us (31%)
  waiting for transfers between devices  12.4 us (14%)
  local copies, waits for them, and re-layouts  7.46 us (8%)
  blocking collectives  6.17 us (7%)
  other arithmetic  3.08 us (3%)
    ppermute x6, starting transfers between devices, along_z(): lax.ppermute(x, 'pb', [(p, p // ZS * ZS + (p + by) % ZS) for p in range(p...  17.3 us
    pallas_call x1, Pallas kernels, on_device(): pl.pallas_call(functools.partial(grad_kernel, width), out_shape=[array((s...  16 us
    pallas_call x1, Pallas kernels, on_device(): pl.pallas_call(functools.partial(stat_kernel, width), out_shape=array((3...  8.65 us
    ppermute x6, waiting for transfers between devices, along_z(): lax.ppermute(x, 'pb', [(p, p // ZS * ZS + (p + by) % ZS) for p in range(p...  8.53 us
    ppermute x3, starting transfers between devices, along_y(): lax.ppermute(x, 'pb', [(p, (p // (ZS * YS) * YS + (p // ZS + by) % YS) *...  7.23 us
    all_gather x1, blocking collectives, on_device(): gathered = lax.all_gather(stats, 'ka')  6.17 us
    unnamed x22, local copies, waits for them, and re-layouts  5.97 us
    ppermute x1, starting transfers between devices, across_x(): lax.ppermute(x, 'pb', [(p, (p + pb_size // 2) % pb_size) for p in range(p...  4.05 us
  transfers between devices with their start and end apart: 13, of which 7 were waited for; matrix products, arithmetic and copies ran while one was open for 3% of the time, Pallas kernels for 4%

profile of v1, /device:TPU:64, one launch (start us, length us, event | category | flops | bytes accessed | tf_op | source)
XLA Modules:
  0.0 88.7 jit_solution(3132415590684809506)
XLA Ops:
  0.7 0.7 stack.32.info
  1.4 1.6 %copy-done = bf16[8,1024,128]{2,1,0:T(8,128)(2,1)S(1)} copy-done((bf16[8,1024,128]{2,1,0:T(8,128)(2,1)S(1)}, bf16[8,1024,128]{2,1,0:T(8,128)(2,1)}, u32[]{:S(2)}) %copy-start) | copy-done | bytes 2097176
  3.0 1.2 %copy-done.1 = bf16[512,1024]{1,0:T(8,128)(2,1)S(1)} copy-done((bf16[512,1024]{1,0:T(8,128)(2,1)S(1)}, bf16[512,1024]{1,0:T(8,128)(2,1)}, u32[]{:S(2)}) %copy-start.1) | copy-done | bytes 1048600
  4.2 1.2 %copy-done.2 = bf16[512,1024]{1,0:T(8,128)(2,1)S(1)} copy-done((bf16[512,1024]{1,0:T(8,128)(2,1)S(1)}, bf16[512,1024]{1,0:T(8,128)(2,1)}, u32[]{:S(2)}) %copy-start.2) | copy-done | bytes 1048600
  5.5 8.6 %row_stats.1 = f32[24,512]{1,0:T(8,128)S(1)} custom-call(s32[7]{0:T(128)S(1)} %stack.32.info, bf16[512,1024]{1,0:T(8,128)(2,1)S(1)} %copy-done.1, bf16[512,1024]{1,0:T(8,128)(2,1)S(1)} %copy-done.2, bf16[8,1024,128]{2,1,0:T(8,128)(2,1)S(1)} %copy-done, bf16[8,1024,128]{2,1,0:T(8,128)(2,1)} %v_ref.3), custom_call_target="tpu_custom_call" | custom-call | tf_op jit(solution)/shard_map/row_stats/pallas_call | solution.py:234
  14.1 6.2 %all-gather = f32[96,512]{1,0:T(8,128)S(1)} all-gather(f32[24,512]{1,0:T(8,128)S(1)} %row_stats.1), channel_id=2, replica_groups=mesh['pb'=64,'ka'=4] {'ka'}, dimensions={0}, use_global_device_ids=true | all-gather | bytes 245760 | tf_op jit(solution)/shard_map/all_gather | solution.py:247
  20.3 16.0 %grads.1 = (f32[128,1024]{1,0:T(8,128)S(1)}, f32[128,1024]{1,0:T(8,128)S(1)}, f32[128,1024]{1,0:T(8,128)S(1)}, f32[128,1024]{1,0:T(8,128)S(1)}, f32[256,128]{1,0...) custom-call(s32[7]{0:T(128)S(1)} %stack.32.info, ...), custom_call_target="tpu_custom_call" | custom-call | tf_op jit(solution)/shard_map/grads/pallas_call | solution.py:252
  36.3 0.6 copy-done.3
  36.9 1.9 %collective-permute-start.3 = (f32[512,128]{1,0:T(8,128)S(1)}, f32[512,128]{1,0:T(8,128)S(1)}, u32[]{:S(2)}, u32[]{:S(2)}) collective-permute-start(f32[512,128]{1,0:T(8,128)S(1)} %get-tuple-element.23), channel_id=1, source_target_pairs={{0,4},{4,8},{8,12},{12,16},{16,20},{20,24},{24,28},{28,0},{32,36},... | collective-permute-start | bytes 786440 | tf_op jit(solution)/shard_map/ppermute | solution.py:274
  38.9 6.4 %collective-permute-start.5 = (f32[128,128]{1,0:T(8,128)S(1)}, f32[128,128]{1,0:T(8,128)S(1)}, u32[]{:S(2)}, u32[]{:S(2)}) collective-permute-start(f32[128,128]{1,0:T(8,128)S(1)} %get-tuple-element.26), channel_id=1, source_target_pairs={{0,8},{4,12},{8,16},{12,20},{16,24},{20,28},{24,0},{28,4},{32,40},... | collective-permute-start | bytes 196616 | tf_op jit(solution)/shard_map/ppermute | solution.py:274
  45.2 2.0 %collective-permute-start.4 = (f32[512,128]{1,0:T(8,128)S(1)}, f32[512,128]{1,0:T(8,128)S(1)}, u32[]{:S(2)}, u32[]{:S(2)}) collective-permute-start(f32[512,128]{1,0:T(8,128)S(1)} %get-tuple-element.24), channel_id=1, source_target_pairs={{0,28},{4,0},{8,4},{12,8},{16,12},{20,16},{24,20},{28,24},{32,60},... | collective-permute-start | bytes 786440 | tf_op jit(solution)/shard_map/ppermute | solution.py:274
  47.6 0.7 fusion.1
  48.3 6.6 %collective-permute-start.6 = (f32[256,128]{1,0:T(8,128)S(1)}, f32[256,128]{1,0:T(8,128)S(1)}, u32[]{:S(2)}, u32[]{:S(2)}) collective-permute-start(f32[256,128]{1,0:T(8,128)S(1)} %get-tuple-element.35), channel_id=1, source_target_pairs={{0,8},{4,12},{8,16},{12,20},{16,24},{20,28},{24,0},{28,4},{32,40},... | collective-permute-start | bytes 393224 | tf_op jit(solution)/shard_map/ppermute | solution.py:274
  54.9 1.4 %collective-permute-done.7 = f32[128,128]{1,0:T(8,128)S(1)} collective-permute-done((f32[128,128]{1,0:T(8,128)S(1)}, f32[128,128]{1,0:T(8,128)S(1)}, u32[]{:S(2)}, u32[]{:S(2)}) %collective-permute-start.7) | collective-permute-done | bytes 65568 | tf_op jit(solution)/shard_map/ppermute | solution.py:274
  56.3 0.7 fusion
  57.0 0.5 collective-permute-start.8
  57.4 4.0 %collective-permute-done.6.far_p = f32[256,128]{1,0:T(8,128)S(1)} collective-permute-done((f32[256,128]{1,0:T(8,128)S(1)}, f32[256,128]{1,0:T(8,128)S(1)}, u32[]{:S(2)}, u32[]{:S(2)}) %collective-permute-start.6) | collective-permute-done | bytes 131104 | tf_op jit(solution)/shard_map/ppermute | solution.py:274
  61.5 2.7 %collective-permute-done.8.far_m = f32[256,128]{1,0:T(8,128)S(1)} collective-permute-done((f32[256,128]{1,0:T(8,128)S(1)}, f32[256,128]{1,0:T(8,128)S(1)}, u32[]{:S(2)}, u32[]{:S(2)}) %collective-permute-start.8) | collective-permute-done | bytes 131104 | tf_op jit(solution)/shard_map/ppermute | solution.py:274
  64.2 0.7 copy-done.7
  64.8 1.9 %add_parts.1 = (f32[4,32,128]{2,1,0:T(8,128)}, f32[4,32,128]{2,1,0:T(8,128)}) custom-call(s32[7]{0:T(128)} %copy-done.4, f32[256,128]{1,0:T(8,128)} %copy-done.3, f32[256,128]{1,0:T(8,128)} %get-tuple-element.36.near_p, f32[256,128]{1,0:T(8,128)} %get-tuple-element.34.near_m, f32[256,128]{1,0:T(8,128)} %copy-done.6, f32[256,128]{1,0:T(8,128)} %copy-done.7), custom_call_target="tpu_custom_call" | custom-call | tf_op jit(solution)/shard_map/add_parts/pallas_call | solution.py:304
  66.7 4.0 %collective-permute-start.9 = (f32[4,32,128]{2,1,0:T(8,128)}, f32[4,32,128]{2,1,0:T(8,128)S(1)}, u32[]{:S(2)}, u32[]{:S(2)}) collective-permute-start(f32[4,32,128]{2,1,0:T(8,128)} %get-tuple-element.30), channel_id=1, source_target_pairs={{0,128},{4,132},{8,136},{12,140},{16,144},{20,148},{24,152},{28,15... | collective-permute-start | bytes 196616 | tf_op jit(solution)/shard_map/ppermute | solution.py:282
  70.7 0.8 fusion.2
  71.5 0.9 %add.37 = f32[128,1024]{1,0:T(8,128)} add(f32[128,1024]{1,0:T(8,128)S(1)} %get-tuple-element.20, f32[128,1024]{1,0:T(8,128)S(1)} %collective-permute-done.1) | non-fusion elementwise | flops 131072 | bytes 1572864 | tf_op jit(solution)/shard_map/add | solution.py:293
  72.4 2.1 %collective-permute-start.2 = (f32[128,1024]{1,0:T(8,128)}, f32[128,1024]{1,0:T(8,128)S(1)}, u32[]{:S(2)}, u32[]{:S(2)}) collective-permute-start(f32[128,1024]{1,0:T(8,128)} %add.37), channel_id=1, source_target_pairs={{0,2},{1,3},{2,0},{3,1},{4,6},{5,7},{6,4},{7,5},{8,10},{9,11},{10,... | collective-permute-start | bytes 1572872 | tf_op jit(solution)/shard_map/ppermute | solution.py:285
  74.5 3.5 %collective-permute-start.10 = (f32[2,32,128]{2,1,0:T(8,128)S(1)}, f32[2,32,128]{2,1,0:T(8,128)S(1)}, u32[]{:S(2)}, u32[]{:S(2)}) collective-permute-start(f32[2,32,128]{2,1,0:T(8,128)S(1)} %pad_maximum_fusion), channel_id=1, source_target_pairs={{0,32},{4,36},{8,40},{12,44},{16,48},{20,52},{24,56},{28,60},{32,6... | collective-permute-start | bytes 98312 | tf_op jit(solution)/shard_map/ppermute | solution.py:277
  78.0 3.7 %collective-permute-start.11 = (f32[2,32,128]{2,1,0:T(8,128)S(1)}, f32[2,32,128]{2,1,0:T(8,128)S(1)}, u32[]{:S(2)}, u32[]{:S(2)}) collective-permute-start(f32[2,32,128]{2,1,0:T(8,128)S(1)} %pad_maximum_fusion.1), channel_id=1, source_target_pairs={{0,64},{4,68},{8,72},{12,76},{16,80},{20,84},{24,88},{28,92},{32,9... | collective-permute-start | bytes 98312 | tf_op jit(solution)/shard_map/ppermute | solution.py:277
  81.8 0.4 collective-permute-done.10.from1
  82.2 1.8 %collective-permute-done.11.from2 = f32[2,32,128]{2,1,0:T(8,128)S(1)} collective-permute-done((f32[2,32,128]{2,1,0:T(8,128)S(1)}, f32[2,32,128]{2,1,0:T(8,128)S(1)}, u32[]{:S(2)}, u32[]{:S(2)}) %collective-permute-start.11) | collective-permute-done | bytes 32800 | tf_op jit(solution)/shard_map/ppermute | solution.py:277
  84.0 1.7 %collective-permute-done.12.from3 = f32[2,32,128]{2,1,0:T(8,128)S(1)} collective-permute-done((f32[2,32,128]{2,1,0:T(8,128)S(1)}, f32[2,32,128]{2,1,0:T(8,128)S(1)}, u32[]{:S(2)}, u32[]{:S(2)}) %collective-permute-start.12) | collective-permute-done | bytes 32800 | tf_op jit(solution)/shard_map/ppermute | solution.py:277
  85.7 0.6 copy-done.10
  86.3 1.6 %place_rows.1 = (bf16[2,64,128]{2,1,0:T(8,128)(2,1)}, bf16[2,64,128]{2,1,0:T(8,128)(2,1)}) custom-call(s32[7]{0:T(128)} %copy-done.4, f32[4,32,128]{2,1,0:T(8,128)} %get-tuple-element.29.mine, f32[4,32,128]{2,1,0:T(8,128)} %copy-done.5, f32[2,32,128]{2,1,0:T(8,128)} %copy-done.8, f32[2,32,128]{2,1,0:T(8,128)} %copy-done.9, f32[2,32,128]{2,1,0:T(8,128)} %copy-done.10), custom_call_target="tpu_custom_call" | custom-call | tf_op jit(solution)/shard_map/place_rows/pallas_call | solution.py:314
  87.9 0.8 add_convert_fusion
  (31 shorter events, 0.5 us)
Async XLA Ops:
  1.4 1.6 %copy-start = (bf16[8,1024,128]{2,1,0:T(8,128)(2,1)S(1)}, bf16[8,1024,128]{2,1,0:T(8,128)(2,1)}, u32[]{:S(2)}) copy-start(bf16[8,1024,128]{2,1,0:T(8,128)(2,1)} %k_ref.3) | copy-start | bytes 6291460
  3.0 1.2 %copy-start.1 = (bf16[512,1024]{1,0:T(8,128)(2,1)S(1)}, bf16[512,1024]{1,0:T(8,128)(2,1)}, u32[]{:S(2)}) copy-start(bf16[512,1024]{1,0:T(8,128)(2,1)} %q_ref.3) | copy-start | bytes 3145732
  4.2 1.2 %copy-start.2 = (bf16[512,1024]{1,0:T(8,128)(2,1)S(1)}, bf16[512,1024]{1,0:T(8,128)(2,1)}, u32[]{:S(2)}) copy-start(bf16[512,1024]{1,0:T(8,128)(2,1)} %g_ref.3) | copy-start | bytes 3145732
  5.5 14.8 %copy-start.4 = (s32[7]{0:T(128)}, s32[7]{0:T(128)S(1)}, u32[]{:S(2)}) copy-start(s32[7]{0:T(128)S(1)} %stack.32.info) | copy-start | bytes 88
  36.3 0.7 copy-start.3
  36.9 10.7 %collective-permute-start.3 = (f32[512,128]{1,0:T(8,128)S(1)}, f32[512,128]{1,0:T(8,128)S(1)}, u32[]{:S(2)}, u32[]{:S(2)}) collective-permute-start(f32[512,128]{1,0:T(8,128)S(1)} %get-tuple-element.23), channel_id=1, source_target_pairs={{0,4},{4,8},{8,12},{12,16},{16,20},{20,24},{24,28},{28,0},{32,36},... | collective-permute-start | bytes 786440 | tf_op jit(solution)/shard_map/ppermute | solution.py:274
  38.9 8.8 %collective-permute-start.5 = (f32[128,128]{1,0:T(8,128)S(1)}, f32[128,128]{1,0:T(8,128)S(1)}, u32[]{:S(2)}, u32[]{:S(2)}) collective-permute-start(f32[128,128]{1,0:T(8,128)S(1)} %get-tuple-element.26), channel_id=1, source_target_pairs={{0,8},{4,12},{8,16},{12,20},{16,24},{20,28},{24,0},{28,4},{32,40},... | collective-permute-start | bytes 196616 | tf_op jit(solution)/shard_map/ppermute | solution.py:274
  45.2 11.1 %collective-permute-start.4 = (f32[512,128]{1,0:T(8,128)S(1)}, f32[512,128]{1,0:T(8,128)S(1)}, u32[]{:S(2)}, u32[]{:S(2)}) collective-permute-start(f32[512,128]{1,0:T(8,128)S(1)} %get-tuple-element.24), channel_id=1, source_target_pairs={{0,28},{4,0},{8,4},{12,8},{16,12},{20,16},{24,20},{28,24},{32,60},... | collective-permute-start | bytes 786440 | tf_op jit(solution)/shard_map/ppermute | solution.py:274
  47.2 9.1 %collective-permute-start.7 = (f32[128,128]{1,0:T(8,128)S(1)}, f32[128,128]{1,0:T(8,128)S(1)}, u32[]{:S(2)}, u32[]{:S(2)}) collective-permute-start(f32[128,128]{1,0:T(8,128)S(1)} %get-tuple-element.28), channel_id=1, source_target_pairs={{0,24},{4,28},{8,0},{12,4},{16,8},{20,12},{24,16},{28,20},{32,56},... | collective-permute-start | bytes 196616 | tf_op jit(solution)/shard_map/ppermute | solution.py:274
  47.2 24.2 %collective-permute-start.1 = (f32[128,1024]{1,0:T(8,128)S(1)}, f32[128,1024]{1,0:T(8,128)S(1)}, u32[]{:S(2)}, u32[]{:S(2)}) collective-permute-start(f32[128,1024]{1,0:T(8,128)S(1)} %get-tuple-element.21), channel_id=1, source_target_pairs={{0,1},{1,0},{2,3},{3,2},{4,5},{5,4},{6,7},{7,6},{8,9},{9,8},{10,11... | collective-permute-start | bytes 1572872 | tf_op jit(solution)/shard_map/ppermute | solution.py:285
  48.3 13.1 %collective-permute-start.6 = (f32[256,128]{1,0:T(8,128)S(1)}, f32[256,128]{1,0:T(8,128)S(1)}, u32[]{:S(2)}, u32[]{:S(2)}) collective-permute-start(f32[256,128]{1,0:T(8,128)S(1)} %get-tuple-element.35), channel_id=1, source_target_pairs={{0,8},{4,12},{8,16},{12,20},{16,24},{20,28},{24,0},{28,4},{32,40},... | collective-permute-start | bytes 393224 | tf_op jit(solution)/shard_map/ppermute | solution.py:274
  57.0 7.2 %collective-permute-start.8 = (f32[256,128]{1,0:T(8,128)S(1)}, f32[256,128]{1,0:T(8,128)S(1)}, u32[]{:S(2)}, u32[]{:S(2)}) collective-permute-start(f32[256,128]{1,0:T(8,128)S(1)} %get-tuple-element.33), channel_id=1, source_target_pairs={{0,24},{4,28},{8,0},{12,4},{16,8},{20,12},{24,16},{28,20},{32,56},... | collective-permute-start | bytes 393224 | tf_op jit(solution)/shard_map/ppermute | solution.py:274
  57.4 30.5 %collective-permute-start = (f32[128,1024]{1,0:T(8,128)S(1)}, f32[128,1024]{1,0:T(8,128)S(1)}, u32[]{:S(2)}, u32[]{:S(2)}) collective-permute-start(f32[128,1024]{1,0:T(8,128)S(1)} %get-tuple-element.19), channel_id=1, source_target_pairs={{0,1},{1,0},{2,3},{3,2},{4,5},{5,4},{6,7},{7,6},{8,9},{9,8},{10,11... | collective-permute-start | bytes 1572872 | tf_op jit(solution)/shard_map/ppermute | solution.py:285
  61.5 2.7 %copy-start.6 = (f32[256,128]{1,0:T(8,128)}, f32[256,128]{1,0:T(8,128)S(1)}, u32[]{:S(2)}) copy-start(f32[256,128]{1,0:T(8,128)S(1)} %collective-permute-done.6.far_p) | copy-start | bytes 393220
  64.2 0.7 copy-start.7
  66.7 7.8 %collective-permute-start.9 = (f32[4,32,128]{2,1,0:T(8,128)}, f32[4,32,128]{2,1,0:T(8,128)S(1)}, u32[]{:S(2)}, u32[]{:S(2)}) collective-permute-start(f32[4,32,128]{2,1,0:T(8,128)} %get-tuple-element.30), channel_id=1, source_target_pairs={{0,128},{4,132},{8,136},{12,140},{16,144},{20,148},{24,152},{28,15... | collective-permute-start | bytes 196616 | tf_op jit(solution)/shard_map/ppermute | solution.py:282
  72.4 15.5 %collective-permute-start.2 = (f32[128,1024]{1,0:T(8,128)}, f32[128,1024]{1,0:T(8,128)S(1)}, u32[]{:S(2)}, u32[]{:S(2)}) collective-permute-start(f32[128,1024]{1,0:T(8,128)} %add.37), channel_id=1, source_target_pairs={{0,2},{1,3},{2,0},{3,1},{4,6},{5,7},{6,4},{7,5},{8,10},{9,11},{10,... | collective-permute-start | bytes 1572872 | tf_op jit(solution)/shard_map/ppermute | solution.py:285
  74.5 11.2 %copy-start.5 = (f32[4,32,128]{2,1,0:T(8,128)}, f32[4,32,128]{2,1,0:T(8,128)S(1)}, u32[]{:S(2)}) copy-start(f32[4,32,128]{2,1,0:T(8,128)S(1)} %collective-permute-done.9.other) | copy-start | bytes 196612
  74.5 7.7 %collective-permute-start.10 = (f32[2,32,128]{2,1,0:T(8,128)S(1)}, f32[2,32,128]{2,1,0:T(8,128)S(1)}, u32[]{:S(2)}, u32[]{:S(2)}) collective-permute-start(f32[2,32,128]{2,1,0:T(8,128)S(1)} %pad_maximum_fusion), channel_id=1, source_target_pairs={{0,32},{4,36},{8,40},{12,44},{16,48},{20,52},{24,56},{28,60},{32,6... | collective-permute-start | bytes 98312 | tf_op jit(solution)/shard_map/ppermute | solution.py:277
  78.0 6.0 %collective-permute-start.11 = (f32[2,32,128]{2,1,0:T(8,128)S(1)}, f32[2,32,128]{2,1,0:T(8,128)S(1)}, u32[]{:S(2)}, u32[]{:S(2)}) collective-permute-start(f32[2,32,128]{2,1,0:T(8,128)S(1)} %pad_maximum_fusion.1), channel_id=1, source_target_pairs={{0,64},{4,68},{8,72},{12,76},{16,80},{20,84},{24,88},{28,92},{32,9... | collective-permute-start | bytes 98312 | tf_op jit(solution)/shard_map/ppermute | solution.py:277
  81.8 3.9 %collective-permute-start.12 = (f32[2,32,128]{2,1,0:T(8,128)S(1)}, f32[2,32,128]{2,1,0:T(8,128)S(1)}, u32[]{:S(2)}, u32[]{:S(2)}) collective-permute-start(f32[2,32,128]{2,1,0:T(8,128)S(1)} %pad_maximum_fusion.2), channel_id=1, source_target_pairs={{0,96},{4,100},{8,104},{12,108},{16,112},{20,116},{24,120},{28,124... | collective-permute-start | bytes 98312 | tf_op jit(solution)/shard_map/ppermute | solution.py:277
  82.2 3.5 %copy-start.8 = (f32[2,32,128]{2,1,0:T(8,128)}, f32[2,32,128]{2,1,0:T(8,128)S(1)}, u32[]{:S(2)}) copy-start(f32[2,32,128]{2,1,0:T(8,128)S(1)} %collective-permute-done.10.from1) | copy-start | bytes 98308
  84.0 1.7 %copy-start.9 = (f32[2,32,128]{2,1,0:T(8,128)}, f32[2,32,128]{2,1,0:T(8,128)S(1)}, u32[]{:S(2)}) copy-start(f32[2,32,128]{2,1,0:T(8,128)S(1)} %collective-permute-done.11.from2) | copy-start | bytes 98308
  85.7 0.6 copy-start.10

commit v2 on v1

v2 whole, which is shorter than its diff:
```python
import functools
import math

import jax
import jax.numpy as jnp
from jax import lax
from jax.experimental import pallas as pl
from jax.experimental.pallas import tpu as pltpu
from jax.sharding import PartitionSpec as P

NEG = -1e30
HIDDEN = -2e30
TILE = 256
GROUP = 4
ZS = 8
YS = 4
F32 = jnp.float32
BF16 = jnp.bfloat16


def nt(a, b):
    return lax.dot_general(a, b, (((1,), (1,)), ((), ())), preferred_element_type=F32)


def nn(a, b):
    return jnp.dot(a, b, preferred_element_type=F32)


def for_tiles(info, work):
    ka = info[2]

    def step(u, carry):
        slot = u // 4
        j = u % 4
        place = jnp.where(j < 2, 2 * ka + j, 2 * (7 - ka) + j - 2)
        block = info[slot]

        @pl.when(place < block)
        def _():
            work(slot, j, False)

        @pl.when(place == block)
        def _():
            work(slot, j, True)

        return carry

    lax.fori_loop(0, 8, step, 0)


def rows_of(index, size):
    return pl.ds(pl.multiple_of(index * size, size), size)


def visible_mask():
    shape = (TILE, TILE)
    return lax.broadcasted_iota(jnp.int32, shape, 0) <= lax.broadcasted_iota(jnp.int32, shape, 1)


def load(pairs, sems):
    copies = [pltpu.make_async_copy(src, dst, sems.at[i]) for i, (src, dst) in enumerate(pairs)]
    for copy in copies:
        copy.start()
    for copy in copies:
        copy.wait()


def stat_kernel(
    width, info, q_hbm, g_hbm, k_hbm, v_hbm, out_ref, q_ref, g_ref, k_ref, v_ref, m_scr, l_scr, d_scr, sems
):
    load([(k_hbm.at[info[3]], k_ref), (q_hbm, q_ref), (v_hbm.at[info[3]], v_ref), (g_hbm, g_ref)], sems)
    factor = width**-0.5 * math.log2(math.e)
    heads = out_ref.shape[0] // 3
    m_scr[...] = jnp.full(m_scr.shape, NEG, F32)
    l_scr[...] = jnp.zeros(l_scr.shape, F32)
    d_scr[...] = jnp.zeros(d_scr.shape, F32)
    def work(slot, j, masked):
        keys = k_ref[rows_of(j, TILE), :]
        values = v_ref[rows_of(j, TILE), :]
        for h in range(heads):
            cols = slice(h * width, (h + 1) * width)
            scores = nt(keys, q_ref[rows_of(slot, TILE), cols]) * factor
            if masked:
                scores = jnp.where(visible_mask(), scores, HIDDEN)
            scores = scores.reshape(TILE // 8, 8, TILE)
            slopes = nt(values, g_ref[rows_of(slot, TILE), cols]).reshape(TILE // 8, 8, TILE)
            old = m_scr[h, slot]
            new = jnp.maximum(old, jnp.max(scores, axis=0))
            weights = jnp.exp2(scores - new[None])
            shrink = jnp.exp2(old - new)
            m_scr[h, slot] = new
            l_scr[h, slot] = l_scr[h, slot] * shrink + jnp.sum(weights, axis=0)
            d_scr[h, slot] = d_scr[h, slot] * shrink + jnp.sum(weights * slopes, axis=0)
    for_tiles(info, work)
    for h in range(heads):
        for slot in range(2):
            cols = slice(slot * TILE, (slot + 1) * TILE)
            m = m_scr[h, slot]
            top = jnp.max(m, axis=0, keepdims=True)
            shrink = jnp.exp2(m - top)
            out_ref[h : h + 1, cols] = top
            out_ref[heads + h : heads + h + 1, cols] = jnp.sum(l_scr[h, slot] * shrink, axis=0, keepdims=True)
            out_ref[2 * heads + h : 2 * heads + h + 1, cols] = jnp.sum(d_scr[h, slot] * shrink, axis=0, keepdims=True)


def grad_kernel(
    width, info, q_hbm, g_hbm, k_hbm, v_hbm, stat_ref,
    dq0, dq1, dq2, dq3, own, near_p, near_m, far_p, far_m, half_p, half_m,
    q_ref, g_ref, k_ref, v_ref, qt_ref, gt_ref, kt_ref, lse_scr, delta_scr, dk_scr, dv_scr, dq_scr,
    dk_rows, dv_rows, sems,
):
    load([(k_hbm.at[info[3]], k_ref), (q_hbm, q_ref), (v_hbm.at[info[3]], v_ref), (g_hbm, g_ref)], sems)
    scale = width**-0.5
    factor = scale * math.log2(math.e)
    heads = lse_scr.shape[0]
    ka_size = stat_ref.shape[0]
    top = stat_ref[0, :heads, :]
    for a in range(1, ka_size):
        top = jnp.maximum(top, stat_ref[a, :heads, :])
    total = jnp.zeros(top.shape, F32)
    dotted = jnp.zeros(top.shape, F32)
    for a in range(ka_size):
        shrink = jnp.exp2(stat_ref[a, :heads, :] - top)
        total += stat_ref[a, heads : 2 * heads, :] * shrink
        dotted += stat_ref[a, 2 * heads :, :] * shrink
    lse_scr[...] = top + jnp.log2(total)
    delta_scr[...] = dotted / total
    dk_scr[...] = jnp.zeros(dk_scr.shape, F32)
    dv_scr[...] = jnp.zeros(dv_scr.shape, F32)
    dq_scr[...] = jnp.zeros(dq_scr.shape, F32)
    for slot in range(2):
        for h in range(heads):
            at = (slot * heads + h) * TILE
            qt_ref[:, at:at + TILE] = q_ref[slot * TILE:(slot + 1) * TILE, h * width:(h + 1) * width].T
            gt_ref[:, at:at + TILE] = g_ref[slot * TILE:(slot + 1) * TILE, h * width:(h + 1) * width].T
    kt_ref[...] = k_ref[...].T

    def work(slot, j, masked):
        keys = k_ref[rows_of(j, TILE), :]
        values = v_ref[rows_of(j, TILE), :]
        kt = kt_ref[:, rows_of(j, TILE)]
        span = GROUP * TILE
        for first in range(0, heads, GROUP):
            at = pl.ds(pl.multiple_of(slot * heads * TILE + first * TILE, TILE), span)
            qt = qt_ref[:, at]
            gt = gt_ref[:, at]
            lows, grads = [], []
            for i in range(GROUP):
                h = first + i
                part = slice(i * TILE, (i + 1) * TILE)
                lse = lse_scr[h : h + 1, rows_of(slot, TILE)]
                delta = delta_scr[h : h + 1, rows_of(slot, TILE)]
                probs = jnp.exp2(nn(keys, qt[:, part]) * factor - lse)
                if masked:
                    probs = jnp.where(visible_mask(), probs, 0.0)
                slopes = nn(values, gt[:, part])
                grads.append((probs * (slopes - delta) * scale).astype(BF16))
                lows.append(probs.astype(BF16))
            low = jnp.concatenate(lows, axis=1)
            grad = jnp.concatenate(grads, axis=1)
            dv_scr[:, rows_of(j, TILE)] += nt(gt, low)
            dk_scr[:, rows_of(j, TILE)] += nt(qt, grad)
            dq_scr[:, at] += nn(kt, grad)
    for_tiles(info, work)

    ka = info[2]
    half = TILE // 2
    for rel, out in enumerate((dq0, dq1, dq2, dq3)):
        share = jnp.bitwise_xor(ka, rel)
        slot, side = share // 2, share % 2
        for h in range(heads):
            start = pl.multiple_of((slot * heads + h) * TILE + side * half, half)
            out[:, h * half:(h + 1) * half] = dq_scr[:, pl.ds(start, half)]
    z = info[4]
    dk_rows[...] = dk_scr[...].T
    dv_rows[...] = dv_scr[...].T

    def put(out, at, rel, pieces):
        for g in pieces:
            row = lax.rem(z + rel, ZS) * 8 + g * 8 * ZS
            for kv, acc in enumerate((dk_rows, dv_rows)):
                for blk in range(2):
                    start = pl.multiple_of(row + blk * (dk_rows.shape[0] // 2), 8)
                    out[at : at + 8, :] = acc[pl.ds(start, 8), :]
                    at += 8

    every = range(8)
    put(own, 0, 0, every)
    put(near_p, 0, 1, every)
    put(near_p, 256, 3, every)
    put(near_m, 0, 7, every)
    put(near_m, 256, 5, every)
    put(far_p, 0, 2, every)
    put(far_m, 0, 6, every)
    put(half_p, 0, 4, range(4))
    put(half_m, 0, 4, range(4, 8))


def sum_kernel(info, own, near_p, near_m, far_p, far_m, mine, other):
    xh, y = info[5], info[6]
    for out, there in ((mine, xh), (other, 1 - xh)):
        for rel in range(YS):
            start = rows_of(there * YS + lax.rem(y + rel, YS), 32)
            out[rel] = (own[start, :] + near_p[start, :] + near_m[start, :]) + (far_p[start, :] + far_m[start, :])


def place_kernel(info, mine, other, from1, from2, from3, dk_ref, dv_ref, scr):
    xh, y = info[5], info[6]
    parts = [(0, mine[0], other[0])]
    parts += [(rel, ref[0], ref[1]) for rel, ref in ((1, from1), (2, from2), (3, from3))]
    for rel, near, far in parts:
        from_y = lax.rem(y + YS - rel, YS)
        for part, from_x in ((near, xh), (far, 1 - xh)):
            head = from_x * YS + from_y
            for kv in range(2):
                for blk in range(2):
                    at = (kv * 2 + blk) * 8
                    scr[kv, blk, :, pl.ds(head, 1), :] = part[at : at + 8, :].reshape(8, 1, part.shape[1])
    for kv, out in enumerate((dk_ref, dv_ref)):
        for blk in range(2):
            out[blk] = scr[kv, blk].reshape(64, out.shape[2]).astype(BF16)


def query_kernel(a_ref, b_ref, c_ref, out_ref):
    rows, width = out_ref.shape[0], a_ref.shape[0]
    for h in range(out_ref.shape[1] // width):
        part = slice(h * rows, (h + 1) * rows)
        total = a_ref[:, part] + b_ref[:, part] + c_ref[:, part]
        out_ref[:, h * width : (h + 1) * width] = total.T.astype(BF16)


def array(shape, dtype=F32):
    return jax.ShapeDtypeStruct(shape, dtype)


SMALL = pl.BlockSpec(memory_space=pltpu.VMEM)
SCALARS = pl.BlockSpec(memory_space=pltpu.SMEM)
LARGE = pl.BlockSpec(memory_space=pltpu.HBM)
PARAMS = pltpu.CompilerParams(vmem_limit_bytes=40 * 2**20)


def row_stats(info, queries, grad_out, keys, values):
    _, key_count, width = keys.shape
    query_count = queries.shape[0]
    heads = queries.shape[1] // width
    return pl.pallas_call(
        functools.partial(stat_kernel, width),
        out_shape=array((3 * heads, query_count)),
        in_specs=[SCALARS] + [LARGE] * 4,
        out_specs=SMALL,
        scratch_shapes=[pltpu.VMEM(queries.shape, BF16)] * 2
        + [pltpu.VMEM((key_count, width), BF16)] * 2
        + [pltpu.VMEM((heads, 2, 8, TILE), F32)] * 3
        + [pltpu.SemaphoreType.DMA((4,))],
        compiler_params=PARAMS,
        name="row_stats",
    )(info, queries, grad_out, keys, values)


def gradients(info, queries, grad_out, keys, values, gathered):
    _, key_count, width = keys.shape
    query_count = queries.shape[0]
    heads = queries.shape[1] // width
    share = query_count // 4
    chunk = (256, width)
    shapes = [chunk, (512, width), (512, width), chunk, chunk, (128, width), (128, width)]
    return pl.pallas_call(
        functools.partial(grad_kernel, width),
        out_shape=[array((width, heads * share))] * 4 + [array(s) for s in shapes],
        in_specs=[SCALARS] + [LARGE] * 4 + [SMALL],
        out_specs=[SMALL] * 11,
        scratch_shapes=[pltpu.VMEM(queries.shape, BF16)] * 2
        + [pltpu.VMEM((key_count, width), BF16)] * 2
        + [pltpu.VMEM((width, query_count * heads), BF16)] * 2
        + [pltpu.VMEM((width, key_count), BF16)]
        + [pltpu.VMEM((heads, query_count), F32)] * 2
        + [pltpu.VMEM((width, key_count), F32)] * 2
        + [pltpu.VMEM((width, query_count * heads), F32)]
        + [pltpu.VMEM((key_count, width), F32)] * 2
        + [pltpu.SemaphoreType.DMA((4,))],
        compiler_params=PARAMS,
        name="grads",
    )(info, queries, grad_out, keys, values, gathered)


def on_device(queries, keys, values, grad_out, query_blocks):
    width = keys.shape[2]
    query_count = queries.shape[0]
    pb = lax.axis_index("pb")
    ka = lax.axis_index("ka")
    pb_size = lax.axis_size("pb")
    owner = pb // ZS
    info = jnp.stack(
        [query_blocks[0], query_blocks[1], ka, owner, pb % ZS, owner // YS, owner % YS]
    ).astype(jnp.int32)
    stats = row_stats(info, queries, grad_out, keys, values)
    gathered = lax.all_gather(stats, "ka")

    outs = gradients(info, queries, grad_out, keys, values, gathered)
    dq0, dq1, dq2, dq3, own, near_p, near_m, far_p, far_m, half_p, half_m = outs

    def along_z(x, by):
        return lax.ppermute(x, "pb", [(p, p // ZS * ZS + (p + by) % ZS) for p in range(pb_size)])

    def along_y(x, by):
        return lax.ppermute(
            x, "pb", [(p, (p // (ZS * YS) * YS + (p // ZS + by) % YS) * ZS + p % ZS) for p in range(pb_size)]
        )

    def across_x(x):
        return lax.ppermute(x, "pb", [(p, (p + pb_size // 2) % pb_size) for p in range(pb_size)])

    def across_ka(x, by):
        return lax.ppermute(x, "ka", [(a, a ^ by) for a in range(4)])

    got_np = along_z(near_p, 1)
    got_nm = along_z(near_m, ZS - 1)
    got_hp = along_z(half_p, 2)
    got_hm = along_z(half_m, ZS - 2)

    got3 = across_ka(dq3, 1)
    for_other = dq2 + got3
    got1 = across_ka(dq1, 1)
    got2 = across_ka(for_other, 2)

    far_p = far_p + got_np[256:] + jnp.pad(got_hp, ((0, 128), (0, 0)))
    far_m = far_m + got_nm[256:] + jnp.pad(got_hm, ((128, 0), (0, 0)))
    got_fp = along_z(far_p, 2)
    got_fm = along_z(far_m, ZS - 2)

    mine, other = pl.pallas_call(
        sum_kernel,
        out_shape=[array((YS, 32, width))] * 2,
        in_specs=[SCALARS] + [SMALL] * 5,
        out_specs=[SMALL] * 2,
        name="add_parts",
    )(info, own, got_np[:256], got_nm[:256], got_fp, got_fm)
    other = across_x(other)
    pairs = [jnp.stack([mine[k], other[k]]) for k in range(1, YS)]
    got_y = [along_y(x, k) for k, x in zip((2, 1, 3), (pairs[1], pairs[0], pairs[2]))]
    grad_keys, grad_values = pl.pallas_call(
        place_kernel,
        out_shape=[array((2, 64, width), BF16)] * 2,
        in_specs=[SCALARS] + [SMALL] * 5,
        out_specs=[SMALL] * 2,
        scratch_shapes=[pltpu.VMEM((2, 2, 8, 8, width), F32)],
        name="place_rows",
    )(info, mine, other, got_y[1], got_y[0], got_y[2])

    grad_queries = pl.pallas_call(
        query_kernel,
        out_shape=array((query_count // 4, queries.shape[1]), BF16),
        in_specs=[SMALL] * 3,
        out_specs=SMALL,
        name="finish_queries",
    )(dq0, got1, got2)
    return grad_queries, grad_keys, grad_values


def solution(mesh):
    placed = (P("pb", None), P(None, "ka", None), P(None, "ka", None), P("pb", None), P("pb"))
    return jax.shard_map(
        on_device,
        mesh=mesh,
        in_specs=placed,
        out_specs=(P(("pb", "ka"), None), P("ka", "pb", None), P("ka", "pb", None)),
        check_vma=False,
    )
```

time: 90.3 us -> 80 us (0.89)
  Pallas kernels: 28.1 us -> 20.8 us
  starting transfers between devices: 30.7 us -> 24.2 us
  local copies, waits for them, and re-layouts: 7.46 us -> 10.8 us
  waiting for transfers between devices: 12.4 us -> 15.6 us
  other arithmetic: 3.08 us -> 1.45 us
    pallas_call x2 -> x3, Pallas kernels: 24.6 us -> 17.3 us  [the longest x1 9.65 us: gradients(): pl.pallas_call(functools.partial(grad_kernel, width), out_shape=[array((w...]
    ppermute x6, starting transfers between devices: 17.3 us -> 12.8 us  [along_z(): lax.ppermute(x, 'pb', [(p, p // ZS * ZS + (p + by) % ZS) for p in range(p...]
    unnamed x22 -> x30, local copies, waits for them, and re-layouts: 5.97 us -> 9.34 us
    ppermute x6, waiting for transfers between devices: 8.53 us -> 11.4 us  [along_z(): lax.ppermute(x, 'pb', [(p, p // ZS * ZS + (p + by) % ZS) for p in range(p...]
    ppermute x3, starting transfers between devices: 2.11 us -> 0.22 us  [across_ka(): return lax.ppermute(x, 'ka', [(a, a ^ by) for a in range(4)])]
    ppermute x1, waiting for transfers between devices: 0.01 us -> 1.66 us  [across_x(): lax.ppermute(x, 'pb', [(p, (p + pb_size // 2) % pb_size) for p in range(p...]
    ppermute x3, waiting for transfers between devices: 3.91 us -> 2.56 us  [along_y(): lax.ppermute(x, 'pb', [(p, (p // (ZS * YS) * YS + (p // ZS + by) % YS) *...]
    ppermute x3, starting transfers between devices: 7.23 us -> 6.29 us  [along_y(): lax.ppermute(x, 'pb', [(p, (p // (ZS * YS) * YS + (p // ZS + by) % YS) *...]
  transfers between devices with their start and end apart: 13 -> 13, of which waited for: 7 -> 8; matrix products, arithmetic and copies ran while one was open for 3% -> 3% of each run, Pallas kernels for 4% -> 4%
where the time goes in v2:
time: 80 us; the launch traced here: 79.3 us
  starting transfers between devices  24.2 us (30%)
  Pallas kernels  20.8 us (26%)
  waiting for transfers between devices  15.6 us (20%)
  local copies, waits for them, and re-layouts  10.8 us (14%)
  blocking collectives  5.61 us (7%)
  other arithmetic  1.45 us (2%)
    ppermute x6, starting transfers between devices, along_z(): lax.ppermute(x, 'pb', [(p, p // ZS * ZS + (p + by) % ZS) for p in range(p...  12.8 us
    ppermute x6, waiting for transfers between devices, along_z(): lax.ppermute(x, 'pb', [(p, p // ZS * ZS + (p + by) % ZS) for p in range(p...  11.4 us
    pallas_call x1, Pallas kernels, gradients(): pl.pallas_call(functools.partial(grad_kernel, width), out_shape=[array((w...  9.65 us
    unnamed x30, local copies, waits for them, and re-layouts  9.34 us
    ppermute x3, starting transfers between devices, along_y(): lax.ppermute(x, 'pb', [(p, (p // (ZS * YS) * YS + (p // ZS + by) % YS) *...  6.29 us
    all_gather x1, blocking collectives, on_device(): gathered = lax.all_gather(stats, 'ka')  5.61 us
    pallas_call x1, Pallas kernels, row_stats(): pl.pallas_call(functools.partial(stat_kernel, width), out_shape=array((3...  5.48 us
    ppermute x1, starting transfers between devices, across_x(): lax.ppermute(x, 'pb', [(p, (p + pb_size // 2) % pb_size) for p in range(p...  4.98 us
  transfers between devices with their start and end apart: 13, of which 8 were waited for; matrix products, arithmetic and copies ran while one was open for 3% of the time, Pallas kernels for 4%

profile of v2, /device:TPU:64, one launch (start us, length us, event | category | flops | bytes accessed | tf_op | source)
XLA Modules:
  0.0 79.3 jit_solution(289248404722813727)
XLA Ops:
  0.7 0.7 stack.32.info
  1.4 1.6 %copy-done = bf16[8,1024,128]{2,1,0:T(8,128)(2,1)S(1)} copy-done((bf16[8,1024,128]{2,1,0:T(8,128)(2,1)S(1)}, bf16[8,1024,128]{2,1,0:T(8,128)(2,1)}, u32[]{:S(2)}) %copy-start) | copy-done | bytes 2097176
  3.0 1.6 %copy-done.1 = bf16[8,1024,128]{2,1,0:T(8,128)(2,1)S(1)} copy-done((bf16[8,1024,128]{2,1,0:T(8,128)(2,1)S(1)}, bf16[8,1024,128]{2,1,0:T(8,128)(2,1)}, u32[]{:S(2)}) %copy-start.1) | copy-done | bytes 2097176
  4.6 1.2 %copy-done.2 = bf16[512,1024]{1,0:T(8,128)(2,1)S(1)} copy-done((bf16[512,1024]{1,0:T(8,128)(2,1)S(1)}, bf16[512,1024]{1,0:T(8,128)(2,1)}, u32[]{:S(2)}) %copy-start.2) | copy-done | bytes 1048600
  5.8 1.2 %copy-done.3 = bf16[512,1024]{1,0:T(8,128)(2,1)S(1)} copy-done((bf16[512,1024]{1,0:T(8,128)(2,1)S(1)}, bf16[512,1024]{1,0:T(8,128)(2,1)}, u32[]{:S(2)}) %copy-start.3) | copy-done | bytes 1048600
  7.0 5.5 %row_stats.1 = f32[24,512]{1,0:T(8,128)S(1)} custom-call(s32[7]{0:T(128)S(1)} %stack.32.info, bf16[512,1024]{1,0:T(8,128)(2,1)S(1)} %copy-done.2, bf16[512,1024]{1,0:T(8,128)(2,1)S(1)} %copy-done.3, bf16[8,1024,128]{2,1,0:T(8,128)(2,1)S(1)} %copy-done, bf16[8,1024,128]{2,1,0:T(8,128)(2,1)S(1)} %copy-done.1), custom_call_target="tpu_custom_call" | custom-call | tf_op jit(solution)/shard_map/row_stats/pallas_call | solution.py:246
  12.5 5.6 %all-gather = f32[96,512]{1,0:T(8,128)S(1)} all-gather(f32[24,512]{1,0:T(8,128)S(1)} %row_stats.1), channel_id=2, replica_groups=mesh['pb'=64,'ka'=4] {'ka'}, dimensions={0}, use_global_device_ids=true | all-gather | bytes 245760 | tf_op jit(solution)/shard_map/all_gather | solution.py:297
  18.1 9.6 %grads.1 = (f32[128,1024]{1,0:T(8,128)S(1)}, f32[128,1024]{1,0:T(8,128)S(1)}, f32[128,1024]{1,0:T(8,128)S(1)}, f32[128,1024]{1,0:T(8,128)S(1)}, f32[256,128]{1,0...) custom-call(s32[7]{0:T(128)S(1)} %stack.32.info, ...), custom_call_target="tpu_custom_call" | custom-call | tf_op jit(solution)/shard_map/grads/pallas_call | solution.py:267
  27.8 0.8 copy-done.4
  28.6 0.7 copy-done.5
  29.3 4.5 %collective-permute-start.5 = (f32[128,128]{1,0:T(8,128)S(1)}, f32[128,128]{1,0:T(8,128)S(1)}, u32[]{:S(2)}, u32[]{:S(2)}) collective-permute-start(f32[128,128]{1,0:T(8,128)S(1)} %get-tuple-element.26), channel_id=1, source_target_pairs={{0,8},{4,12},{8,16},{12,20},{16,24},{20,28},{24,0},{28,4},{32,40},... | collective-permute-start | bytes 196616 | tf_op jit(solution)/shard_map/ppermute | solution.py:303
  33.8 2.0 %collective-permute-start.4 = (f32[512,128]{1,0:T(8,128)S(1)}, f32[512,128]{1,0:T(8,128)S(1)}, u32[]{:S(2)}, u32[]{:S(2)}) collective-permute-start(f32[512,128]{1,0:T(8,128)S(1)} %get-tuple-element.24), channel_id=1, source_target_pairs={{0,28},{4,0},{8,4},{12,8},{16,12},{20,16},{24,20},{28,24},{32,60},... | collective-permute-start | bytes 786440 | tf_op jit(solution)/shard_map/ppermute | solution.py:303
  35.8 1.6 %collective-permute-done.5 = f32[128,128]{1,0:T(8,128)S(1)} collective-permute-done((f32[128,128]{1,0:T(8,128)S(1)}, f32[128,128]{1,0:T(8,128)S(1)}, u32[]{:S(2)}, u32[]{:S(2)}) %collective-permute-start.5) | collective-permute-done | bytes 65568 | tf_op jit(solution)/shard_map/ppermute | solution.py:303
  37.4 1.1 %collective-permute-done.3 = f32[512,128]{1,0:T(8,128)S(1)} collective-permute-done((f32[512,128]{1,0:T(8,128)S(1)}, f32[512,128]{1,0:T(8,128)S(1)}, u32[]{:S(2)}, u32[]{:S(2)}) %collective-permute-start.3) | collective-permute-done | bytes 262176 | tf_op jit(solution)/shard_map/ppermute | solution.py:303
  38.5 0.7 fusion.1
  39.1 5.7 %collective-permute-start.6 = (f32[256,128]{1,0:T(8,128)S(1)}, f32[256,128]{1,0:T(8,128)S(1)}, u32[]{:S(2)}, u32[]{:S(2)}) collective-permute-start(f32[256,128]{1,0:T(8,128)S(1)} %get-tuple-element.35), channel_id=1, source_target_pairs={{0,8},{4,12},{8,16},{12,20},{16,24},{20,28},{24,0},{28,4},{32,40},... | collective-permute-start | bytes 393224 | tf_op jit(solution)/shard_map/ppermute | solution.py:303
  44.9 0.7 collective-permute-done.7
  45.6 0.7 fusion
  46.7 2.5 %collective-permute-done.6.far_p = f32[256,128]{1,0:T(8,128)S(1)} collective-permute-done((f32[256,128]{1,0:T(8,128)S(1)}, f32[256,128]{1,0:T(8,128)S(1)}, u32[]{:S(2)}, u32[]{:S(2)}) %collective-permute-start.6) | collective-permute-done | bytes 131104 | tf_op jit(solution)/shard_map/ppermute | solution.py:303
  49.2 5.6 %collective-permute-done.8.far_m = f32[256,128]{1,0:T(8,128)S(1)} collective-permute-done((f32[256,128]{1,0:T(8,128)S(1)}, f32[256,128]{1,0:T(8,128)S(1)}, u32[]{:S(2)}, u32[]{:S(2)}) %collective-permute-start.8) | collective-permute-done | bytes 131104 | tf_op jit(solution)/shard_map/ppermute | solution.py:303
  55.4 1.9 %add_parts.1 = (f32[4,32,128]{2,1,0:T(8,128)}, f32[4,32,128]{2,1,0:T(8,128)}) custom-call(s32[7]{0:T(128)} %copy-done.6, f32[256,128]{1,0:T(8,128)} %copy-done.5, f32[256,128]{1,0:T(8,128)} %get-tuple-element.36.near_p, f32[256,128]{1,0:T(8,128)} %get-tuple-element.34.near_m, f32[256,128]{1,0:T(8,128)} %copy-done.10, f32[256,128]{1,0:T(8,128)} %copy-done.11), custom_call_target="tpu_custom_call" | custom-call | tf_op jit(solution)/shard_map/add_parts/pallas_call | solution.py:331
  57.3 5.0 %collective-permute-start.9 = (f32[4,32,128]{2,1,0:T(8,128)}, f32[4,32,128]{2,1,0:T(8,128)S(1)}, u32[]{:S(2)}, u32[]{:S(2)}) collective-permute-start(f32[4,32,128]{2,1,0:T(8,128)} %get-tuple-element.30), channel_id=1, source_target_pairs={{0,128},{4,132},{8,136},{12,140},{16,144},{20,148},{24,152},{28,15... | collective-permute-start | bytes 196616 | tf_op jit(solution)/shard_map/ppermute | solution.py:311
  62.2 0.8 fusion.2
  63.3 1.7 %collective-permute-done.9.other = f32[4,32,128]{2,1,0:T(8,128)S(1)} collective-permute-done((f32[4,32,128]{2,1,0:T(8,128)}, f32[4,32,128]{2,1,0:T(8,128)S(1)}, u32[]{:S(2)}, u32[]{:S(2)}) %collective-permute-start.9) | collective-permute-done | bytes 65568 | tf_op jit(solution)/shard_map/ppermute | solution.py:311
  65.0 0.9 %collective-permute-start.10 = (f32[2,32,128]{2,1,0:T(8,128)S(1)}, f32[2,32,128]{2,1,0:T(8,128)S(1)}, u32[]{:S(2)}, u32[]{:S(2)}) collective-permute-start(f32[2,32,128]{2,1,0:T(8,128)S(1)} %pad_maximum_fusion), channel_id=1, source_target_pairs={{0,32},{4,36},{8,40},{12,44},{16,48},{20,52},{24,56},{28,60},{32,6... | collective-permute-start | bytes 98312 | tf_op jit(solution)/shard_map/ppermute | solution.py:306
  65.9 4.0 %collective-permute-start.11 = (f32[2,32,128]{2,1,0:T(8,128)S(1)}, f32[2,32,128]{2,1,0:T(8,128)S(1)}, u32[]{:S(2)}, u32[]{:S(2)}) collective-permute-start(f32[2,32,128]{2,1,0:T(8,128)S(1)} %pad_maximum_fusion.1), channel_id=1, source_target_pairs={{0,64},{4,68},{8,72},{12,76},{16,80},{20,84},{24,88},{28,92},{32,9... | collective-permute-start | bytes 98312 | tf_op jit(solution)/shard_map/ppermute | solution.py:306
  69.9 1.3 %collective-permute-start.12 = (f32[2,32,128]{2,1,0:T(8,128)S(1)}, f32[2,32,128]{2,1,0:T(8,128)S(1)}, u32[]{:S(2)}, u32[]{:S(2)}) collective-permute-start(f32[2,32,128]{2,1,0:T(8,128)S(1)} %pad_maximum_fusion.2), channel_id=1, source_target_pairs={{0,96},{4,100},{8,104},{12,108},{16,112},{20,116},{24,120},{28,124... | collective-permute-start | bytes 98312 | tf_op jit(solution)/shard_map/ppermute | solution.py:306
  71.3 0.9 %collective-permute-done.11.from2 = f32[2,32,128]{2,1,0:T(8,128)S(1)} collective-permute-done((f32[2,32,128]{2,1,0:T(8,128)S(1)}, f32[2,32,128]{2,1,0:T(8,128)S(1)}, u32[]{:S(2)}, u32[]{:S(2)}) %collective-permute-start.11) | collective-permute-done | bytes 32800 | tf_op jit(solution)/shard_map/ppermute | solution.py:306
  72.2 1.7 %collective-permute-done.12.from3 = f32[2,32,128]{2,1,0:T(8,128)S(1)} collective-permute-done((f32[2,32,128]{2,1,0:T(8,128)S(1)}, f32[2,32,128]{2,1,0:T(8,128)S(1)}, u32[]{:S(2)}, u32[]{:S(2)}) %collective-permute-start.12) | collective-permute-done | bytes 32800 | tf_op jit(solution)/shard_map/ppermute | solution.py:306
  74.5 1.6 %place_rows.1 = (bf16[2,64,128]{2,1,0:T(8,128)(2,1)}, bf16[2,64,128]{2,1,0:T(8,128)(2,1)}) custom-call(s32[7]{0:T(128)} %copy-done.6, f32[4,32,128]{2,1,0:T(8,128)} %get-tuple-element.29.mine, f32[4,32,128]{2,1,0:T(8,128)} %copy-done.9, f32[2,32,128]{2,1,0:T(8,128)} %copy-done.12, f32[2,32,128]{2,1,0:T(8,128)} %copy-done.13, f32[2,32,128]{2,1,0:T(8,128)} %copy-done.14), custom_call_target="tpu_custom_call" | custom-call | tf_op jit(solution)/shard_map/place_rows/pallas_call | solution.py:341
  76.1 0.8 copy-done.7
  77.1 2.2 %finish_queries.1 = bf16[128,1024]{1,0:T(8,128)(2,1)} custom-call(f32[128,1024]{1,0:T(8,128)} %copy-done.4, f32[128,1024]{1,0:T(8,128)} %copy-done.7, f32[128,1024]{1,0:T(8,128)} %copy-done.8), custom_call_target="tpu_custom_call" | custom-call | tf_op jit(solution)/shard_map/finish_queries/pallas_call | solution.py:350
  (39 shorter events, 2.3 us)
Async XLA Ops:
  1.4 1.6 %copy-start = (bf16[8,1024,128]{2,1,0:T(8,128)(2,1)S(1)}, bf16[8,1024,128]{2,1,0:T(8,128)(2,1)}, u32[]{:S(2)}) copy-start(bf16[8,1024,128]{2,1,0:T(8,128)(2,1)} %k_hbm.3) | copy-start | bytes 6291460
  3.0 1.6 %copy-start.1 = (bf16[8,1024,128]{2,1,0:T(8,128)(2,1)S(1)}, bf16[8,1024,128]{2,1,0:T(8,128)(2,1)}, u32[]{:S(2)}) copy-start(bf16[8,1024,128]{2,1,0:T(8,128)(2,1)} %v_hbm.3) | copy-start | bytes 6291460
  4.6 1.2 %copy-start.2 = (bf16[512,1024]{1,0:T(8,128)(2,1)S(1)}, bf16[512,1024]{1,0:T(8,128)(2,1)}, u32[]{:S(2)}) copy-start(bf16[512,1024]{1,0:T(8,128)(2,1)} %q_hbm.3) | copy-start | bytes 3145732
  5.8 1.2 %copy-start.3 = (bf16[512,1024]{1,0:T(8,128)(2,1)S(1)}, bf16[512,1024]{1,0:T(8,128)(2,1)}, u32[]{:S(2)}) copy-start(bf16[512,1024]{1,0:T(8,128)(2,1)} %g_hbm.3) | copy-start | bytes 3145732
  7.0 11.1 %copy-start.6 = (s32[7]{0:T(128)}, s32[7]{0:T(128)S(1)}, u32[]{:S(2)}) copy-start(s32[7]{0:T(128)S(1)} %stack.32.info) | copy-start | bytes 88
  27.8 0.8 %copy-start.4 = (f32[128,1024]{1,0:T(8,128)}, f32[128,1024]{1,0:T(8,128)S(1)}, u32[]{:S(2)}) copy-start(f32[128,1024]{1,0:T(8,128)S(1)} %get-tuple-element.18.a_ref) | copy-start | bytes 1572868
  28.6 0.7 copy-start.5
  29.3 9.2 %collective-permute-start.3 = (f32[512,128]{1,0:T(8,128)S(1)}, f32[512,128]{1,0:T(8,128)S(1)}, u32[]{:S(2)}, u32[]{:S(2)}) collective-permute-start(f32[512,128]{1,0:T(8,128)S(1)} %get-tuple-element.23), channel_id=1, source_target_pairs={{0,4},{4,8},{8,12},{12,16},{16,20},{20,24},{24,28},{28,0},{32,36},... | collective-permute-start | bytes 786440 | tf_op jit(solution)/shard_map/ppermute | solution.py:303
  29.3 8.1 %collective-permute-start.5 = (f32[128,128]{1,0:T(8,128)S(1)}, f32[128,128]{1,0:T(8,128)S(1)}, u32[]{:S(2)}, u32[]{:S(2)}) collective-permute-start(f32[128,128]{1,0:T(8,128)S(1)} %get-tuple-element.26), channel_id=1, source_target_pairs={{0,8},{4,12},{8,16},{12,20},{16,24},{20,28},{24,0},{28,4},{32,40},... | collective-permute-start | bytes 196616 | tf_op jit(solution)/shard_map/ppermute | solution.py:303
  33.8 11.8 %collective-permute-start.4 = (f32[512,128]{1,0:T(8,128)S(1)}, f32[512,128]{1,0:T(8,128)S(1)}, u32[]{:S(2)}, u32[]{:S(2)}) collective-permute-start(f32[512,128]{1,0:T(8,128)S(1)} %get-tuple-element.24), channel_id=1, source_target_pairs={{0,28},{4,0},{8,4},{12,8},{16,12},{20,16},{24,20},{28,24},{32,60},... | collective-permute-start | bytes 786440 | tf_op jit(solution)/shard_map/ppermute | solution.py:303
  35.8 9.8 %collective-permute-start.7 = (f32[128,128]{1,0:T(8,128)S(1)}, f32[128,128]{1,0:T(8,128)S(1)}, u32[]{:S(2)}, u32[]{:S(2)}) collective-permute-start(f32[128,128]{1,0:T(8,128)S(1)} %get-tuple-element.28), channel_id=1, source_target_pairs={{0,24},{4,28},{8,0},{12,4},{16,8},{20,12},{24,16},{28,20},{32,56},... | collective-permute-start | bytes 196616 | tf_op jit(solution)/shard_map/ppermute | solution.py:303
  35.8 27.2 %collective-permute-start.1 = (f32[128,1024]{1,0:T(8,128)S(1)}, f32[128,1024]{1,0:T(8,128)S(1)}, u32[]{:S(2)}, u32[]{:S(2)}) collective-permute-start(f32[128,1024]{1,0:T(8,128)S(1)} %get-tuple-element.21), channel_id=1, source_target_pairs={{0,1},{1,0},{2,3},{3,2},{4,5},{5,4},{6,7},{7,6},{8,9},{9,8},{10,11... | collective-permute-start | bytes 1572872 | tf_op jit(solution)/shard_map/ppermute | solution.py:314
  39.1 10.1 %collective-permute-start.6 = (f32[256,128]{1,0:T(8,128)S(1)}, f32[256,128]{1,0:T(8,128)S(1)}, u32[]{:S(2)}, u32[]{:S(2)}) collective-permute-start(f32[256,128]{1,0:T(8,128)S(1)} %get-tuple-element.35), channel_id=1, source_target_pairs={{0,8},{4,12},{8,16},{12,20},{16,24},{20,28},{24,0},{28,4},{32,40},... | collective-permute-start | bytes 393224 | tf_op jit(solution)/shard_map/ppermute | solution.py:303
  46.3 8.5 %collective-permute-start.8 = (f32[256,128]{1,0:T(8,128)S(1)}, f32[256,128]{1,0:T(8,128)S(1)}, u32[]{:S(2)}, u32[]{:S(2)}) collective-permute-start(f32[256,128]{1,0:T(8,128)S(1)} %get-tuple-element.33), channel_id=1, source_target_pairs={{0,24},{4,28},{8,0},{12,4},{16,8},{20,12},{24,16},{28,20},{32,56},... | collective-permute-start | bytes 393224 | tf_op jit(solution)/shard_map/ppermute | solution.py:303
  46.7 29.3 %collective-permute-start = (f32[128,1024]{1,0:T(8,128)S(1)}, f32[128,1024]{1,0:T(8,128)S(1)}, u32[]{:S(2)}, u32[]{:S(2)}) collective-permute-start(f32[128,1024]{1,0:T(8,128)S(1)} %get-tuple-element.19), channel_id=1, source_target_pairs={{0,1},{1,0},{2,3},{3,2},{4,5},{5,4},{6,7},{7,6},{8,9},{9,8},{10,11... | collective-permute-start | bytes 1572872 | tf_op jit(solution)/shard_map/ppermute | solution.py:314
  49.2 5.6 %copy-start.10 = (f32[256,128]{1,0:T(8,128)}, f32[256,128]{1,0:T(8,128)S(1)}, u32[]{:S(2)}) copy-start(f32[256,128]{1,0:T(8,128)S(1)} %collective-permute-done.6.far_p) | copy-start | bytes 393220
  54.8 0.6 copy-start.11
  57.3 7.7 %collective-permute-start.9 = (f32[4,32,128]{2,1,0:T(8,128)}, f32[4,32,128]{2,1,0:T(8,128)S(1)}, u32[]{:S(2)}, u32[]{:S(2)}) collective-permute-start(f32[4,32,128]{2,1,0:T(8,128)} %get-tuple-element.30), channel_id=1, source_target_pairs={{0,128},{4,132},{8,136},{12,140},{16,144},{20,148},{24,152},{28,15... | collective-permute-start | bytes 196616 | tf_op jit(solution)/shard_map/ppermute | solution.py:311
  63.1 13.0 %collective-permute-start.2 = (f32[128,1024]{1,0:T(8,128)S(1)}, f32[128,1024]{1,0:T(8,128)S(1)}, u32[]{:S(2)}, u32[]{:S(2)}) collective-permute-start(f32[128,1024]{1,0:T(8,128)S(1)} %add.30), channel_id=1, source_target_pairs={{0,2},{1,3},{2,0},{3,1},{4,6},{5,7},{6,4},{7,5},{8,10},{9,11},{10,... | collective-permute-start | bytes 1572872 | tf_op jit(solution)/shard_map/ppermute | solution.py:314
  65.0 8.9 %copy-start.9 = (f32[4,32,128]{2,1,0:T(8,128)}, f32[4,32,128]{2,1,0:T(8,128)S(1)}, u32[]{:S(2)}) copy-start(f32[4,32,128]{2,1,0:T(8,128)S(1)} %collective-permute-done.9.other) | copy-start | bytes 196612
  65.0 6.3 %collective-permute-start.10 = (f32[2,32,128]{2,1,0:T(8,128)S(1)}, f32[2,32,128]{2,1,0:T(8,128)S(1)}, u32[]{:S(2)}, u32[]{:S(2)}) collective-permute-start(f32[2,32,128]{2,1,0:T(8,128)S(1)} %pad_maximum_fusion), channel_id=1, source_target_pairs={{0,32},{4,36},{8,40},{12,44},{16,48},{20,52},{24,56},{28,60},{32,6... | collective-permute-start | bytes 98312 | tf_op jit(solution)/shard_map/ppermute | solution.py:306
  65.9 6.3 %collective-permute-start.11 = (f32[2,32,128]{2,1,0:T(8,128)S(1)}, f32[2,32,128]{2,1,0:T(8,128)S(1)}, u32[]{:S(2)}, u32[]{:S(2)}) collective-permute-start(f32[2,32,128]{2,1,0:T(8,128)S(1)} %pad_maximum_fusion.1), channel_id=1, source_target_pairs={{0,64},{4,68},{8,72},{12,76},{16,80},{20,84},{24,88},{28,92},{32,9... | collective-permute-start | bytes 98312 | tf_op jit(solution)/shard_map/ppermute | solution.py:306
  69.9 3.9 %collective-permute-start.12 = (f32[2,32,128]{2,1,0:T(8,128)S(1)}, f32[2,32,128]{2,1,0:T(8,128)S(1)}, u32[]{:S(2)}, u32[]{:S(2)}) collective-permute-start(f32[2,32,128]{2,1,0:T(8,128)S(1)} %pad_maximum_fusion.2), channel_id=1, source_target_pairs={{0,96},{4,100},{8,104},{12,108},{16,112},{20,116},{24,120},{28,124... | collective-permute-start | bytes 98312 | tf_op jit(solution)/shard_map/ppermute | solution.py:306
  71.3 2.6 %copy-start.12 = (f32[2,32,128]{2,1,0:T(8,128)}, f32[2,32,128]{2,1,0:T(8,128)S(1)}, u32[]{:S(2)}) copy-start(f32[2,32,128]{2,1,0:T(8,128)S(1)} %collective-permute-done.10.from1) | copy-start | bytes 98308
  72.2 1.7 %copy-start.13 = (f32[2,32,128]{2,1,0:T(8,128)}, f32[2,32,128]{2,1,0:T(8,128)S(1)}, u32[]{:S(2)}) copy-start(f32[2,32,128]{2,1,0:T(8,128)S(1)} %collective-permute-done.11.from2) | copy-start | bytes 98308
  73.8 0.6 copy-start.14
  76.1 0.8 %copy-start.7 = (f32[128,1024]{1,0:T(8,128)}, f32[128,1024]{1,0:T(8,128)S(1)}, u32[]{:S(2)}) copy-start(f32[128,1024]{1,0:T(8,128)S(1)} %collective-permute-done.b_ref) | copy-start | bytes 1572868
  76.1 1.0 %copy-start.8 = (f32[128,1024]{1,0:T(8,128)}, f32[128,1024]{1,0:T(8,128)S(1)}, u32[]{:S(2)}) copy-start(f32[128,1024]{1,0:T(8,128)S(1)} %collective-permute-done.2.c_ref) | copy-start | bytes 1572868

commit v3 on v2

v3 whole, which is shorter than its diff:
```python
import functools
import math

import jax
import jax.numpy as jnp
from jax import lax
from jax.experimental import pallas as pl
from jax.experimental.pallas import tpu as pltpu
from jax.sharding import PartitionSpec as P

NEG = -1e30
HIDDEN = -2e30
TILE = 256
GROUP = 8
ZS = 8
YS = 4
F32 = jnp.float32
BF16 = jnp.bfloat16


def nt(a, b):
    return lax.dot_general(a, b, (((1,), (1,)), ((), ())), preferred_element_type=F32)


def nn(a, b):
    return jnp.dot(a, b, preferred_element_type=F32)


def own_head():
    return lax.axis_index("pb") // ZS


def own_z():
    return lax.axis_index("pb") % ZS


def for_tiles(blocks, work, before_slot=None):
    ka = lax.axis_index("ka")

    def step(u, n):
        slot = u // 4
        j = u % 4
        place = jnp.where(j < 2, 2 * ka + j, 2 * (7 - ka) + j - 2)
        block = blocks[slot]
        if before_slot is not None:
            pl.when(u == 4)(functools.partial(before_slot, 1))

        @pl.when(place < block)
        def _():
            work(slot, j, False, n)

        @pl.when(place == block)
        def _():
            work(slot, j, True, n)

        return n + jnp.where(place <= block, 1, 0)

    if before_slot is not None:
        before_slot(0)
    lax.fori_loop(0, 8, step, 0)


def rows_of(index, size):
    return pl.ds(pl.multiple_of(index * size, size), size)


def visible_mask():
    shape = (TILE, TILE)
    return lax.broadcasted_iota(jnp.int32, shape, 0) <= lax.broadcasted_iota(jnp.int32, shape, 1)


def stat_kernel(
    width, blocks, q_hbm, g_hbm, k_hbm, v_hbm,
    out_ref, qt_ref, gt_ref, k_ref, v_ref, kt_ref,
    q_ref, g_ref, m_scr, l_scr, d_scr, sems,
):
    def slot_rows(slot):
        return slice(slot * TILE, (slot + 1) * TILE)

    head = own_head()
    copies = [
        pltpu.make_async_copy(k_hbm.at[head], k_ref, sems.at[0]),
        pltpu.make_async_copy(v_hbm.at[head], v_ref, sems.at[1]),
    ]
    for slot in range(2):
        rows = slot_rows(slot)
        copies.append(pltpu.make_async_copy(q_hbm.at[rows], q_ref.at[rows], sems.at[2 + 2 * slot]))
        copies.append(pltpu.make_async_copy(g_hbm.at[rows], g_ref.at[rows], sems.at[3 + 2 * slot]))
    for copy in copies:
        copy.start()
    factor = width**-0.5 * math.log2(math.e)
    heads = out_ref.shape[0] // 3
    m_scr[...] = jnp.full(m_scr.shape, NEG, F32)
    l_scr[...] = jnp.zeros(l_scr.shape, F32)
    d_scr[...] = jnp.zeros(d_scr.shape, F32)

    def before_slot(slot):
        if slot == 0:
            for copy in copies[:2]:
                copy.wait()
            kt_ref[...] = k_ref[...].T
        for copy in copies[2 + 2 * slot : 4 + 2 * slot]:
            copy.wait()
        for h in range(heads):
            cols = slice(h * width, (h + 1) * width)
            at = (slot * heads + h) * TILE
            qt_ref[:, at : at + TILE] = q_ref[slot_rows(slot), cols].T
            gt_ref[:, at : at + TILE] = g_ref[slot_rows(slot), cols].T

    def work(slot, j, masked, n):
        keys = k_ref[rows_of(j, TILE), :]
        values = v_ref[rows_of(j, TILE), :]
        for h in range(heads):
            at = rows_of(slot * heads + h, TILE)
            scores = nn(keys, qt_ref[:, at]) * factor
            if masked:
                scores = jnp.where(visible_mask(), scores, HIDDEN)
            scores = scores.reshape(TILE // 8, 8, TILE)
            slopes = nn(values, gt_ref[:, at]).reshape(TILE // 8, 8, TILE)
            old = m_scr[h, slot]
            new = jnp.maximum(old, jnp.max(scores, axis=0))
            weights = jnp.exp2(scores - new[None])
            shrink = jnp.exp2(old - new)
            m_scr[h, slot] = new
            l_scr[h, slot] = l_scr[h, slot] * shrink + jnp.sum(weights, axis=0)
            d_scr[h, slot] = d_scr[h, slot] * shrink + jnp.sum(weights * slopes, axis=0)

    for_tiles(blocks, work, before_slot)
    for h in range(heads):
        for slot in range(2):
            cols = slot_rows(slot)
            m = m_scr[h, slot]
            top = jnp.max(m, axis=0, keepdims=True)
            shrink = jnp.exp2(m - top)
            out_ref[h : h + 1, cols] = top
            out_ref[heads + h : heads + h + 1, cols] = jnp.sum(l_scr[h, slot] * shrink, axis=0, keepdims=True)
            out_ref[2 * heads + h : 2 * heads + h + 1, cols] = jnp.sum(d_scr[h, slot] * shrink, axis=0, keepdims=True)


def grad_kernel(
    width, blocks, qt_ref, gt_ref, k_ref, v_ref, kt_ref, stat_ref,
    dq0, dq1, dq2, dq3, own, near_p, near_m, far_p, far_m, half_p, half_m,
    lse_scr, delta_scr, dk_scr, dv_scr, dk_rows, dv_rows, dq_scr,
):
    scale = width**-0.5
    factor = scale * math.log2(math.e)
    heads = lse_scr.shape[0]
    ka_size = stat_ref.shape[0]
    top = stat_ref[0, :heads, :]
    for a in range(1, ka_size):
        top = jnp.maximum(top, stat_ref[a, :heads, :])
    total = jnp.zeros(top.shape, F32)
    dotted = jnp.zeros(top.shape, F32)
    for a in range(ka_size):
        shrink = jnp.exp2(stat_ref[a, :heads, :] - top)
        total += stat_ref[a, heads : 2 * heads, :] * shrink
        dotted += stat_ref[a, 2 * heads :, :] * shrink
    lse_scr[...] = top + jnp.log2(total)
    delta_scr[...] = dotted / total
    dk_scr[...] = jnp.zeros(dk_scr.shape, F32)
    dv_scr[...] = jnp.zeros(dv_scr.shape, F32)
    dq_scr[...] = jnp.zeros(dq_scr.shape, F32)

    def work(slot, j, masked, n):
        kt = kt_ref[:, rows_of(j, TILE)]
        keys = k_ref[rows_of(j, TILE), :]
        values = v_ref[rows_of(j, TILE), :]
        span = GROUP * TILE
        for first in range(0, heads, GROUP):
            at = pl.ds(pl.multiple_of((slot * heads + first) * TILE, TILE), span)
            qt = qt_ref[:, at]
            gt = gt_ref[:, at]
            lows, grads = [], []
            for i in range(GROUP):
                h = first + i
                part = slice(i * TILE, (i + 1) * TILE)
                lse = lse_scr[h : h + 1, rows_of(slot, TILE)]
                delta = delta_scr[h : h + 1, rows_of(slot, TILE)]
                probs = jnp.exp2(nn(keys, qt[:, part]) * factor - lse)
                if masked:
                    probs = jnp.where(visible_mask(), probs, 0.0)
                slopes = nn(values, gt[:, part])
                grads.append((probs * (slopes - delta) * scale).astype(BF16))
                lows.append(probs.astype(BF16))
            low = jnp.concatenate(lows, axis=1)
            grad = jnp.concatenate(grads, axis=1)
            dq_scr[:, at] += nn(kt, grad)
            dv_scr[:, rows_of(j, TILE)] += nt(gt, low)
            dk_scr[:, rows_of(j, TILE)] += nt(qt, grad)

    for_tiles(blocks, work)

    ka = lax.axis_index("ka")
    half = TILE // 2
    for rel, out in enumerate((dq0, dq1, dq2, dq3)):
        share = jnp.bitwise_xor(ka, rel)
        slot, side = share // 2, share % 2
        for h in range(heads):
            start = pl.multiple_of((slot * heads + h) * TILE + side * half, half)
            out[:, h * half : (h + 1) * half] = dq_scr[:, pl.ds(start, half)]

    z = own_z()
    dk_rows[...] = dk_scr[...].T
    dv_rows[...] = dv_scr[...].T

    def put(out, at, rel, pieces):
        for g in pieces:
            row = lax.rem(z + rel, ZS) * 8 + g * 8 * ZS
            for acc in (dk_rows, dv_rows):
                for blk in range(2):
                    start = pl.multiple_of(row + blk * (dk_rows.shape[0] // 2), 8)
                    out[at : at + 8, :] = acc[pl.ds(start, 8), :]
                    at += 8

    every = range(8)
    put(own, 0, 0, every)
    put(near_p, 0, 1, every)
    put(near_p, 256, 3, every)
    put(near_m, 0, 7, every)
    put(near_m, 256, 5, every)
    put(far_p, 0, 2, every)
    put(far_m, 0, 6, every)
    put(half_p, 0, 4, range(4))
    put(half_m, 0, 4, range(4, 8))


def merge_kernel(far_p, got_np, got_hp, far_m, got_nm, got_hm, dq, got_dq, out_p, out_m, out_dq):
    out_dq[...] = dq[...] + got_dq[...]
    half = got_hp.shape[0]
    out_p[:half] = far_p[:half] + got_np[2 * half :][:half] + got_hp[...]
    out_p[half:] = far_p[half:] + got_np[3 * half :]
    out_m[:half] = far_m[:half] + got_nm[2 * half :][:half]
    out_m[half:] = far_m[half:] + got_nm[3 * half :] + got_hm[...]


def sum_kernel(own, near_p, near_m, far_p, far_m, out):
    rows = own.shape[0]
    out[...] = (own[...] + near_p[:rows] + near_m[:rows]) + (far_p[...] + far_m[...])


def place_kernel(parts, dk_ref, dv_ref, scr):
    for head in range(parts.shape[0] // 32):
        for kv in range(2):
            for blk in range(2):
                at = head * 32 + (kv * 2 + blk) * 8
                scr[kv, blk, :, head : head + 1, :] = parts[at : at + 8, :].reshape(8, 1, parts.shape[1])
    for kv, out in enumerate((dk_ref, dv_ref)):
        for blk in range(2):
            out[blk] = scr[kv, blk].reshape(64, out.shape[2]).astype(BF16)


def query_kernel(a_ref, b_ref, c_ref, out_ref):
    rows, width = out_ref.shape[0], a_ref.shape[0]
    for h in range(out_ref.shape[1] // width):
        part = slice(h * rows, (h + 1) * rows)
        total = a_ref[:, part] + b_ref[:, part] + c_ref[:, part]
        out_ref[:, h * width : (h + 1) * width] = total.T.astype(BF16)


def array(shape, dtype=F32):
    return jax.ShapeDtypeStruct(shape, dtype)


SMALL = pl.BlockSpec(memory_space=pltpu.VMEM)
SCALARS = pl.BlockSpec(memory_space=pltpu.SMEM)
LARGE = pl.BlockSpec(memory_space=pltpu.HBM)


def vmem(mib):
    return pltpu.CompilerParams(vmem_limit_bytes=int(mib * 2**20))


def row_stats(blocks, queries, grad_out, keys, values):
    _, key_count, width = keys.shape
    query_count = queries.shape[0]
    heads = queries.shape[1] // width
    turned = array((width, query_count * heads), BF16)
    own = array((key_count, width), BF16)
    return pl.pallas_call(
        functools.partial(stat_kernel, width),
        out_shape=[array((3 * heads, query_count)), turned, turned, own, own, array((width, key_count), BF16)],
        in_specs=[SCALARS] + [LARGE] * 4,
        out_specs=[SMALL] * 6,
        scratch_shapes=[pltpu.VMEM(queries.shape, BF16)] * 2
        + [pltpu.VMEM((heads, 2, 8, TILE), F32)] * 3
        + [pltpu.SemaphoreType.DMA((6,))],
        compiler_params=vmem(24),
        name="row_stats",
    )(blocks, queries, grad_out, keys, values)


def gradients(blocks, turned_q, turned_g, keys, values, turned_k, gathered):
    key_count, width = keys.shape
    heads = gathered.shape[1] // 3
    query_count = gathered.shape[2]
    chunk = (256, width)
    shapes = [chunk, (512, width), (512, width), chunk, chunk, (128, width), (128, width)]
    return pl.pallas_call(
        functools.partial(grad_kernel, width),
        out_shape=[array((width, heads * TILE // 2))] * 4 + [array(s) for s in shapes],
        in_specs=[SCALARS] + [SMALL] * 6,
        out_specs=[SMALL] * 11,
        scratch_shapes=[pltpu.VMEM((heads, query_count), F32)] * 2
        + [pltpu.VMEM((width, key_count), F32)] * 2
        + [pltpu.VMEM((key_count, width), F32)] * 2
        + [pltpu.VMEM((width, query_count * heads), F32)],
        compiler_params=vmem(24),
        name="grads",
    )(blocks, turned_q, turned_g, keys, values, turned_k, gathered)


def on_device(queries, keys, values, grad_out, query_blocks):
    queries, grad_out, keys, values, blocks = (
        pltpu.with_memory_space_constraint(x, pltpu.HBM) for x in (queries, grad_out, keys, values, query_blocks)
    )
    width = keys.shape[2]
    query_count = queries.shape[0]
    pb_size = lax.axis_size("pb")
    stats, turned_q, turned_g, own_k, own_v, turned_k = row_stats(blocks, queries, grad_out, keys, values)
    gathered = lax.all_gather(stats, "ka")

    dq0, dq1, dq2, dq3, own, near_p, near_m, far_p, far_m, half_p, half_m = gradients(
        blocks, turned_q, turned_g, own_k, own_v, turned_k, gathered
    )

    def along_z(x, by):
        return lax.ppermute(x, "pb", [(p, p // ZS * ZS + (p + by) % ZS) for p in range(pb_size)])

    def across_ka(x, by):
        return lax.ppermute(x, "ka", [(a, a ^ by) for a in range(4)])

    got_np = along_z(near_p, 1)
    got_nm = along_z(near_m, ZS - 1)
    got_hp = along_z(half_p, 2)
    got_hm = along_z(half_m, ZS - 2)

    got3 = across_ka(dq3, 1)
    got1 = across_ka(dq1, 1)
    far_p, far_m, for_other = pl.pallas_call(
        merge_kernel,
        out_shape=[array(far_p.shape), array(far_m.shape), array(dq2.shape)],
        in_specs=[SMALL] * 8,
        out_specs=[SMALL] * 3,
        compiler_params=vmem(8),
        name="merge",
    )(far_p, got_np, got_hp, far_m, got_nm, got_hm, dq2, got3)
    got_fp = along_z(far_p, 2)
    got_fm = along_z(far_m, ZS - 2)
    got2 = across_ka(for_other, 2)
    total = pl.pallas_call(
        sum_kernel,
        out_shape=array(own.shape),
        in_specs=[SMALL] * 5,
        out_specs=SMALL,
        compiler_params=vmem(8),
        name="add_parts",
    )(own, got_np, got_nm, got_fp, got_fm)
    lines = [list(range(z, pb_size, ZS)) for z in range(ZS)]
    parts = lax.all_to_all(total, "pb", 0, 0, axis_index_groups=lines, tiled=True)
    grad_keys, grad_values = pl.pallas_call(
        place_kernel,
        out_shape=[array((2, 64, width), BF16)] * 2,
        in_specs=[SMALL],
        out_specs=[SMALL] * 2,
        scratch_shapes=[pltpu.VMEM((2, 2, 8, 8, width), F32)],
        compiler_params=vmem(4),
        name="place_rows",
    )(parts)

    grad_queries = pl.pallas_call(
        query_kernel,
        out_shape=array((query_count // 4, queries.shape[1]), BF16),
        in_specs=[SMALL] * 3,
        out_specs=SMALL,
        compiler_params=vmem(8),
        name="finish_queries",
    )(dq0, got1, got2)
    return grad_queries, grad_keys, grad_values


def solution(mesh):
    placed = (P("pb", None), P(None, "ka", None), P(None, "ka", None), P("pb", None), P("pb"))
    return jax.shard_map(
        on_device,
        mesh=mesh,
        in_specs=placed,
        out_specs=(P(("pb", "ka"), None), P("ka", "pb", None), P("ka", "pb", None)),
        check_vma=False,
    )
```

time: 80 us -> 67.2 us (0.84)
  the two profiles are of different devices: /device:TPU:64 before, /device:TPU:8 now
where the time goes in v3:
time: 67.2 us; the launch traced here: 67 us
  blocking collectives  20.7 us (31%)
  starting transfers between devices  17 us (25%)
  Pallas kernels  15.6 us (23%)
  waiting for transfers between devices  13 us (19%)
  between operations  0.69 us (1%)
    ppermute x6, starting transfers between devices, along_z(): lax.ppermute(x, 'pb', [(p, p // ZS * ZS + (p + by) % ZS) for p in range(p...  15.3 us
    all_to_all x1, blocking collectives, on_device(): lax.all_to_all(total, 'pb', 0, 0, axis_index_groups=lines, tiled=True)  14.6 us
    ppermute x6, waiting for transfers between devices, along_z(): lax.ppermute(x, 'pb', [(p, p // ZS * ZS + (p + by) % ZS) for p in range(p...  13 us
    pallas_call x1, Pallas kernels, gradients(): pl.pallas_call(functools.partial(grad_kernel, width), out_shape=[array((w...  7.36 us
    pallas_call x1, Pallas kernels, row_stats(): pl.pallas_call(functools.partial(stat_kernel, width), out_shape=[array((3...  6.59 us
    all_gather x1, blocking collectives, on_device(): gathered = lax.all_gather(stats, 'ka')  6.12 us
    ppermute x3, starting transfers between devices, across_ka(): return lax.ppermute(x, 'ka', [(a, a ^ by) for a in range(4)])  1.71 us
  transfers between devices with their start and end apart: 9, of which 3 were waited for; matrix products, arithmetic and copies ran while one was open for 0% of the time, Pallas kernels for 1%

profile of v3, /device:TPU:8, one launch (start us, length us, event | category | flops | bytes accessed | tf_op | source)
XLA Modules:
  0.0 67.0 jit_solution(12230783501968945338)
XLA Ops:
  0.6 6.6 %row_stats.1 = (f32[24,512]{1,0:T(8,128)S(1)}, bf16[128,4096]{1,0:T(8,128)(2,1)S(1)}, bf16[128,4096]{1,0:T(8,128)(2,1)S(1)}, bf16[1024,128]{1,0:T(8,128)(2,1)S(1...) custom-call(s32[2]{0:T(128)} %blocks.3, bf16[512,1024]{1,0:T(8,128)(2,1)} %q_hbm.1, ...), custom_call_target="tpu_custom_call" | custom-call | tf_op jit(solution)/shard_map/row_stats/pallas_call | solution.py:279
  7.2 6.1 %all-gather = f32[96,512]{1,0:T(8,128)S(1)} all-gather(f32[24,512]{1,0:T(8,128)S(1)} %get-tuple-element.30), channel_id=2, replica_groups=mesh['pb'=64,'ka'=4] {'ka'}, dimensions={0}, use_global_device_ids=true | all-gather | bytes 245760 | tf_op jit(solution)/shard_map/all_gather | solution.py:320
  13.3 7.4 %grads.1 = (f32[128,1024]{1,0:T(8,128)S(1)}, f32[128,1024]{1,0:T(8,128)S(1)}, f32[128,1024]{1,0:T(8,128)S(1)}, f32[128,1024]{1,0:T(8,128)S(1)}, f32[256,128]{1,0...) custom-call(s32[2]{0:T(128)} %blocks.3, ...), custom_call_target="tpu_custom_call" | custom-call | tf_op jit(solution)/shard_map/grads/pallas_call | solution.py:298
  20.7 0.4 collective-permute-start.5
  21.2 1.4 %collective-permute-start.1 = (f32[512,128]{1,0:T(8,128)S(1)}, f32[512,128]{1,0:T(8,128)S(1)}, u32[]{:S(2)}, u32[]{:S(2)}) collective-permute-start(f32[512,128]{1,0:T(8,128)S(1)} %get-tuple-element.34), channel_id=1, source_target_pairs={{0,4},{4,8},{8,12},{12,16},{16,20},{20,24},{24,28},{28,0},{32,36},... | collective-permute-start | bytes 786440 | tf_op jit(solution)/shard_map/ppermute | solution.py:327
  22.5 5.5 %collective-permute-start.3 = (f32[512,128]{1,0:T(8,128)S(1)}, f32[512,128]{1,0:T(8,128)S(1)}, u32[]{:S(2)}, u32[]{:S(2)}) collective-permute-start(f32[512,128]{1,0:T(8,128)S(1)} %get-tuple-element.37), channel_id=1, source_target_pairs={{0,28},{4,0},{8,4},{12,8},{16,12},{20,16},{24,20},{28,24},{32,60},... | collective-permute-start | bytes 786440 | tf_op jit(solution)/shard_map/ppermute | solution.py:327
  28.0 0.0 collective-permute-start.2
  28.0 4.1 %collective-permute-start.4 = (f32[128,128]{1,0:T(8,128)S(1)}, f32[128,128]{1,0:T(8,128)S(1)}, u32[]{:S(2)}, u32[]{:S(2)}) collective-permute-start(f32[128,128]{1,0:T(8,128)S(1)} %get-tuple-element.38), channel_id=1, source_target_pairs={{0,24},{4,28},{8,0},{12,4},{16,8},{20,12},{24,16},{28,20},{32,56},... | collective-permute-start | bytes 196616 | tf_op jit(solution)/shard_map/ppermute | solution.py:327
  32.1 5.1 %collective-permute-done.2.got_hp = f32[128,128]{1,0:T(8,128)S(1)} collective-permute-done((f32[128,128]{1,0:T(8,128)S(1)}, f32[128,128]{1,0:T(8,128)S(1)}, u32[]{:S(2)}, u32[]{:S(2)}) %collective-permute-start.2) | collective-permute-done | bytes 65568 | tf_op jit(solution)/shard_map/ppermute | solution.py:327
  37.2 0.0 collective-permute-start
  37.2 0.0 collective-permute-done.4.got_hm
  37.3 0.0 collective-permute-done.1.got_np.near_p
  37.3 0.0 collective-permute-done.3.got_nm.near_m
  37.3 0.0 collective-permute-done.5.got_dq
  37.3 0.1 merge.1
  37.4 1.3 %collective-permute-start.6 = (f32[128,1024]{1,0:T(8,128)S(1)}, f32[128,1024]{1,0:T(8,128)S(1)}, u32[]{:S(2)}, u32[]{:S(2)}) collective-permute-start(f32[128,1024]{1,0:T(8,128)S(1)} %get-tuple-element.41), channel_id=1, source_target_pairs={{0,2},{1,3},{2,0},{3,1},{4,6},{5,7},{6,4},{7,5},{8,10},{9,11},{10,... | collective-permute-start | bytes 1572872 | tf_op jit(solution)/shard_map/ppermute | solution.py:330
  38.6 4.3 %collective-permute-start.7 = (f32[256,128]{1,0:T(8,128)S(1)}, f32[256,128]{1,0:T(8,128)S(1)}, u32[]{:S(2)}, u32[]{:S(2)}) collective-permute-start(f32[256,128]{1,0:T(8,128)S(1)} %get-tuple-element.43), channel_id=1, source_target_pairs={{0,8},{4,12},{8,16},{12,20},{16,24},{20,28},{24,0},{28,4},{32,40},... | collective-permute-start | bytes 393224 | tf_op jit(solution)/shard_map/ppermute | solution.py:327
  42.9 0.0 collective-permute-start.8
  43.0 5.1 %collective-permute-done.7.far_p = f32[256,128]{1,0:T(8,128)S(1)} collective-permute-done((f32[256,128]{1,0:T(8,128)S(1)}, f32[256,128]{1,0:T(8,128)S(1)}, u32[]{:S(2)}, u32[]{:S(2)}) %collective-permute-start.7) | collective-permute-done | bytes 131104 | tf_op jit(solution)/shard_map/ppermute | solution.py:327
  48.0 2.8 %collective-permute-done.8.far_m = f32[256,128]{1,0:T(8,128)S(1)} collective-permute-done((f32[256,128]{1,0:T(8,128)S(1)}, f32[256,128]{1,0:T(8,128)S(1)}, u32[]{:S(2)}, u32[]{:S(2)}) %collective-permute-start.8) | collective-permute-done | bytes 131104 | tf_op jit(solution)/shard_map/ppermute | solution.py:327
  50.9 14.6 %all_to_all.11 = f32[8,32,128]{2,1,0:T(8,128)S(1)} all-to-all(f32[8,32,128]{2,1,0:T(8,128)S(1)} %bitcast.5), channel_id=1, replica_groups={{0,32,64,96,128,160,192,224},{4,36,68,100,132,164,196,228},{8,40,72,104..., dimensions={0} | all-to-all | bytes 262144 | tf_op jit(solution)/shard_map/all_to_all | solution.py:359
  65.5 0.7 %place_rows.1 = (bf16[2,64,128]{2,1,0:T(8,128)(2,1)}, bf16[2,64,128]{2,1,0:T(8,128)(2,1)}) custom-call(f32[256,128]{1,0:T(8,128)S(1)} %bitcast.4), custom_call_target="tpu_custom_call" | custom-call | tf_op jit(solution)/shard_map/place_rows/pallas_call | solution.py:360
  66.2 0.0 collective-permute-done.b_ref
  66.2 0.0 collective-permute-done.6.c_ref
  66.2 0.8 %finish_queries.1 = bf16[128,1024]{1,0:T(8,128)(2,1)} custom-call(f32[128,1024]{1,0:T(8,128)S(1)} %get-tuple-element.31.a_ref, f32[128,1024]{1,0:T(8,128)S(1)} %collective-permute-done.b_ref, f32[128,1024]{1,0:T(8,128)S(1)} %collective-permute-done.6.c_ref), custom_call_target="tpu_custom_call" | custom-call | tf_op jit(solution)/shard_map/finish_queries/pallas_call | solution.py:370
  (1 shorter events, 0.0 us)
Async XLA Ops:
  20.7 16.6 %collective-permute-start.5 = (f32[128,1024]{1,0:T(8,128)S(1)}, f32[128,1024]{1,0:T(8,128)S(1)}, u32[]{:S(2)}, u32[]{:S(2)}) collective-permute-start(f32[128,1024]{1,0:T(8,128)S(1)} %get-tuple-element.40), channel_id=1, source_target_pairs={{0,1},{1,0},{2,3},{3,2},{4,5},{5,4},{6,7},{7,6},{8,9},{9,8},{10,11... | collective-permute-start | bytes 1572872 | tf_op jit(solution)/shard_map/ppermute | solution.py:330
  21.2 16.1 %collective-permute-start.1 = (f32[512,128]{1,0:T(8,128)S(1)}, f32[512,128]{1,0:T(8,128)S(1)}, u32[]{:S(2)}, u32[]{:S(2)}) collective-permute-start(f32[512,128]{1,0:T(8,128)S(1)} %get-tuple-element.34), channel_id=1, source_target_pairs={{0,4},{4,8},{8,12},{12,16},{16,20},{20,24},{24,28},{28,0},{32,36},... | collective-permute-start | bytes 786440 | tf_op jit(solution)/shard_map/ppermute | solution.py:327
  22.5 14.7 %collective-permute-start.3 = (f32[512,128]{1,0:T(8,128)S(1)}, f32[512,128]{1,0:T(8,128)S(1)}, u32[]{:S(2)}, u32[]{:S(2)}) collective-permute-start(f32[512,128]{1,0:T(8,128)S(1)} %get-tuple-element.37), channel_id=1, source_target_pairs={{0,28},{4,0},{8,4},{12,8},{16,12},{20,16},{24,20},{28,24},{32,60},... | collective-permute-start | bytes 786440 | tf_op jit(solution)/shard_map/ppermute | solution.py:327
  28.0 9.2 %collective-permute-start.2 = (f32[128,128]{1,0:T(8,128)S(1)}, f32[128,128]{1,0:T(8,128)S(1)}, u32[]{:S(2)}, u32[]{:S(2)}) collective-permute-start(f32[128,128]{1,0:T(8,128)S(1)} %get-tuple-element.35), channel_id=1, source_target_pairs={{0,8},{4,12},{8,16},{12,20},{16,24},{20,28},{24,0},{28,4},{32,40},... | collective-permute-start | bytes 196616 | tf_op jit(solution)/shard_map/ppermute | solution.py:327
  28.0 9.2 %collective-permute-start.4 = (f32[128,128]{1,0:T(8,128)S(1)}, f32[128,128]{1,0:T(8,128)S(1)}, u32[]{:S(2)}, u32[]{:S(2)}) collective-permute-start(f32[128,128]{1,0:T(8,128)S(1)} %get-tuple-element.38), channel_id=1, source_target_pairs={{0,24},{4,28},{8,0},{12,4},{16,8},{20,12},{24,16},{28,20},{32,56},... | collective-permute-start | bytes 196616 | tf_op jit(solution)/shard_map/ppermute | solution.py:327
  37.2 28.9 %collective-permute-start = (f32[128,1024]{1,0:T(8,128)S(1)}, f32[128,1024]{1,0:T(8,128)S(1)}, u32[]{:S(2)}, u32[]{:S(2)}) collective-permute-start(f32[128,1024]{1,0:T(8,128)S(1)} %get-tuple-element.32), channel_id=1, source_target_pairs={{0,1},{1,0},{2,3},{3,2},{4,5},{5,4},{6,7},{7,6},{8,9},{9,8},{10,11... | collective-permute-start | bytes 1572872 | tf_op jit(solution)/shard_map/ppermute | solution.py:330
  37.4 28.8 %collective-permute-start.6 = (f32[128,1024]{1,0:T(8,128)S(1)}, f32[128,1024]{1,0:T(8,128)S(1)}, u32[]{:S(2)}, u32[]{:S(2)}) collective-permute-start(f32[128,1024]{1,0:T(8,128)S(1)} %get-tuple-element.41), channel_id=1, source_target_pairs={{0,2},{1,3},{2,0},{3,1},{4,6},{5,7},{6,4},{7,5},{8,10},{9,11},{10,... | collective-permute-start | bytes 1572872 | tf_op jit(solution)/shard_map/ppermute | solution.py:330
  38.6 9.4 %collective-permute-start.7 = (f32[256,128]{1,0:T(8,128)S(1)}, f32[256,128]{1,0:T(8,128)S(1)}, u32[]{:S(2)}, u32[]{:S(2)}) collective-permute-start(f32[256,128]{1,0:T(8,128)S(1)} %get-tuple-element.43), channel_id=1, source_target_pairs={{0,8},{4,12},{8,16},{12,20},{16,24},{20,28},{24,0},{28,4},{32,40},... | collective-permute-start | bytes 393224 | tf_op jit(solution)/shard_map/ppermute | solution.py:327
  42.9 7.9 %collective-permute-start.8 = (f32[256,128]{1,0:T(8,128)S(1)}, f32[256,128]{1,0:T(8,128)S(1)}, u32[]{:S(2)}, u32[]{:S(2)}) collective-permute-start(f32[256,128]{1,0:T(8,128)S(1)} %get-tuple-element.44), channel_id=1, source_target_pairs={{0,24},{4,28},{8,0},{12,4},{16,8},{20,12},{24,16},{28,20},{32,56},... | collective-permute-start | bytes 393224 | tf_op jit(solution)/shard_map/ppermute | solution.py:327

commit v4 on v3

--- a/solution.py
+++ b/solution.py
@@ -89,7 +89,7 @@
     for copy in copies:
         copy.start()
     factor = width**-0.5 * math.log2(math.e)
-    heads = out_ref.shape[0] // 3
+    heads = out_ref.shape[0] // 2
     m_scr[...] = jnp.full(m_scr.shape, NEG, F32)
     l_scr[...] = jnp.zeros(l_scr.shape, F32)
     d_scr[...] = jnp.zeros(d_scr.shape, F32)
@@ -132,15 +132,16 @@
             m = m_scr[h, slot]
             top = jnp.max(m, axis=0, keepdims=True)
             shrink = jnp.exp2(m - top)
-            out_ref[h : h + 1, cols] = top
-            out_ref[heads + h : heads + h + 1, cols] = jnp.sum(l_scr[h, slot] * shrink, axis=0, keepdims=True)
-            out_ref[2 * heads + h : 2 * heads + h + 1, cols] = jnp.sum(d_scr[h, slot] * shrink, axis=0, keepdims=True)
+            total = jnp.sum(l_scr[h, slot] * shrink, axis=0, keepdims=True)
+            dotted = jnp.sum(d_scr[h, slot] * shrink, axis=0, keepdims=True)
+            out_ref[h : h + 1, cols] = top + jnp.log2(total)
+            out_ref[heads + h : heads + h + 1, cols] = jnp.where(total > 0, dotted / total, 0.0)
 
 
 def grad_kernel(
-    width, blocks, qt_ref, gt_ref, k_ref, v_ref, kt_ref, stat_ref,
-    dq0, dq1, dq2, dq3, own, near_p, near_m, far_p, far_m, half_p, half_m,
-    lse_scr, delta_scr, dk_scr, dv_scr, dk_rows, dv_rows, dq_scr,
+    width, blocks, qt_ref, gt_ref, k_ref, v_ref, stat_ref,
+    stash, own, near_p, near_m, next_p, next_m, far_p, far_m, half_p, half_m,
+    lse_scr, delta_scr, dk_scr, dv_scr, dk_rows, dv_rows,
 ):
     scale = width**-0.5
     factor = scale * math.log2(math.e)
@@ -152,17 +153,15 @@
     total = jnp.zeros(top.shape, F32)
     dotted = jnp.zeros(top.shape, F32)
     for a in range(ka_size):
-        shrink = jnp.exp2(stat_ref[a, :heads, :] - top)
-        total += stat_ref[a, heads : 2 * heads, :] * shrink
-        dotted += stat_ref[a, 2 * heads :, :] * shrink
+        share = jnp.exp2(stat_ref[a, :heads, :] - top)
+        total += share
+        dotted += stat_ref[a, heads:, :] * share
     lse_scr[...] = top + jnp.log2(total)
     delta_scr[...] = dotted / total
     dk_scr[...] = jnp.zeros(dk_scr.shape, F32)
     dv_scr[...] = jnp.zeros(dv_scr.shape, F32)
-    dq_scr[...] = jnp.zeros(dq_scr.shape, F32)
 
     def work(slot, j, masked, n):
-        kt = kt_ref[:, rows_of(j, TILE)]
         keys = k_ref[rows_of(j, TILE), :]
         values = v_ref[rows_of(j, TILE), :]
         span = GROUP * TILE
@@ -184,20 +183,11 @@
                 lows.append(probs.astype(BF16))
             low = jnp.concatenate(lows, axis=1)
             grad = jnp.concatenate(grads, axis=1)
-            dq_scr[:, at] += nn(kt, grad)
+            stash[n, :, first * TILE : first * TILE + span] = grad
             dv_scr[:, rows_of(j, TILE)] += nt(gt, low)
             dk_scr[:, rows_of(j, TILE)] += nt(qt, grad)
 
     for_tiles(blocks, work)
-
-    ka = lax.axis_index("ka")
-    half = TILE // 2
-    for rel, out in enumerate((dq0, dq1, dq2, dq3)):
-        share = jnp.bitwise_xor(ka, rel)
-        slot, side = share // 2, share % 2
-        for h in range(heads):
-            start = pl.multiple_of((slot * heads + h) * TILE + side * half, half)
-            out[:, h * half : (h + 1) * half] = dq_scr[:, pl.ds(start, half)]
 
     z = own_z()
     dk_rows[...] = dk_scr[...].T
@@ -214,28 +204,48 @@
 
     every = range(8)
     put(own, 0, 0, every)
-    put(near_p, 0, 1, every)
-    put(near_p, 256, 3, every)
-    put(near_m, 0, 7, every)
-    put(near_m, 256, 5, every)
+    put(near_p, 0, 3, every)
+    put(near_m, 0, 5, every)
+    put(next_p, 0, 1, every)
+    put(next_m, 0, 7, every)
     put(far_p, 0, 2, every)
     put(far_m, 0, 6, every)
     put(half_p, 0, 4, range(4))
     put(half_m, 0, 4, range(4, 8))
 
 
-def merge_kernel(far_p, got_np, got_hp, far_m, got_nm, got_hm, dq, got_dq, out_p, out_m, out_dq):
-    out_dq[...] = dq[...] + got_dq[...]
+def query_grad_kernel(blocks, kt_ref, stash, dq_near, dq_far, dq_core, dq_scr):
+    dq_scr[...] = jnp.zeros(dq_scr.shape, F32)
+    span = stash.shape[2]
+
+    def work(slot, j, masked, n):
+        del masked
+        kt = kt_ref[:, rows_of(j, TILE)]
+        dq_scr[:, rows_of(slot, span)] += nn(kt, stash[n])
+
+    for_tiles(blocks, work)
+    ka = lax.axis_index("ka")
+    half = TILE // 2
+    heads = span // TILE
+    places = ((dq_near, 0), (dq_core, 0), (dq_far, 0), (dq_core, kt_ref.shape[0]))
+    for rel, (out, at) in enumerate(places):
+        share = jnp.bitwise_xor(ka, rel)
+        slot, side = share // 2, share % 2
+        for h in range(heads):
+            start = pl.multiple_of((slot * heads + h) * TILE + side * half, half)
+            out[at : at + kt_ref.shape[0], h * half : (h + 1) * half] = dq_scr[:, pl.ds(start, half)]
+
+
+def merge_kernel(far_p, got_np, got_hp, far_m, got_nm, got_hm, out_p, out_m):
     half = got_hp.shape[0]
-    out_p[:half] = far_p[:half] + got_np[2 * half :][:half] + got_hp[...]
-    out_p[half:] = far_p[half:] + got_np[3 * half :]
-    out_m[:half] = far_m[:half] + got_nm[2 * half :][:half]
-    out_m[half:] = far_m[half:] + got_nm[3 * half :] + got_hm[...]
-
-
-def sum_kernel(own, near_p, near_m, far_p, far_m, out):
-    rows = own.shape[0]
-    out[...] = (own[...] + near_p[:rows] + near_m[:rows]) + (far_p[...] + far_m[...])
+    out_p[:half] = far_p[:half] + got_np[:half] + got_hp[...]
+    out_p[half:] = far_p[half:] + got_np[half:]
+    out_m[:half] = far_m[:half] + got_nm[:half]
+    out_m[half:] = far_m[half:] + got_nm[half:] + got_hm[...]
+
+
+def sum_kernel(own, next_p, next_m, far_p, far_m, out):
+    out[...] = (own[...] + next_p[...] + next_m[...]) + (far_p[...] + far_m[...])
 
 
 def place_kernel(parts, dk_ref, dv_ref, scr):
@@ -249,11 +259,15 @@
             out[blk] = scr[kv, blk].reshape(64, out.shape[2]).astype(BF16)
 
 
+def add_kernel(a_ref, b_ref, out_ref):
+    out_ref[...] = a_ref[...] + b_ref[a_ref.shape[0] :]
+
+
 def query_kernel(a_ref, b_ref, c_ref, out_ref):
     rows, width = out_ref.shape[0], a_ref.shape[0]
     for h in range(out_ref.shape[1] // width):
         part = slice(h * rows, (h + 1) * rows)
-        total = a_ref[:, part] + b_ref[:, part] + c_ref[:, part]
+        total = a_ref[:, part] + b_ref[:width, part] + c_ref[:, part]
         out_ref[:, h * width : (h + 1) * width] = total.T.astype(BF16)
 
 
@@ -264,6 +278,10 @@
 SMALL = pl.BlockSpec(memory_space=pltpu.VMEM)
 SCALARS = pl.BlockSpec(memory_space=pltpu.SMEM)
 LARGE = pl.BlockSpec(memory_space=pltpu.HBM)
+
+
+def cost(us):
+    return pl.CostEstimate(flops=int(us * 1.15e9), bytes_accessed=0, transcendentals=0)
 
 
 def vmem(mib):
@@ -278,7 +296,7 @@
     own = array((key_count, width), BF16)
     return pl.pallas_call(
         functools.partial(stat_kernel, width),
-        out_shape=[array((3 * heads, query_count)), turned, turned, own, own, array((width, key_count), BF16)],
+        out_shape=[array((2 * heads, query_count)), turned, turned, own, own, array((width, key_count), BF16)],
         in_specs=[SCALARS] + [LARGE] * 4,
         out_specs=[SMALL] * 6,
         scratch_shapes=[pltpu.VMEM(queries.shape, BF16)] * 2
@@ -289,24 +307,38 @@
     )(blocks, queries, grad_out, keys, values)
 
 
-def gradients(blocks, turned_q, turned_g, keys, values, turned_k, gathered):
+def key_gradients(blocks, turned_q, turned_g, keys, values, gathered):
     key_count, width = keys.shape
-    heads = gathered.shape[1] // 3
+    heads = gathered.shape[1] // 2
     query_count = gathered.shape[2]
     chunk = (256, width)
-    shapes = [chunk, (512, width), (512, width), chunk, chunk, (128, width), (128, width)]
+    shapes = [chunk] * 7 + [(128, width)] * 2
     return pl.pallas_call(
         functools.partial(grad_kernel, width),
-        out_shape=[array((width, heads * TILE // 2))] * 4 + [array(s) for s in shapes],
-        in_specs=[SCALARS] + [SMALL] * 6,
-        out_specs=[SMALL] * 11,
+        out_shape=[array((5, TILE, heads * TILE), BF16)] + [array(s) for s in shapes],
+        in_specs=[SCALARS] + [SMALL] * 5,
+        out_specs=[SMALL] * 10,
         scratch_shapes=[pltpu.VMEM((heads, query_count), F32)] * 2
         + [pltpu.VMEM((width, key_count), F32)] * 2
-        + [pltpu.VMEM((key_count, width), F32)] * 2
-        + [pltpu.VMEM((width, query_count * heads), F32)],
+        + [pltpu.VMEM((key_count, width), F32)] * 2,
         compiler_params=vmem(24),
-        name="grads",
-    )(blocks, turned_q, turned_g, keys, values, turned_k, gathered)
+        name="key_grads",
+    )(blocks, turned_q, turned_g, keys, values, gathered)
+
+
+def query_gradients(blocks, turned_k, stash):
+    width = turned_k.shape[0]
+    span = stash.shape[2]
+    return pl.pallas_call(
+        query_grad_kernel,
+        out_shape=[array((width, span // 2))] * 2 + [array((2 * width, span // 2))],
+        in_specs=[SCALARS, SMALL, SMALL],
+        out_specs=[SMALL] * 3,
+        scratch_shapes=[pltpu.VMEM((width, 2 * span), F32)],
+        compiler_params=vmem(16),
+        cost_estimate=cost(2.5),
+        name="query_grads",
+    )(blocks, turned_k, stash)
 
 
 def on_device(queries, keys, values, grad_out, query_blocks):
@@ -319,8 +351,8 @@
     stats, turned_q, turned_g, own_k, own_v, turned_k = row_stats(blocks, queries, grad_out, keys, values)
     gathered = lax.all_gather(stats, "ka")
 
-    dq0, dq1, dq2, dq3, own, near_p, near_m, far_p, far_m, half_p, half_m = gradients(
-        blocks, turned_q, turned_g, own_k, own_v, turned_k, gathered
+    stash, own, near_p, near_m, next_p, next_m, far_p, far_m, half_p, half_m = key_gradients(
+        blocks, turned_q, turned_g, own_k, own_v, gathered
     )
 
     def along_z(x, by):
@@ -332,21 +364,32 @@
     got_np = along_z(near_p, 1)
     got_nm = along_z(near_m, ZS - 1)
     got_hp = along_z(half_p, 2)
+    next_p = along_z(next_p, 1)
+    next_m = along_z(next_m, ZS - 1)
     got_hm = along_z(half_m, ZS - 2)
 
-    got3 = across_ka(dq3, 1)
-    got1 = across_ka(dq1, 1)
-    far_p, far_m, for_other = pl.pallas_call(
+    dq_near, dq_far, dq_core = query_gradients(blocks, turned_k, stash)
+    got_core = across_ka(dq_core, 1)
+    for_other = pl.pallas_call(
+        add_kernel,
+        out_shape=array(dq_far.shape),
+        in_specs=[SMALL] * 2,
+        out_specs=SMALL,
+        compiler_params=vmem(4),
+        name="add_queries",
+    )(dq_far, got_core)
+    got_far = across_ka(for_other, 2)
+    far_p, far_m = pl.pallas_call(
         merge_kernel,
-        out_shape=[array(far_p.shape), array(far_m.shape), array(dq2.shape)],
-        in_specs=[SMALL] * 8,
-        out_specs=[SMALL] * 3,
+        out_shape=[array(far_p.shape), array(far_m.shape)],
+        in_specs=[SMALL] * 6,
+        out_specs=[SMALL] * 2,
         compiler_params=vmem(8),
+        cost_estimate=cost(10),
         name="merge",
-    )(far_p, got_np, got_hp, far_m, got_nm, got_hm, dq2, got3)
+    )(far_p, got_np, got_hp, far_m, got_nm, got_hm)
     got_fp = along_z(far_p, 2)
     got_fm = along_z(far_m, ZS - 2)
-    got2 = across_ka(for_other, 2)
     total = pl.pallas_call(
         sum_kernel,
         out_shape=array(own.shape),
@@ -354,7 +397,7 @@
         out_specs=SMALL,
         compiler_params=vmem(8),
         name="add_parts",
-    )(own, got_np, got_nm, got_fp, got_fm)
+    )(own, next_p, next_m, got_fp, got_fm)
     lines = [list(range(z, pb_size, ZS)) for z in range(ZS)]
     parts = lax.all_to_all(total, "pb", 0, 0, axis_index_groups=lines, tiled=True)
     grad_keys, grad_values = pl.pallas_call(
@@ -364,6 +407,7 @@
         out_specs=[SMALL] * 2,
         scratch_shapes=[pltpu.VMEM((2, 2, 8, 8, width), F32)],
         compiler_params=vmem(4),
+        cost_estimate=cost(3),
         name="place_rows",
     )(parts)
 
@@ -374,7 +418,7 @@
         out_specs=SMALL,
         compiler_params=vmem(8),
         name="finish_queries",
-    )(dq0, got1, got2)
+    )(dq_near, got_core, got_far)
     return grad_queries, grad_keys, grad_values
 
 

time: 67.2 us -> 64.5 us (0.960)
  the two profiles are of different devices: /device:TPU:8 before, /device:TPU:64 now
where the time goes in v4:
time: 64.5 us; the launch traced here: 64.2 us
  blocking collectives  22.5 us (35%)
  Pallas kernels  17.5 us (27%)
  starting transfers between devices  14 us (22%)
  waiting for transfers between devices  9.54 us (15%)
  between operations  0.71 us (1%)
    all_to_all x1, blocking collectives, on_device(): lax.all_to_all(total, 'pb', 0, 0, axis_index_groups=lines, tiled=True)  17.1 us
    ppermute x8, starting transfers between devices, along_z(): lax.ppermute(x, 'pb', [(p, p // ZS * ZS + (p + by) % ZS) for p in range(p...  12.8 us
    ppermute x8, waiting for transfers between devices, along_z(): lax.ppermute(x, 'pb', [(p, p // ZS * ZS + (p + by) % ZS) for p in range(p...  9.54 us
    pallas_call x1, Pallas kernels, key_gradients(): pl.pallas_call(functools.partial(grad_kernel, width), out_shape=[array((5...  6.7 us
    pallas_call x1, Pallas kernels, row_stats(): pl.pallas_call(functools.partial(stat_kernel, width), out_shape=[array((2...  6.62 us
    all_gather x1, blocking collectives, on_device(): gathered = lax.all_gather(stats, 'ka')  5.43 us
    pallas_call x1, Pallas kernels, query_gradients(): pl.pallas_call(query_grad_kernel, out_shape=[array((width, span // 2))] *...  2.5 us
  transfers between devices with their start and end apart: 10, of which 4 were waited for; matrix products, arithmetic and copies ran while one was open for 0% of the time, Pallas kernels for 5%

profile of v4, /device:TPU:64, one launch (start us, length us, event | category | flops | bytes accessed | tf_op | source)
XLA Modules:
  0.0 64.2 jit_solution(15230128182097633367)
XLA Ops:
  0.6 6.6 %row_stats.1 = (f32[16,512]{1,0:T(8,128)S(1)}, bf16[128,4096]{1,0:T(8,128)(2,1)S(1)}, bf16[128,4096]{1,0:T(8,128)(2,1)S(1)}, bf16[1024,128]{1,0:T(8,128)(2,1)S(1...) custom-call(s32[2]{0:T(128)} %blocks.5, bf16[512,1024]{1,0:T(8,128)(2,1)} %q_hbm.1, ...), custom_call_target="tpu_custom_call" | custom-call | tf_op jit(solution)/shard_map/row_stats/pallas_call | solution.py:297
  7.3 5.4 %all-gather = f32[64,512]{1,0:T(8,128)S(1)} all-gather(f32[16,512]{1,0:T(8,128)S(1)} %get-tuple-element.31), channel_id=2, replica_groups=mesh['pb'=64,'ka'=4] {'ka'}, dimensions={0}, use_global_device_ids=true | all-gather | bytes 163840 | tf_op jit(solution)/shard_map/all_gather | solution.py:352
  12.7 6.7 %key_grads.1 = (bf16[5,256,2048]{2,1,0:T(8,128)(2,1)S(1)}, f32[256,128]{1,0:T(8,128)S(1)}, f32[256,128]{1,0:T(8,128)S(1)}, f32[256,128]{1,0:T(8,128)S(1)}, f32[2...) custom-call(s32[2]{0:T(128)} %blocks.5, ...), custom_call_target="tpu_custom_call" | custom-call | tf_op jit(solution)/shard_map/key_grads/pallas_call | solution.py:316
  19.4 4.6 %collective-permute-start.5 = (f32[128,128]{1,0:T(8,128)S(1)}, f32[128,128]{1,0:T(8,128)S(1)}, u32[]{:S(2)}, u32[]{:S(2)}) collective-permute-start(f32[128,128]{1,0:T(8,128)S(1)} %get-tuple-element.41), channel_id=1, source_target_pairs={{0,8},{4,12},{8,16},{12,20},{16,24},{20,28},{24,0},{28,4},{32,40},... | collective-permute-start | bytes 196616 | tf_op jit(solution)/shard_map/ppermute | solution.py:359
  24.0 0.0 collective-permute-start.7
  24.0 3.1 %collective-permute-start.2 = (f32[256,128]{1,0:T(8,128)S(1)}, f32[256,128]{1,0:T(8,128)S(1)}, u32[]{:S(2)}, u32[]{:S(2)}) collective-permute-start(f32[256,128]{1,0:T(8,128)S(1)} %get-tuple-element.37), channel_id=1, source_target_pairs={{0,4},{4,8},{8,12},{12,16},{16,20},{20,24},{24,28},{28,0},{32,36},... | collective-permute-start | bytes 393224 | tf_op jit(solution)/shard_map/ppermute | solution.py:359
  27.1 1.6 %collective-permute-start.4 = (f32[256,128]{1,0:T(8,128)S(1)}, f32[256,128]{1,0:T(8,128)S(1)}, u32[]{:S(2)}, u32[]{:S(2)}) collective-permute-start(f32[256,128]{1,0:T(8,128)S(1)} %get-tuple-element.40), channel_id=1, source_target_pairs={{0,4},{4,8},{8,12},{12,16},{16,20},{20,24},{24,28},{28,0},{32,36},... | collective-permute-start | bytes 393224 | tf_op jit(solution)/shard_map/ppermute | solution.py:359
  28.7 0.4 collective-permute-start.6
  29.1 2.5 %query_grads.1 = (f32[128,1024]{1,0:T(8,128)S(1)}, f32[128,1024]{1,0:T(8,128)S(1)}, f32[256,1024]{1,0:T(8,128)S(1)}) custom-call(s32[2]{0:T(128)} %blocks.5, bf16[128,1024]{1,0:T(8,128)(2,1)S(1)} %get-tuple-element.26.kt_ref, bf16[5,256,2048]{2,1,0:T(8,128)(2,1)S(1)} %get-tuple-element.32.stash), custom_call_target="tpu_custom_call" | custom-call | flops 2875000064 | tf_op jit(solution)/shard_map/query_grads/pallas_call | solution.py:332
  31.6 0.0 collective-permute-done.5.got_hp
  31.6 0.1 collective-permute-start.3
  31.7 0.0 collective-permute-done.7.got_hm
  31.7 0.1 collective-permute-start
  31.8 1.2 %collective-permute-done.4.got_np = f32[256,128]{1,0:T(8,128)S(1)} collective-permute-done((f32[256,128]{1,0:T(8,128)S(1)}, f32[256,128]{1,0:T(8,128)S(1)}, u32[]{:S(2)}, u32[]{:S(2)}) %collective-permute-start.4) | collective-permute-done | bytes 131104 | tf_op jit(solution)/shard_map/ppermute | solution.py:359
  33.0 2.9 %collective-permute-done.6.got_nm = f32[256,128]{1,0:T(8,128)S(1)} collective-permute-done((f32[256,128]{1,0:T(8,128)S(1)}, f32[256,128]{1,0:T(8,128)S(1)}, u32[]{:S(2)}, u32[]{:S(2)}) %collective-permute-start.6) | collective-permute-done | bytes 131104 | tf_op jit(solution)/shard_map/ppermute | solution.py:359
  35.9 2.0 %collective-permute-start.8 = (f32[256,128]{1,0:T(8,128)S(1)}, f32[256,128]{1,0:T(8,128)S(1)}, u32[]{:S(2)}, u32[]{:S(2)}) collective-permute-start(f32[256,128]{1,0:T(8,128)S(1)} %get-tuple-element.45), channel_id=1, source_target_pairs={{0,8},{4,12},{8,16},{12,20},{16,24},{20,28},{24,0},{28,4},{32,40},... | collective-permute-start | bytes 393224 | tf_op jit(solution)/shard_map/ppermute | solution.py:359
  37.9 1.0 %collective-permute-start.9 = (f32[256,128]{1,0:T(8,128)S(1)}, f32[256,128]{1,0:T(8,128)S(1)}, u32[]{:S(2)}, u32[]{:S(2)}) collective-permute-start(f32[256,128]{1,0:T(8,128)S(1)} %get-tuple-element.46), channel_id=1, source_target_pairs={{0,24},{4,28},{8,0},{12,4},{16,8},{20,12},{24,16},{28,20},{32,56},... | collective-permute-start | bytes 393224 | tf_op jit(solution)/shard_map/ppermute | solution.py:359
  38.9 0.0 collective-permute-done.b_ref
  38.9 0.1 add_queries.1
  39.0 1.1 %collective-permute-start.1 = (f32[128,1024]{1,0:T(8,128)S(1)}, f32[128,1024]{1,0:T(8,128)S(1)}, u32[]{:S(2)}, u32[]{:S(2)}) collective-permute-start(f32[128,1024]{1,0:T(8,128)S(1)} %add_queries.1), channel_id=1, source_target_pairs={{0,2},{1,3},{2,0},{3,1},{4,6},{5,7},{6,4},{7,5},{8,10},{9,11},{10,... | collective-permute-start | bytes 1572872 | tf_op jit(solution)/shard_map/ppermute | solution.py:362
  40.1 0.0 collective-permute-done.2.next_p
  40.1 0.0 collective-permute-done.3.next_m
  40.1 3.0 %collective-permute-done.8.far_p = f32[256,128]{1,0:T(8,128)S(1)} collective-permute-done((f32[256,128]{1,0:T(8,128)S(1)}, f32[256,128]{1,0:T(8,128)S(1)}, u32[]{:S(2)}, u32[]{:S(2)}) %collective-permute-start.8) | collective-permute-done | bytes 131104 | tf_op jit(solution)/shard_map/ppermute | solution.py:359
  43.1 2.5 %collective-permute-done.9.far_m = f32[256,128]{1,0:T(8,128)S(1)} collective-permute-done((f32[256,128]{1,0:T(8,128)S(1)}, f32[256,128]{1,0:T(8,128)S(1)}, u32[]{:S(2)}, u32[]{:S(2)}) %collective-permute-start.9) | collective-permute-done | bytes 131104 | tf_op jit(solution)/shard_map/ppermute | solution.py:359
  45.6 17.1 %all_to_all.11 = f32[8,32,128]{2,1,0:T(8,128)S(1)} all-to-all(f32[8,32,128]{2,1,0:T(8,128)S(1)} %bitcast.4), channel_id=1, replica_groups={{0,32,64,96,128,160,192,224},{4,36,68,100,132,164,196,228},{8,40,72,104..., dimensions={0} | all-to-all | bytes 262144 | tf_op jit(solution)/shard_map/all_to_all | solution.py:402
  62.7 0.7 %place_rows.1 = (bf16[2,64,128]{2,1,0:T(8,128)(2,1)}, bf16[2,64,128]{2,1,0:T(8,128)(2,1)}) custom-call(f32[256,128]{1,0:T(8,128)S(1)} %bitcast.5), custom_call_target="tpu_custom_call" | custom-call | flops 3449999872 | tf_op jit(solution)/shard_map/place_rows/pallas_call | solution.py:403
  63.4 0.0 collective-permute-done.1.c_ref
  63.4 0.8 %finish_queries.1 = bf16[128,1024]{1,0:T(8,128)(2,1)} custom-call(f32[128,1024]{1,0:T(8,128)S(1)} %get-tuple-element.33.a_ref, f32[256,1024]{1,0:T(8,128)S(1)} %collective-permute-done.b_ref, f32[128,1024]{1,0:T(8,128)S(1)} %collective-permute-done.1.c_ref), custom_call_target="tpu_custom_call" | custom-call | tf_op jit(solution)/shard_map/finish_queries/pallas_call | solution.py:414
  (2 shorter events, 0.1 us)
Async XLA Ops:
  19.4 12.2 %collective-permute-start.5 = (f32[128,128]{1,0:T(8,128)S(1)}, f32[128,128]{1,0:T(8,128)S(1)}, u32[]{:S(2)}, u32[]{:S(2)}) collective-permute-start(f32[128,128]{1,0:T(8,128)S(1)} %get-tuple-element.41), channel_id=1, source_target_pairs={{0,8},{4,12},{8,16},{12,20},{16,24},{20,28},{24,0},{28,4},{32,40},... | collective-permute-start | bytes 196616 | tf_op jit(solution)/shard_map/ppermute | solution.py:359
  24.0 7.8 %collective-permute-start.7 = (f32[128,128]{1,0:T(8,128)S(1)}, f32[128,128]{1,0:T(8,128)S(1)}, u32[]{:S(2)}, u32[]{:S(2)}) collective-permute-start(f32[128,128]{1,0:T(8,128)S(1)} %get-tuple-element.44), channel_id=1, source_target_pairs={{0,24},{4,28},{8,0},{12,4},{16,8},{20,12},{24,16},{28,20},{32,56},... | collective-permute-start | bytes 196616 | tf_op jit(solution)/shard_map/ppermute | solution.py:359
  24.0 16.1 %collective-permute-start.2 = (f32[256,128]{1,0:T(8,128)S(1)}, f32[256,128]{1,0:T(8,128)S(1)}, u32[]{:S(2)}, u32[]{:S(2)}) collective-permute-start(f32[256,128]{1,0:T(8,128)S(1)} %get-tuple-element.37), channel_id=1, source_target_pairs={{0,4},{4,8},{8,12},{12,16},{16,20},{20,24},{24,28},{28,0},{32,36},... | collective-permute-start | bytes 393224 | tf_op jit(solution)/shard_map/ppermute | solution.py:359
  27.1 5.9 %collective-permute-start.4 = (f32[256,128]{1,0:T(8,128)S(1)}, f32[256,128]{1,0:T(8,128)S(1)}, u32[]{:S(2)}, u32[]{:S(2)}) collective-permute-start(f32[256,128]{1,0:T(8,128)S(1)} %get-tuple-element.40), channel_id=1, source_target_pairs={{0,4},{4,8},{8,12},{12,16},{16,20},{20,24},{24,28},{28,0},{32,36},... | collective-permute-start | bytes 393224 | tf_op jit(solution)/shard_map/ppermute | solution.py:359
  28.7 7.2 %collective-permute-start.6 = (f32[256,128]{1,0:T(8,128)S(1)}, f32[256,128]{1,0:T(8,128)S(1)}, u32[]{:S(2)}, u32[]{:S(2)}) collective-permute-start(f32[256,128]{1,0:T(8,128)S(1)} %get-tuple-element.43), channel_id=1, source_target_pairs={{0,28},{4,0},{8,4},{12,8},{16,12},{20,16},{24,20},{28,24},{32,60},... | collective-permute-start | bytes 393224 | tf_op jit(solution)/shard_map/ppermute | solution.py:359
  31.6 8.4 %collective-permute-start.3 = (f32[256,128]{1,0:T(8,128)S(1)}, f32[256,128]{1,0:T(8,128)S(1)}, u32[]{:S(2)}, u32[]{:S(2)}) collective-permute-start(f32[256,128]{1,0:T(8,128)S(1)} %get-tuple-element.38), channel_id=1, source_target_pairs={{0,28},{4,0},{8,4},{12,8},{16,12},{20,16},{24,20},{28,24},{32,60},... | collective-permute-start | bytes 393224 | tf_op jit(solution)/shard_map/ppermute | solution.py:359
  31.7 7.2 %collective-permute-start = (f32[256,1024]{1,0:T(8,128)S(1)}, f32[256,1024]{1,0:T(8,128)S(1)}, u32[]{:S(2)}, u32[]{:S(2)}) collective-permute-start(f32[256,1024]{1,0:T(8,128)S(1)} %get-tuple-element.34), channel_id=1, source_target_pairs={{0,1},{1,0},{2,3},{3,2},{4,5},{5,4},{6,7},{7,6},{8,9},{9,8},{10,11... | collective-permute-start | bytes 3145736 | tf_op jit(solution)/shard_map/ppermute | solution.py:362
  35.9 7.2 %collective-permute-start.8 = (f32[256,128]{1,0:T(8,128)S(1)}, f32[256,128]{1,0:T(8,128)S(1)}, u32[]{:S(2)}, u32[]{:S(2)}) collective-permute-start(f32[256,128]{1,0:T(8,128)S(1)} %get-tuple-element.45), channel_id=1, source_target_pairs={{0,8},{4,12},{8,16},{12,20},{16,24},{20,28},{24,0},{28,4},{32,40},... | collective-permute-start | bytes 393224 | tf_op jit(solution)/shard_map/ppermute | solution.py:359
  37.9 7.6 %collective-permute-start.9 = (f32[256,128]{1,0:T(8,128)S(1)}, f32[256,128]{1,0:T(8,128)S(1)}, u32[]{:S(2)}, u32[]{:S(2)}) collective-permute-start(f32[256,128]{1,0:T(8,128)S(1)} %get-tuple-element.46), channel_id=1, source_target_pairs={{0,24},{4,28},{8,0},{12,4},{16,8},{20,12},{24,16},{28,20},{32,56},... | collective-permute-start | bytes 393224 | tf_op jit(solution)/shard_map/ppermute | solution.py:359
  39.0 24.4 %collective-permute-start.1 = (f32[128,1024]{1,0:T(8,128)S(1)}, f32[128,1024]{1,0:T(8,128)S(1)}, u32[]{:S(2)}, u32[]{:S(2)}) collective-permute-start(f32[128,1024]{1,0:T(8,128)S(1)} %add_queries.1), channel_id=1, source_target_pairs={{0,2},{1,3},{2,0},{3,1},{4,6},{5,7},{6,4},{7,5},{8,10},{9,11},{10,... | collective-permute-start | bytes 1572872 | tf_op jit(solution)/shard_map/ppermute | solution.py:362

commit v5 on v4

--- a/solution.py
+++ b/solution.py
@@ -11,7 +11,7 @@
 NEG = -1e30
 HIDDEN = -2e30
 TILE = 256
-GROUP = 8
+GROUP = 4
 ZS = 8
 YS = 4
 F32 = jnp.float32
@@ -69,23 +69,24 @@
     return lax.broadcasted_iota(jnp.int32, shape, 0) <= lax.broadcasted_iota(jnp.int32, shape, 1)
 
 
-def stat_kernel(
-    width, blocks, q_hbm, g_hbm, k_hbm, v_hbm,
-    out_ref, qt_ref, gt_ref, k_ref, v_ref, kt_ref,
-    q_ref, g_ref, m_scr, l_scr, d_scr, sems,
-):
-    def slot_rows(slot):
-        return slice(slot * TILE, (slot + 1) * TILE)
-
+def slot_rows(slot):
+    return slice(slot * TILE, (slot + 1) * TILE)
+
+
+def copies_in(q_hbm, g_hbm, k_hbm, v_hbm, q_ref, g_ref, k_ref, v_ref, sems):
     head = own_head()
-    copies = [
-        pltpu.make_async_copy(k_hbm.at[head], k_ref, sems.at[0]),
-        pltpu.make_async_copy(v_hbm.at[head], v_ref, sems.at[1]),
-    ]
+    pairs = [(k_hbm.at[head], k_ref), (v_hbm.at[head], v_ref)]
     for slot in range(2):
         rows = slot_rows(slot)
-        copies.append(pltpu.make_async_copy(q_hbm.at[rows], q_ref.at[rows], sems.at[2 + 2 * slot]))
-        copies.append(pltpu.make_async_copy(g_hbm.at[rows], g_ref.at[rows], sems.at[3 + 2 * slot]))
+        pairs += [(q_hbm.at[rows], q_ref.at[rows]), (g_hbm.at[rows], g_ref.at[rows])]
+    return [pltpu.make_async_copy(src, dst, sems.at[i]) for i, (src, dst) in enumerate(pairs)]
+
+
+def stat_kernel(
+    width, blocks, q_hbm, g_hbm, k_hbm, v_hbm, out_ref,
+    q_ref, g_ref, k_ref, v_ref, m_scr, l_scr, d_scr, sems,
+):
+    copies = copies_in(q_hbm, g_hbm, k_hbm, v_hbm, q_ref, g_ref, k_ref, v_ref, sems)
     for copy in copies:
         copy.start()
     factor = width**-0.5 * math.log2(math.e)
@@ -95,28 +96,19 @@
     d_scr[...] = jnp.zeros(d_scr.shape, F32)
 
     def before_slot(slot):
-        if slot == 0:
-            for copy in copies[:2]:
-                copy.wait()
-            kt_ref[...] = k_ref[...].T
-        for copy in copies[2 + 2 * slot : 4 + 2 * slot]:
+        for copy in copies[:2] * (slot == 0) + copies[2 + 2 * slot : 4 + 2 * slot]:
             copy.wait()
-        for h in range(heads):
-            cols = slice(h * width, (h + 1) * width)
-            at = (slot * heads + h) * TILE
-            qt_ref[:, at : at + TILE] = q_ref[slot_rows(slot), cols].T
-            gt_ref[:, at : at + TILE] = g_ref[slot_rows(slot), cols].T
 
     def work(slot, j, masked, n):
         keys = k_ref[rows_of(j, TILE), :]
         values = v_ref[rows_of(j, TILE), :]
         for h in range(heads):
-            at = rows_of(slot * heads + h, TILE)
-            scores = nn(keys, qt_ref[:, at]) * factor
+            cols = slice(h * width, (h + 1) * width)
+            scores = nt(keys, q_ref[rows_of(slot, TILE), cols]) * factor
             if masked:
                 scores = jnp.where(visible_mask(), scores, HIDDEN)
             scores = scores.reshape(TILE // 8, 8, TILE)
-            slopes = nn(values, gt_ref[:, at]).reshape(TILE // 8, 8, TILE)
+            slopes = nt(values, g_ref[rows_of(slot, TILE), cols]).reshape(TILE // 8, 8, TILE)
             old = m_scr[h, slot]
             new = jnp.maximum(old, jnp.max(scores, axis=0))
             weights = jnp.exp2(scores - new[None])
@@ -138,24 +130,50 @@
             out_ref[heads + h : heads + h + 1, cols] = jnp.where(total > 0, dotted / total, 0.0)
 
 
+def turn_kernel(
+    q_hbm, g_hbm, k_hbm, v_hbm, qt_ref, gt_ref, k_ref, v_ref, kt_ref, q_ref, g_ref, sems
+):
+    copies = copies_in(q_hbm, g_hbm, k_hbm, v_hbm, q_ref, g_ref, k_ref, v_ref, sems)
+    width = k_ref.shape[1]
+    heads = q_ref.shape[1] // width
+    for copy in copies:
+        copy.start()
+    for copy in copies[:2]:
+        copy.wait()
+    kt_ref[...] = k_ref[...].T
+    for slot in range(2):
+        for copy in copies[2 + 2 * slot : 4 + 2 * slot]:
+            copy.wait()
+        for h in range(heads):
+            cols = slice(h * width, (h + 1) * width)
+            at = (slot * heads + h) * TILE
+            qt_ref[:, at : at + TILE] = q_ref[slot_rows(slot), cols].T
+            gt_ref[:, at : at + TILE] = g_ref[slot_rows(slot), cols].T
+
+
 def grad_kernel(
-    width, blocks, qt_ref, gt_ref, k_ref, v_ref, stat_ref,
+    width, blocks, qt_ref, gt_ref, k_ref, v_ref, *refs,
+):
+    grad_body(width, blocks, qt_ref, gt_ref, k_ref, v_ref, refs[:4], *refs[4:])
+
+
+def grad_body(
+    width, blocks, qt_ref, gt_ref, k_ref, v_ref, stats,
     stash, own, near_p, near_m, next_p, next_m, far_p, far_m, half_p, half_m,
     lse_scr, delta_scr, dk_scr, dv_scr, dk_rows, dv_rows,
 ):
     scale = width**-0.5
     factor = scale * math.log2(math.e)
     heads = lse_scr.shape[0]
-    ka_size = stat_ref.shape[0]
-    top = stat_ref[0, :heads, :]
-    for a in range(1, ka_size):
-        top = jnp.maximum(top, stat_ref[a, :heads, :])
+    top = stats[0][:heads]
+    for stat in stats[1:]:
+        top = jnp.maximum(top, stat[:heads])
     total = jnp.zeros(top.shape, F32)
     dotted = jnp.zeros(top.shape, F32)
-    for a in range(ka_size):
-        share = jnp.exp2(stat_ref[a, :heads, :] - top)
+    for stat in stats:
+        share = jnp.exp2(stat[:heads] - top)
         total += share
-        dotted += stat_ref[a, heads:, :] * share
+        dotted += stat[heads:] * share
     lse_scr[...] = top + jnp.log2(total)
     delta_scr[...] = dotted / total
     dk_scr[...] = jnp.zeros(dk_scr.shape, F32)
@@ -165,6 +183,8 @@
         keys = k_ref[rows_of(j, TILE), :]
         values = v_ref[rows_of(j, TILE), :]
         span = GROUP * TILE
+        value_sum = dv_scr[:, rows_of(j, TILE)]
+        key_sum = dk_scr[:, rows_of(j, TILE)]
         for first in range(0, heads, GROUP):
             at = pl.ds(pl.multiple_of((slot * heads + first) * TILE, TILE), span)
             qt = qt_ref[:, at]
@@ -184,8 +204,10 @@
             low = jnp.concatenate(lows, axis=1)
             grad = jnp.concatenate(grads, axis=1)
             stash[n, :, first * TILE : first * TILE + span] = grad
-            dv_scr[:, rows_of(j, TILE)] += nt(gt, low)
-            dk_scr[:, rows_of(j, TILE)] += nt(qt, grad)
+            value_sum = value_sum + nt(gt, low)
+            key_sum = key_sum + nt(qt, grad)
+        dv_scr[:, rows_of(j, TILE)] = value_sum
+        dk_scr[:, rows_of(j, TILE)] = key_sum
 
     for_tiles(blocks, work)
 
@@ -244,16 +266,31 @@
     out_m[half:] = far_m[half:] + got_nm[half:] + got_hm[...]
 
 
-def sum_kernel(own, next_p, next_m, far_p, far_m, out):
-    out[...] = (own[...] + next_p[...] + next_m[...]) + (far_p[...] + far_m[...])
-
-
-def place_kernel(parts, dk_ref, dv_ref, scr):
-    for head in range(parts.shape[0] // 32):
-        for kv in range(2):
-            for blk in range(2):
-                at = head * 32 + (kv * 2 + blk) * 8
-                scr[kv, blk, :, head : head + 1, :] = parts[at : at + 8, :].reshape(8, 1, parts.shape[1])
+def sum_kernel(own, next_p, next_m, far_p, far_m, *outs):
+    xh, y = own_head() // YS, own_head() % YS
+    size = outs[0].shape[1]
+    for rel, out in enumerate(outs):
+        for i, x in enumerate((xh, 1 - xh)):
+            rows = rows_of(x * YS + lax.rem(y + rel, YS), size)
+            out[i] = (own[rows, :] + next_p[rows, :] + next_m[rows, :]) + (far_p[rows, :] + far_m[rows, :])
+
+
+def cross_kernel(own, from1, from2, from3, out):
+    for rel, part in enumerate((own, from1, from2, from3)):
+        out[rel] = part[1]
+
+
+def place_kernel(own, from1, from2, from3, crossed, after, dk_ref, dv_ref, scr):
+    del after
+    xh, y = own_head() // YS, own_head() % YS
+    for rel, near in enumerate((own, from1, from2, from3)):
+        from_y = lax.rem(y + YS - rel, YS)
+        for part, from_x in ((near[0], xh), (crossed[rel], 1 - xh)):
+            head = from_x * YS + from_y
+            for kv in range(2):
+                for blk in range(2):
+                    at = (kv * 2 + blk) * 8
+                    scr[kv, blk, :, pl.ds(head, 1), :] = part[at : at + 8, :].reshape(8, 1, part.shape[1])
     for kv, out in enumerate((dk_ref, dv_ref)):
         for blk in range(2):
             out[blk] = scr[kv, blk].reshape(64, out.shape[2]).astype(BF16)
@@ -263,7 +300,8 @@
     out_ref[...] = a_ref[...] + b_ref[a_ref.shape[0] :]
 
 
-def query_kernel(a_ref, b_ref, c_ref, out_ref):
+def query_kernel(a_ref, b_ref, c_ref, out_ref, token_ref):
+    token_ref[...] = jnp.zeros(token_ref.shape, F32)
     rows, width = out_ref.shape[0], a_ref.shape[0]
     for h in range(out_ref.shape[1] // width):
         part = slice(h * rows, (h + 1) * rows)
@@ -292,14 +330,13 @@
     _, key_count, width = keys.shape
     query_count = queries.shape[0]
     heads = queries.shape[1] // width
-    turned = array((width, query_count * heads), BF16)
-    own = array((key_count, width), BF16)
     return pl.pallas_call(
         functools.partial(stat_kernel, width),
-        out_shape=[array((2 * heads, query_count)), turned, turned, own, own, array((width, key_count), BF16)],
+        out_shape=array((2 * heads, query_count)),
         in_specs=[SCALARS] + [LARGE] * 4,
-        out_specs=[SMALL] * 6,
+        out_specs=SMALL,
         scratch_shapes=[pltpu.VMEM(queries.shape, BF16)] * 2
+        + [pltpu.VMEM((key_count, width), BF16)] * 2
         + [pltpu.VMEM((heads, 2, 8, TILE), F32)] * 3
         + [pltpu.SemaphoreType.DMA((6,))],
         compiler_params=vmem(24),
@@ -307,23 +344,39 @@
     )(blocks, queries, grad_out, keys, values)
 
 
-def key_gradients(blocks, turned_q, turned_g, keys, values, gathered):
+def turned_inputs(queries, grad_out, keys, values):
+    _, key_count, width = keys.shape
+    turned = array((width, queries.size // width), BF16)
+    own = array((key_count, width), BF16)
+    return pl.pallas_call(
+        turn_kernel,
+        out_shape=[turned, turned, own, own, array((width, key_count), BF16)],
+        in_specs=[LARGE] * 4,
+        out_specs=[SMALL] * 5,
+        scratch_shapes=[pltpu.VMEM(queries.shape, BF16)] * 2 + [pltpu.SemaphoreType.DMA((6,))],
+        compiler_params=vmem(16),
+        cost_estimate=cost(3),
+        name="turn_inputs",
+    )(queries, grad_out, keys, values)
+
+
+def key_gradients(blocks, turned_q, turned_g, keys, values, stats):
     key_count, width = keys.shape
-    heads = gathered.shape[1] // 2
-    query_count = gathered.shape[2]
+    heads = stats[0].shape[0] // 2
+    query_count = stats[0].shape[1]
     chunk = (256, width)
     shapes = [chunk] * 7 + [(128, width)] * 2
     return pl.pallas_call(
         functools.partial(grad_kernel, width),
         out_shape=[array((5, TILE, heads * TILE), BF16)] + [array(s) for s in shapes],
-        in_specs=[SCALARS] + [SMALL] * 5,
+        in_specs=[SCALARS] + [SMALL] * 8,
         out_specs=[SMALL] * 10,
         scratch_shapes=[pltpu.VMEM((heads, query_count), F32)] * 2
         + [pltpu.VMEM((width, key_count), F32)] * 2
         + [pltpu.VMEM((key_count, width), F32)] * 2,
         compiler_params=vmem(24),
         name="key_grads",
-    )(blocks, turned_q, turned_g, keys, values, gathered)
+    )(blocks, turned_q, turned_g, keys, values, *stats)
 
 
 def query_gradients(blocks, turned_k, stash):
@@ -332,7 +385,7 @@
     return pl.pallas_call(
         query_grad_kernel,
         out_shape=[array((width, span // 2))] * 2 + [array((2 * width, span // 2))],
-        in_specs=[SCALARS, SMALL, SMALL],
+        in_specs=[SCALARS] + [SMALL] * 2,
         out_specs=[SMALL] * 3,
         scratch_shapes=[pltpu.VMEM((width, 2 * span), F32)],
         compiler_params=vmem(16),
@@ -348,27 +401,33 @@
     width = keys.shape[2]
     query_count = queries.shape[0]
     pb_size = lax.axis_size("pb")
-    stats, turned_q, turned_g, own_k, own_v, turned_k = row_stats(blocks, queries, grad_out, keys, values)
-    gathered = lax.all_gather(stats, "ka")
-
+
+    def across_ka(x, by):
+        return lax.ppermute(x, "ka", [(a, a ^ by) for a in range(4)])
+
+    own_stats = row_stats(blocks, queries, grad_out, keys, values)
+    stats = [own_stats] + [across_ka(own_stats, by) for by in (2, 3, 1)]
+    turned_q, turned_g, own_k, own_v, turned_k = turned_inputs(queries, grad_out, keys, values)
     stash, own, near_p, near_m, next_p, next_m, far_p, far_m, half_p, half_m = key_gradients(
-        blocks, turned_q, turned_g, own_k, own_v, gathered
+        blocks, turned_q, turned_g, own_k, own_v, stats
     )
+
+    def along_y(x, by):
+        return lax.ppermute(
+            x, "pb", [(p, (p // (ZS * YS) * YS + (p // ZS + by) % YS) * ZS + p % ZS) for p in range(pb_size)]
+        )
 
     def along_z(x, by):
         return lax.ppermute(x, "pb", [(p, p // ZS * ZS + (p + by) % ZS) for p in range(pb_size)])
-
-    def across_ka(x, by):
-        return lax.ppermute(x, "ka", [(a, a ^ by) for a in range(4)])
 
     got_np = along_z(near_p, 1)
     got_nm = along_z(near_m, ZS - 1)
     got_hp = along_z(half_p, 2)
+    got_hm = along_z(half_m, ZS - 2)
+
+    dq_near, dq_far, dq_core = query_gradients(blocks, turned_k, stash)
     next_p = along_z(next_p, 1)
     next_m = along_z(next_m, ZS - 1)
-    got_hm = along_z(half_m, ZS - 2)
-
-    dq_near, dq_far, dq_core = query_gradients(blocks, turned_k, stash)
     got_core = across_ka(dq_core, 1)
     for_other = pl.pallas_call(
         add_kernel,
@@ -390,35 +449,44 @@
     )(far_p, got_np, got_hp, far_m, got_nm, got_hm)
     got_fp = along_z(far_p, 2)
     got_fm = along_z(far_m, ZS - 2)
-    total = pl.pallas_call(
+    parts = pl.pallas_call(
         sum_kernel,
-        out_shape=array(own.shape),
+        out_shape=[array((2, 32, width))] * YS,
         in_specs=[SMALL] * 5,
-        out_specs=SMALL,
+        out_specs=[SMALL] * YS,
         compiler_params=vmem(8),
         name="add_parts",
     )(own, next_p, next_m, got_fp, got_fm)
-    lines = [list(range(z, pb_size, ZS)) for z in range(ZS)]
-    parts = lax.all_to_all(total, "pb", 0, 0, axis_index_groups=lines, tiled=True)
+    parts = [parts[0]] + [along_y(parts[k], k) for k in range(1, YS)]
+    crossed = pl.pallas_call(
+        cross_kernel,
+        out_shape=array((YS, 32, width)),
+        in_specs=[SMALL] * YS,
+        out_specs=SMALL,
+        compiler_params=vmem(4),
+        cost_estimate=cost(3),
+        name="cross_parts",
+    )(*parts)
+    crossed = lax.ppermute(crossed, "pb", [(p, (p + pb_size // 2) % pb_size) for p in range(pb_size)])
+    grad_queries, token = pl.pallas_call(
+        query_kernel,
+        out_shape=[array((query_count // 4, queries.shape[1]), BF16), array((8, 128))],
+        in_specs=[SMALL] * 3,
+        out_specs=[SMALL] * 2,
+        compiler_params=vmem(8),
+        name="finish_queries",
+    )(dq_near, got_core, got_far)
     grad_keys, grad_values = pl.pallas_call(
         place_kernel,
         out_shape=[array((2, 64, width), BF16)] * 2,
-        in_specs=[SMALL],
+        in_specs=[SMALL] * (YS + 1) + [pl.BlockSpec(memory_space=pl.ANY)],
         out_specs=[SMALL] * 2,
         scratch_shapes=[pltpu.VMEM((2, 2, 8, 8, width), F32)],
         compiler_params=vmem(4),
         cost_estimate=cost(3),
         name="place_rows",
-    )(parts)
-
-    grad_queries = pl.pallas_call(
-        query_kernel,
-        out_shape=array((query_count // 4, queries.shape[1]), BF16),
-        in_specs=[SMALL] * 3,
-        out_specs=SMALL,
-        compiler_params=vmem(8),
-        name="finish_queries",
-    )(dq_near, got_core, got_far)
+    )(*parts, crossed, token)
+
     return grad_queries, grad_keys, grad_values
 
 

time: 64.5 us -> 62.4 us (0.967)
  blocking collectives: 22.5 us -> 0 us
  starting transfers between devices: 14 us -> 28.3 us
  waiting for transfers between devices: 9.54 us -> 14.1 us
  Pallas kernels: 17.5 us -> 18.8 us
    all_to_all x1 -> x0, blocking collectives: 17.1 us -> none  [on_device(): lax.all_to_all(total, 'pb', 0, 0, axis_index_groups=lines, tiled=True)]
    ppermute x0 -> x4, starting transfers between devices: none -> 12 us  [the longest x3 8.48 us: along_y(): lax.ppermute(x, 'pb', [(p, (p // (ZS * YS) * YS + (p // ZS + by) % YS) *...]
    all_gather x1 -> x0, blocking collectives: 5.43 us -> none  [on_device(): gathered = lax.all_gather(stats, 'ka')]
    ppermute x0 -> x4, waiting for transfers between devices: none -> 3.15 us  [the longest x3 1.75 us: along_y(): lax.ppermute(x, 'pb', [(p, (p // (ZS * YS) * YS + (p // ZS + by) % YS) *...]
    ppermute x2 -> x5, starting transfers between devices: 1.17 us -> 3.84 us  [across_ka(): return lax.ppermute(x, 'ka', [(a, a ^ by) for a in range(4)])]
    pallas_call x3 -> x5, Pallas kernels: 7.49 us -> 8.98 us  [the longest x1 6.03 us: row_stats(): pl.pallas_call(functools.partial(stat_kernel, width), out_shape=array((2...]
    ppermute x2 -> x5, waiting for transfers between devices: 0.01 us -> 1.34 us  [across_ka(): return lax.ppermute(x, 'ka', [(a, a ^ by) for a in range(4)])]
  transfers between devices with their start and end apart: 10 -> 17, of which waited for: 4 -> 7; matrix products, arithmetic and copies ran while one was open for 0% -> 0% of each run, Pallas kernels for 5% -> 9%
where the time goes in v5:
time: 62.4 us; the launch traced here: 62 us
  starting transfers between devices  28.3 us (45%)
  Pallas kernels  18.8 us (30%)
  waiting for transfers between devices  14.1 us (23%)
  between operations  0.74 us (1%)
    ppermute x8, starting transfers between devices, along_z(): lax.ppermute(x, 'pb', [(p, p // ZS * ZS + (p + by) % ZS) for p in range(p...  12.5 us
    ppermute x8, waiting for transfers between devices, along_z(): lax.ppermute(x, 'pb', [(p, p // ZS * ZS + (p + by) % ZS) for p in range(p...  9.6 us
    ppermute x3, starting transfers between devices, along_y(): lax.ppermute(x, 'pb', [(p, (p // (ZS * YS) * YS + (p // ZS + by) % YS) *...  8.48 us
    pallas_call x1, Pallas kernels, key_gradients(): pl.pallas_call(functools.partial(grad_kernel, width), out_shape=[array((5...  6.49 us
    pallas_call x1, Pallas kernels, row_stats(): pl.pallas_call(functools.partial(stat_kernel, width), out_shape=array((2...  6.03 us
    ppermute x5, starting transfers between devices, across_ka(): return lax.ppermute(x, 'ka', [(a, a ^ by) for a in range(4)])  3.84 us
    ppermute x1, starting transfers between devices, on_device(): lax.ppermute(crossed, 'pb', [(p, (p + pb_size // 2) % pb_size) for p in r...  3.54 us
    pallas_call x1, Pallas kernels, query_gradients(): pl.pallas_call(query_grad_kernel, out_shape=[array((width, span // 2))] *...  2.5 us
  transfers between devices with their start and end apart: 17, of which 7 were waited for; matrix products, arithmetic and copies ran while one was open for 0% of the time, Pallas kernels for 9%

profile of v5, /device:TPU:64, one launch (start us, length us, event | category | flops | bytes accessed | tf_op | source)
XLA Modules:
  0.0 62.0 jit_solution(1476675214102366840)
XLA Ops:
  0.6 6.0 %row_stats.1.refs_0_ = f32[16,512]{1,0:T(8,128)S(1)} custom-call(s32[2]{0:T(128)} %blocks.5, bf16[512,1024]{1,0:T(8,128)(2,1)} %q_hbm.3, bf16[512,1024]{1,0:T(8,128)(2,1)} %g_hbm.3, bf16[8,1024,128]{2,1,0:T(8,128)(2,1)} %k_hbm.3, bf16[8,1024,128]{2,1,0:T(8,128)(2,1)} %v_hbm.3), custom_call_target="tpu_custom_call" | custom-call | tf_op jit(solution)/shard_map/row_stats/pallas_call | solution.py:333
  6.7 0.7 %collective-permute-start.2 = (f32[16,512]{1,0:T(8,128)S(1)}, f32[16,512]{1,0:T(8,128)S(1)}, u32[]{:S(2)}, u32[]{:S(2)}) collective-permute-start(f32[16,512]{1,0:T(8,128)S(1)} %row_stats.1.refs_0_), channel_id=1, source_target_pairs={{0,1},{1,0},{2,3},{3,2},{4,5},{5,4},{6,7},{7,6},{8,9},{9,8},{10,11... | collective-permute-start | bytes 98312 | tf_op jit(solution)/shard_map/ppermute | solution.py:406
  7.4 1.2 %collective-permute-start.1 = (f32[16,512]{1,0:T(8,128)S(1)}, f32[16,512]{1,0:T(8,128)S(1)}, u32[]{:S(2)}, u32[]{:S(2)}) collective-permute-start(f32[16,512]{1,0:T(8,128)S(1)} %row_stats.1.refs_0_), channel_id=1, source_target_pairs={{0,3},{1,2},{2,1},{3,0},{4,7},{5,6},{6,5},{7,4},{8,11},{9,10},{10,... | collective-permute-start | bytes 98312 | tf_op jit(solution)/shard_map/ppermute | solution.py:406
  8.6 0.5 collective-permute-start
  9.1 2.1 %turn_inputs.1 = (bf16[128,4096]{1,0:T(8,128)(2,1)S(1)}, bf16[128,4096]{1,0:T(8,128)(2,1)S(1)}, bf16[1024,128]{1,0:T(8,128)(2,1)S(1)}, bf16[1024,128]{1,0:T(8,128)(2,1)S(1)}, bf16[128,1024]{1,0:T(8,128)(2,1)S(1)}) custom-call(bf16[512,1024]{1,0:T(8,128)(2,1)} %q_hbm.3, bf16[512,1024]{1,0:T(8,128)(2,1)} %g_hbm.3, bf16[8,1024,128]{2,1,0:T(8,128)(2,1)} %k_hbm.3, ...), custom_call_target="tpu_custom_call" | custom-call | flops 3449999872 | tf_op jit(solution)/shard_map/turn_inputs/pallas_call | solution.py:351
  11.2 0.0 collective-permute-done.1.refs_2_
  11.2 1.3 %collective-permute-done.refs_1_ = f32[16,512]{1,0:T(8,128)S(1)} collective-permute-done((f32[16,512]{1,0:T(8,128)S(1)}, f32[16,512]{1,0:T(8,128)S(1)}, u32[]{:S(2)}, u32[]{:S(2)}) %collective-permute-start) | collective-permute-done | bytes 32800 | tf_op jit(solution)/shard_map/ppermute | solution.py:406
  12.5 6.5 %key_grads.1 = (bf16[5,256,2048]{2,1,0:T(8,128)(2,1)S(1)}, f32[256,128]{1,0:T(8,128)S(1)}, f32[256,128]{1,0:T(8,128)S(1)}, f32[256,128]{1,0:T(8,128)S(1)}, f32[2...) custom-call(s32[2]{0:T(128)} %blocks.5, ...), custom_call_target="tpu_custom_call" | custom-call | tf_op jit(solution)/shard_map/key_grads/pallas_call | solution.py:369
  19.0 4.5 %collective-permute-start.8 = (f32[128,128]{1,0:T(8,128)S(1)}, f32[128,128]{1,0:T(8,128)S(1)}, u32[]{:S(2)}, u32[]{:S(2)}) collective-permute-start(f32[128,128]{1,0:T(8,128)S(1)} %get-tuple-element.46), channel_id=1, source_target_pairs={{0,8},{4,12},{8,16},{12,20},{16,24},{20,28},{24,0},{28,4},{32,40},... | collective-permute-start | bytes 196616 | tf_op jit(solution)/shard_map/ppermute | solution.py:421
  23.5 1.6 %collective-permute-start.5 = (f32[256,128]{1,0:T(8,128)S(1)}, f32[256,128]{1,0:T(8,128)S(1)}, u32[]{:S(2)}, u32[]{:S(2)}) collective-permute-start(f32[256,128]{1,0:T(8,128)S(1)} %get-tuple-element.42), channel_id=1, source_target_pairs={{0,4},{4,8},{8,12},{12,16},{16,20},{20,24},{24,28},{28,0},{32,36},... | collective-permute-start | bytes 393224 | tf_op jit(solution)/shard_map/ppermute | solution.py:421
  25.2 3.1 %collective-permute-start.7 = (f32[256,128]{1,0:T(8,128)S(1)}, f32[256,128]{1,0:T(8,128)S(1)}, u32[]{:S(2)}, u32[]{:S(2)}) collective-permute-start(f32[256,128]{1,0:T(8,128)S(1)} %get-tuple-element.45), channel_id=1, source_target_pairs={{0,4},{4,8},{8,12},{12,16},{16,20},{20,24},{24,28},{28,0},{32,36},... | collective-permute-start | bytes 393224 | tf_op jit(solution)/shard_map/ppermute | solution.py:421
  28.2 0.0 collective-permute-start.9
  28.2 2.5 %query_grads.1 = (f32[128,1024]{1,0:T(8,128)S(1)}, f32[128,1024]{1,0:T(8,128)S(1)}, f32[256,1024]{1,0:T(8,128)S(1)}) custom-call(s32[2]{0:T(128)} %blocks.5, bf16[128,1024]{1,0:T(8,128)(2,1)S(1)} %get-tuple-element.31.kt_ref, bf16[5,256,2048]{2,1,0:T(8,128)(2,1)S(1)} %get-tuple-element.36.stash), custom_call_target="tpu_custom_call" | custom-call | flops 2875000064 | tf_op jit(solution)/shard_map/query_grads/pallas_call | solution.py:385
  30.8 0.3 collective-permute-start.6
  31.0 0.1 collective-permute-start.3
  31.2 3.2 %collective-permute-done.9.got_nm = f32[256,128]{1,0:T(8,128)S(1)} collective-permute-done((f32[256,128]{1,0:T(8,128)S(1)}, f32[256,128]{1,0:T(8,128)S(1)}, u32[]{:S(2)}, u32[]{:S(2)}) %collective-permute-start.9) | collective-permute-done | bytes 131104 | tf_op jit(solution)/shard_map/ppermute | solution.py:421
  34.4 2.1 %collective-permute-start.11 = (f32[256,128]{1,0:T(8,128)S(1)}, f32[256,128]{1,0:T(8,128)S(1)}, u32[]{:S(2)}, u32[]{:S(2)}) collective-permute-start(f32[256,128]{1,0:T(8,128)S(1)} %get-tuple-element.50), channel_id=1, source_target_pairs={{0,8},{4,12},{8,16},{12,20},{16,24},{20,28},{24,0},{28,4},{32,40},... | collective-permute-start | bytes 393224 | tf_op jit(solution)/shard_map/ppermute | solution.py:421
  36.5 0.9 %collective-permute-start.12 = (f32[256,128]{1,0:T(8,128)S(1)}, f32[256,128]{1,0:T(8,128)S(1)}, u32[]{:S(2)}, u32[]{:S(2)}) collective-permute-start(f32[256,128]{1,0:T(8,128)S(1)} %get-tuple-element.51), channel_id=1, source_target_pairs={{0,24},{4,28},{8,0},{12,4},{16,8},{20,12},{24,16},{28,20},{32,56},... | collective-permute-start | bytes 393224 | tf_op jit(solution)/shard_map/ppermute | solution.py:421
  37.4 0.0 collective-permute-done.3.b_ref
  37.4 0.1 add_queries.1
  37.5 1.3 %collective-permute-start.4 = (f32[128,1024]{1,0:T(8,128)S(1)}, f32[128,1024]{1,0:T(8,128)S(1)}, u32[]{:S(2)}, u32[]{:S(2)}) collective-permute-start(f32[128,1024]{1,0:T(8,128)S(1)} %add_queries.1), channel_id=1, source_target_pairs={{0,2},{1,3},{2,0},{3,1},{4,6},{5,7},{6,4},{7,5},{8,10},{9,11},{10,... | collective-permute-start | bytes 1572872 | tf_op jit(solution)/shard_map/ppermute | solution.py:406
  38.8 2.4 %collective-permute-done.11.far_p = f32[256,128]{1,0:T(8,128)S(1)} collective-permute-done((f32[256,128]{1,0:T(8,128)S(1)}, f32[256,128]{1,0:T(8,128)S(1)}, u32[]{:S(2)}, u32[]{:S(2)}) %collective-permute-start.11) | collective-permute-done | bytes 131104 | tf_op jit(solution)/shard_map/ppermute | solution.py:421
  41.2 4.0 %collective-permute-done.12.far_m = f32[256,128]{1,0:T(8,128)S(1)} collective-permute-done((f32[256,128]{1,0:T(8,128)S(1)}, f32[256,128]{1,0:T(8,128)S(1)}, u32[]{:S(2)}, u32[]{:S(2)}) %collective-permute-start.12) | collective-permute-done | bytes 131104 | tf_op jit(solution)/shard_map/ppermute | solution.py:421
  45.2 2.8 %collective-permute-start.13 = (f32[2,32,128]{2,1,0:T(8,128)S(1)}, f32[2,32,128]{2,1,0:T(8,128)S(1)}, u32[]{:S(2)}, u32[]{:S(2)}) collective-permute-start(f32[2,32,128]{2,1,0:T(8,128)S(1)} %get-tuple-element.53), channel_id=1, source_target_pairs={{0,32},{4,36},{8,40},{12,44},{16,48},{20,52},{24,56},{28,60},{32,6... | collective-permute-start | bytes 98312 | tf_op jit(solution)/shard_map/ppermute | solution.py:416
  48.1 3.5 %collective-permute-start.14 = (f32[2,32,128]{2,1,0:T(8,128)S(1)}, f32[2,32,128]{2,1,0:T(8,128)S(1)}, u32[]{:S(2)}, u32[]{:S(2)}) collective-permute-start(f32[2,32,128]{2,1,0:T(8,128)S(1)} %get-tuple-element.54), channel_id=1, source_target_pairs={{0,64},{4,68},{8,72},{12,76},{16,80},{20,84},{24,88},{28,92},{32,9... | collective-permute-start | bytes 98312 | tf_op jit(solution)/shard_map/ppermute | solution.py:416
  51.5 2.2 %collective-permute-start.15 = (f32[2,32,128]{2,1,0:T(8,128)S(1)}, f32[2,32,128]{2,1,0:T(8,128)S(1)}, u32[]{:S(2)}, u32[]{:S(2)}) collective-permute-start(f32[2,32,128]{2,1,0:T(8,128)S(1)} %get-tuple-element.55), channel_id=1, source_target_pairs={{0,96},{4,100},{8,104},{12,108},{16,112},{20,116},{24,120},{28,124... | collective-permute-start | bytes 98312 | tf_op jit(solution)/shard_map/ppermute | solution.py:416
  53.7 0.1 collective-permute-done.14.from2
  53.8 1.7 %collective-permute-done.15.from3 = f32[2,32,128]{2,1,0:T(8,128)S(1)} collective-permute-done((f32[2,32,128]{2,1,0:T(8,128)S(1)}, f32[2,32,128]{2,1,0:T(8,128)S(1)}, u32[]{:S(2)}, u32[]{:S(2)}) %collective-permute-start.15) | collective-permute-done | bytes 32800 | tf_op jit(solution)/shard_map/ppermute | solution.py:416
  55.5 3.5 %collective-permute-start.16 = (f32[4,32,128]{2,1,0:T(8,128)S(1)}, f32[4,32,128]{2,1,0:T(8,128)S(1)}, u32[]{:S(2)}, u32[]{:S(2)}) collective-permute-start(f32[4,32,128]{2,1,0:T(8,128)S(1)} %cross_parts.1), channel_id=1, source_target_pairs={{0,128},{4,132},{8,136},{12,140},{16,144},{20,148},{24,152},{28,15... | collective-permute-start | bytes 196616 | tf_op jit(solution)/shard_map/ppermute | solution.py:470
  59.0 0.8 %finish_queries.1 = (bf16[128,1024]{1,0:T(8,128)(2,1)}, f32[8,128]{1,0:T(8,128)S(1)}) custom-call(f32[128,1024]{1,0:T(8,128)S(1)} %get-tuple-element.37.a_ref, f32[256,1024]{1,0:T(8,128)S(1)} %collective-permute-done.3.b_ref, f32[128,1024]{1,0:T(8,128)S(1)} %collective-permute-done.4.c_ref), custom_call_target="tpu_custom_call" | custom-call | tf_op jit(solution)/shard_map/finish_queries/pallas_call | solution.py:471
  59.9 1.4 %collective-permute-done.16.crossed = f32[4,32,128]{2,1,0:T(8,128)S(1)} collective-permute-done((f32[4,32,128]{2,1,0:T(8,128)S(1)}, f32[4,32,128]{2,1,0:T(8,128)S(1)}, u32[]{:S(2)}, u32[]{:S(2)}) %collective-permute-start.16) | collective-permute-done | bytes 65568 | tf_op jit(solution)/shard_map/ppermute | solution.py:470
  61.3 0.7 %place_rows.1 = (bf16[2,64,128]{2,1,0:T(8,128)(2,1)}, bf16[2,64,128]{2,1,0:T(8,128)(2,1)}) custom-call(f32[2,32,128]{2,1,0:T(8,128)S(1)} %get-tuple-element.52.own, f32[2,32,128]{2,1,0:T(8,128)S(1)} %collective-permute-done.13.from1, f32[2,32,128]{2,1,0:T(8,128)S(1)} %collective-permute-done.14.from2, f32[2,32,128]{2,1,0:T(8,128)S(1)} %collective-permute-done.15.from3, ...), custom_call_target="tpu_custom_call" | custom-call | flops 3449999872 | tf_op jit(solution)/shard_map/place_rows/pallas_call | solution.py:479
  (12 shorter events, 0.1 us)
Async XLA Ops:
  6.7 4.5 %collective-permute-start.2 = (f32[16,512]{1,0:T(8,128)S(1)}, f32[16,512]{1,0:T(8,128)S(1)}, u32[]{:S(2)}, u32[]{:S(2)}) collective-permute-start(f32[16,512]{1,0:T(8,128)S(1)} %row_stats.1.refs_0_), channel_id=1, source_target_pairs={{0,1},{1,0},{2,3},{3,2},{4,5},{5,4},{6,7},{7,6},{8,9},{9,8},{10,11... | collective-permute-start | bytes 98312 | tf_op jit(solution)/shard_map/ppermute | solution.py:406
  7.4 3.8 %collective-permute-start.1 = (f32[16,512]{1,0:T(8,128)S(1)}, f32[16,512]{1,0:T(8,128)S(1)}, u32[]{:S(2)}, u32[]{:S(2)}) collective-permute-start(f32[16,512]{1,0:T(8,128)S(1)} %row_stats.1.refs_0_), channel_id=1, source_target_pairs={{0,3},{1,2},{2,1},{3,0},{4,7},{5,6},{6,5},{7,4},{8,11},{9,10},{10,... | collective-permute-start | bytes 98312 | tf_op jit(solution)/shard_map/ppermute | solution.py:406
  8.6 3.9 %collective-permute-start = (f32[16,512]{1,0:T(8,128)S(1)}, f32[16,512]{1,0:T(8,128)S(1)}, u32[]{:S(2)}, u32[]{:S(2)}) collective-permute-start(f32[16,512]{1,0:T(8,128)S(1)} %row_stats.1.refs_0_), channel_id=1, source_target_pairs={{0,2},{1,3},{2,0},{3,1},{4,6},{5,7},{6,4},{7,5},{8,10},{9,11},{10,... | collective-permute-start | bytes 98312 | tf_op jit(solution)/shard_map/ppermute | solution.py:406
  19.0 11.7 %collective-permute-start.8 = (f32[128,128]{1,0:T(8,128)S(1)}, f32[128,128]{1,0:T(8,128)S(1)}, u32[]{:S(2)}, u32[]{:S(2)}) collective-permute-start(f32[128,128]{1,0:T(8,128)S(1)} %get-tuple-element.46), channel_id=1, source_target_pairs={{0,8},{4,12},{8,16},{12,20},{16,24},{20,28},{24,0},{28,4},{32,40},... | collective-permute-start | bytes 196616 | tf_op jit(solution)/shard_map/ppermute | solution.py:421
  23.5 7.5 %collective-permute-start.10 = (f32[128,128]{1,0:T(8,128)S(1)}, f32[128,128]{1,0:T(8,128)S(1)}, u32[]{:S(2)}, u32[]{:S(2)}) collective-permute-start(f32[128,128]{1,0:T(8,128)S(1)} %get-tuple-element.49), channel_id=1, source_target_pairs={{0,24},{4,28},{8,0},{12,4},{16,8},{20,12},{24,16},{28,20},{32,56},... | collective-permute-start | bytes 196616 | tf_op jit(solution)/shard_map/ppermute | solution.py:421
  23.5 15.2 %collective-permute-start.5 = (f32[256,128]{1,0:T(8,128)S(1)}, f32[256,128]{1,0:T(8,128)S(1)}, u32[]{:S(2)}, u32[]{:S(2)}) collective-permute-start(f32[256,128]{1,0:T(8,128)S(1)} %get-tuple-element.42), channel_id=1, source_target_pairs={{0,4},{4,8},{8,12},{12,16},{16,20},{20,24},{24,28},{28,0},{32,36},... | collective-permute-start | bytes 393224 | tf_op jit(solution)/shard_map/ppermute | solution.py:421
  25.2 6.0 %collective-permute-start.7 = (f32[256,128]{1,0:T(8,128)S(1)}, f32[256,128]{1,0:T(8,128)S(1)}, u32[]{:S(2)}, u32[]{:S(2)}) collective-permute-start(f32[256,128]{1,0:T(8,128)S(1)} %get-tuple-element.45), channel_id=1, source_target_pairs={{0,4},{4,8},{8,12},{12,16},{16,20},{20,24},{24,28},{28,0},{32,36},... | collective-permute-start | bytes 393224 | tf_op jit(solution)/shard_map/ppermute | solution.py:421
  28.2 6.1 %collective-permute-start.9 = (f32[256,128]{1,0:T(8,128)S(1)}, f32[256,128]{1,0:T(8,128)S(1)}, u32[]{:S(2)}, u32[]{:S(2)}) collective-permute-start(f32[256,128]{1,0:T(8,128)S(1)} %get-tuple-element.48), channel_id=1, source_target_pairs={{0,28},{4,0},{8,4},{12,8},{16,12},{20,16},{24,20},{28,24},{32,60},... | collective-permute-start | bytes 393224 | tf_op jit(solution)/shard_map/ppermute | solution.py:421
  30.8 8.0 %collective-permute-start.6 = (f32[256,128]{1,0:T(8,128)S(1)}, f32[256,128]{1,0:T(8,128)S(1)}, u32[]{:S(2)}, u32[]{:S(2)}) collective-permute-start(f32[256,128]{1,0:T(8,128)S(1)} %get-tuple-element.43), channel_id=1, source_target_pairs={{0,28},{4,0},{8,4},{12,8},{16,12},{20,16},{24,20},{28,24},{32,60},... | collective-permute-start | bytes 393224 | tf_op jit(solution)/shard_map/ppermute | solution.py:421
  31.0 6.3 %collective-permute-start.3 = (f32[256,1024]{1,0:T(8,128)S(1)}, f32[256,1024]{1,0:T(8,128)S(1)}, u32[]{:S(2)}, u32[]{:S(2)}) collective-permute-start(f32[256,1024]{1,0:T(8,128)S(1)} %get-tuple-element.38), channel_id=1, source_target_pairs={{0,1},{1,0},{2,3},{3,2},{4,5},{5,4},{6,7},{7,6},{8,9},{9,8},{10,11... | collective-permute-start | bytes 3145736 | tf_op jit(solution)/shard_map/ppermute | solution.py:406
  34.4 6.8 %collective-permute-start.11 = (f32[256,128]{1,0:T(8,128)S(1)}, f32[256,128]{1,0:T(8,128)S(1)}, u32[]{:S(2)}, u32[]{:S(2)}) collective-permute-start(f32[256,128]{1,0:T(8,128)S(1)} %get-tuple-element.50), channel_id=1, source_target_pairs={{0,8},{4,12},{8,16},{12,20},{16,24},{20,28},{24,0},{28,4},{32,40},... | collective-permute-start | bytes 393224 | tf_op jit(solution)/shard_map/ppermute | solution.py:421
  36.5 8.7 %collective-permute-start.12 = (f32[256,128]{1,0:T(8,128)S(1)}, f32[256,128]{1,0:T(8,128)S(1)}, u32[]{:S(2)}, u32[]{:S(2)}) collective-permute-start(f32[256,128]{1,0:T(8,128)S(1)} %get-tuple-element.51), channel_id=1, source_target_pairs={{0,24},{4,28},{8,0},{12,4},{16,8},{20,12},{24,16},{28,20},{32,56},... | collective-permute-start | bytes 393224 | tf_op jit(solution)/shard_map/ppermute | solution.py:421
  37.5 21.6 %collective-permute-start.4 = (f32[128,1024]{1,0:T(8,128)S(1)}, f32[128,1024]{1,0:T(8,128)S(1)}, u32[]{:S(2)}, u32[]{:S(2)}) collective-permute-start(f32[128,1024]{1,0:T(8,128)S(1)} %add_queries.1), channel_id=1, source_target_pairs={{0,2},{1,3},{2,0},{3,1},{4,6},{5,7},{6,4},{7,5},{8,10},{9,11},{10,... | collective-permute-start | bytes 1572872 | tf_op jit(solution)/shard_map/ppermute | solution.py:406
  45.2 8.5 %collective-permute-start.13 = (f32[2,32,128]{2,1,0:T(8,128)S(1)}, f32[2,32,128]{2,1,0:T(8,128)S(1)}, u32[]{:S(2)}, u32[]{:S(2)}) collective-permute-start(f32[2,32,128]{2,1,0:T(8,128)S(1)} %get-tuple-element.53), channel_id=1, source_target_pairs={{0,32},{4,36},{8,40},{12,44},{16,48},{20,52},{24,56},{28,60},{32,6... | collective-permute-start | bytes 98312 | tf_op jit(solution)/shard_map/ppermute | solution.py:416
  48.1 5.7 %collective-permute-start.14 = (f32[2,32,128]{2,1,0:T(8,128)S(1)}, f32[2,32,128]{2,1,0:T(8,128)S(1)}, u32[]{:S(2)}, u32[]{:S(2)}) collective-permute-start(f32[2,32,128]{2,1,0:T(8,128)S(1)} %get-tuple-element.54), channel_id=1, source_target_pairs={{0,64},{4,68},{8,72},{12,76},{16,80},{20,84},{24,88},{28,92},{32,9... | collective-permute-start | bytes 98312 | tf_op jit(solution)/shard_map/ppermute | solution.py:416
  51.5 3.9 %collective-permute-start.15 = (f32[2,32,128]{2,1,0:T(8,128)S(1)}, f32[2,32,128]{2,1,0:T(8,128)S(1)}, u32[]{:S(2)}, u32[]{:S(2)}) collective-permute-start(f32[2,32,128]{2,1,0:T(8,128)S(1)} %get-tuple-element.55), channel_id=1, source_target_pairs={{0,96},{4,100},{8,104},{12,108},{16,112},{20,116},{24,120},{28,124... | collective-permute-start | bytes 98312 | tf_op jit(solution)/shard_map/ppermute | solution.py:416
  55.5 5.8 %collective-permute-start.16 = (f32[4,32,128]{2,1,0:T(8,128)S(1)}, f32[4,32,128]{2,1,0:T(8,128)S(1)}, u32[]{:S(2)}, u32[]{:S(2)}) collective-permute-start(f32[4,32,128]{2,1,0:T(8,128)S(1)} %cross_parts.1), channel_id=1, source_target_pairs={{0,128},{4,132},{8,136},{12,140},{16,144},{20,148},{24,152},{28,15... | collective-permute-start | bytes 196616 | tf_op jit(solution)/shard_map/ppermute | solution.py:470

commit v6 on v5

--- a/solution.py
+++ b/solution.py
@@ -159,7 +159,7 @@
 
 def grad_body(
     width, blocks, qt_ref, gt_ref, k_ref, v_ref, stats,
-    stash, own, near_p, near_m, next_p, next_m, far_p, far_m, half_p, half_m,
+    stash, own, near_p, near_m, next_p, next_m, far_p, far_m, across,
     lse_scr, delta_scr, dk_scr, dv_scr, dk_rows, dv_rows,
 ):
     scale = width**-0.5
@@ -232,11 +232,14 @@
     put(next_m, 0, 7, every)
     put(far_p, 0, 2, every)
     put(far_m, 0, 6, every)
-    put(half_p, 0, 4, range(4))
-    put(half_m, 0, 4, range(4, 8))
-
-
-def query_grad_kernel(blocks, kt_ref, stash, dq_near, dq_far, dq_core, dq_scr):
+    put(across, 0, 4, every)
+
+
+def query_grad_kernel(
+    blocks, kt_ref, stash, next_p, next_m, dq_near, dq_far, dq_core, out_p, out_m, dq_scr
+):
+    out_p[...] = next_p[...]
+    out_m[...] = next_m[...]
     dq_scr[...] = jnp.zeros(dq_scr.shape, F32)
     span = stash.shape[2]
 
@@ -258,12 +261,18 @@
             out[at : at + kt_ref.shape[0], h * half : (h + 1) * half] = dq_scr[:, pl.ds(start, half)]
 
 
-def merge_kernel(far_p, got_np, got_hp, far_m, got_nm, got_hm, out_p, out_m):
-    half = got_hp.shape[0]
-    out_p[:half] = far_p[:half] + got_np[:half] + got_hp[...]
-    out_p[half:] = far_p[half:] + got_np[half:]
-    out_m[:half] = far_m[:half] + got_nm[:half]
-    out_m[half:] = far_m[half:] + got_nm[half:] + got_hm[...]
+def merge_kernel(far_p, got_np, far_m, got_nm, got_across, out_p, out_m):
+    upward = lax.axis_index("ka") % 2 == 0
+    out_p[...] = far_p[...] + got_np[...]
+    out_m[...] = far_m[...] + got_nm[...]
+
+    @pl.when(upward)
+    def _():
+        out_p[...] += got_across[...]
+
+    @pl.when(jnp.logical_not(upward))
+    def _():
+        out_m[...] += got_across[...]
 
 
 def sum_kernel(own, next_p, next_m, far_p, far_m, *outs):
@@ -365,12 +374,12 @@
     heads = stats[0].shape[0] // 2
     query_count = stats[0].shape[1]
     chunk = (256, width)
-    shapes = [chunk] * 7 + [(128, width)] * 2
+    shapes = [chunk] * 8
     return pl.pallas_call(
         functools.partial(grad_kernel, width),
         out_shape=[array((5, TILE, heads * TILE), BF16)] + [array(s) for s in shapes],
         in_specs=[SCALARS] + [SMALL] * 8,
-        out_specs=[SMALL] * 10,
+        out_specs=[SMALL] * 9,
         scratch_shapes=[pltpu.VMEM((heads, query_count), F32)] * 2
         + [pltpu.VMEM((width, key_count), F32)] * 2
         + [pltpu.VMEM((key_count, width), F32)] * 2,
@@ -379,19 +388,19 @@
     )(blocks, turned_q, turned_g, keys, values, *stats)
 
 
-def query_gradients(blocks, turned_k, stash):
+def query_gradients(blocks, turned_k, stash, next_p, next_m):
     width = turned_k.shape[0]
     span = stash.shape[2]
     return pl.pallas_call(
         query_grad_kernel,
-        out_shape=[array((width, span // 2))] * 2 + [array((2 * width, span // 2))],
-        in_specs=[SCALARS] + [SMALL] * 2,
-        out_specs=[SMALL] * 3,
+        out_shape=[array((width, span // 2))] * 2 + [array((2 * width, span // 2))] + [array(next_p.shape)] * 2,
+        in_specs=[SCALARS] + [SMALL] * 4,
+        out_specs=[SMALL] * 5,
         scratch_shapes=[pltpu.VMEM((width, 2 * span), F32)],
         compiler_params=vmem(16),
         cost_estimate=cost(2.5),
         name="query_grads",
-    )(blocks, turned_k, stash)
+    )(blocks, turned_k, stash, next_p, next_m)
 
 
 def on_device(queries, keys, values, grad_out, query_blocks):
@@ -408,7 +417,7 @@
     own_stats = row_stats(blocks, queries, grad_out, keys, values)
     stats = [own_stats] + [across_ka(own_stats, by) for by in (2, 3, 1)]
     turned_q, turned_g, own_k, own_v, turned_k = turned_inputs(queries, grad_out, keys, values)
-    stash, own, near_p, near_m, next_p, next_m, far_p, far_m, half_p, half_m = key_gradients(
+    stash, own, near_p, near_m, next_p, next_m, far_p, far_m, across = key_gradients(
         blocks, turned_q, turned_g, own_k, own_v, stats
     )
 
@@ -420,12 +429,16 @@
     def along_z(x, by):
         return lax.ppermute(x, "pb", [(p, p // ZS * ZS + (p + by) % ZS) for p in range(pb_size)])
 
+    pairs = []
+    for p in range(pb_size):
+        for a in range(4):
+            there = p // ZS * ZS + (p + (2 if a % 2 == 0 else ZS - 2)) % ZS
+            pairs.append((p * 4 + a, there * 4 + a))
+    got_across = lax.ppermute(across, ("pb", "ka"), pairs)
     got_np = along_z(near_p, 1)
     got_nm = along_z(near_m, ZS - 1)
-    got_hp = along_z(half_p, 2)
-    got_hm = along_z(half_m, ZS - 2)
-
-    dq_near, dq_far, dq_core = query_gradients(blocks, turned_k, stash)
+
+    dq_near, dq_far, dq_core, next_p, next_m = query_gradients(blocks, turned_k, stash, next_p, next_m)
     next_p = along_z(next_p, 1)
     next_m = along_z(next_m, ZS - 1)
     got_core = across_ka(dq_core, 1)
@@ -441,12 +454,12 @@
     far_p, far_m = pl.pallas_call(
         merge_kernel,
         out_shape=[array(far_p.shape), array(far_m.shape)],
-        in_specs=[SMALL] * 6,
+        in_specs=[SMALL] * 5,
         out_specs=[SMALL] * 2,
         compiler_params=vmem(8),
         cost_estimate=cost(10),
         name="merge",
-    )(far_p, got_np, got_hp, far_m, got_nm, got_hm)
+    )(far_p, got_np, far_m, got_nm, got_across)
     got_fp = along_z(far_p, 2)
     got_fm = along_z(far_m, ZS - 2)
     parts = pl.pallas_call(

time: 62.4 us -> 59.8 us (0.958)
  the two profiles are of different devices: /device:TPU:64 before, /device:TPU:24 now
where the time goes in v6:
time: 59.8 us; the launch traced here: 59.5 us
  starting transfers between devices  21.5 us (36%)
  Pallas kernels  21.3 us (36%)
  waiting for transfers between devices  16.1 us (27%)
  between operations  0.72 us (1%)
    ppermute x6, starting transfers between devices, along_z(): lax.ppermute(x, 'pb', [(p, p // ZS * ZS + (p + by) % ZS) for p in range(p...  12.4 us
    pallas_call x1, Pallas kernels, key_gradients(): pl.pallas_call(functools.partial(grad_kernel, width), out_shape=[array((5...  7.82 us
    pallas_call x1, Pallas kernels, row_stats(): pl.pallas_call(functools.partial(stat_kernel, width), out_shape=array((2...  6.8 us
    ppermute x3, waiting for transfers between devices, along_y(): lax.ppermute(x, 'pb', [(p, (p // (ZS * YS) * YS + (p // ZS + by) % YS) *...  5.12 us
    ppermute x6, waiting for transfers between devices, along_z(): lax.ppermute(x, 'pb', [(p, p // ZS * ZS + (p + by) % ZS) for p in range(p...  4.66 us
    ppermute x3, starting transfers between devices, along_y(): lax.ppermute(x, 'pb', [(p, (p // (ZS * YS) * YS + (p // ZS + by) % YS) *...  3.8 us
    ppermute x5, starting transfers between devices, across_ka(): return lax.ppermute(x, 'ka', [(a, a ^ by) for a in range(4)])  3.34 us
    ppermute x1, waiting for transfers between devices, on_device(): lax.ppermute(crossed, 'pb', [(p, (p + pb_size // 2) % pb_size) for p in r...  3.02 us
  transfers between devices with their start and end apart: 16, of which 8 were waited for; matrix products, arithmetic and copies ran while one was open for 0% of the time, Pallas kernels for 10%

profile of v6, /device:TPU:24, one launch (start us, length us, event | category | flops | bytes accessed | tf_op | source)
XLA Modules:
  0.0 59.5 jit_solution(9328751627557187335)
XLA Ops:
  0.6 6.8 %row_stats.1.refs_0_ = f32[16,512]{1,0:T(8,128)S(1)} custom-call(s32[2]{0:T(128)} %blocks.5, bf16[512,1024]{1,0:T(8,128)(2,1)} %q_hbm.3, bf16[512,1024]{1,0:T(8,128)(2,1)} %g_hbm.3, bf16[8,1024,128]{2,1,0:T(8,128)(2,1)} %k_hbm.3, bf16[8,1024,128]{2,1,0:T(8,128)(2,1)} %v_hbm.3), custom_call_target="tpu_custom_call" | custom-call | tf_op jit(solution)/shard_map/row_stats/pallas_call | solution.py:342
  7.4 0.1 collective-permute-start.2
  7.5 0.8 %collective-permute-start.1 = (f32[16,512]{1,0:T(8,128)S(1)}, f32[16,512]{1,0:T(8,128)S(1)}, u32[]{:S(2)}, u32[]{:S(2)}) collective-permute-start(f32[16,512]{1,0:T(8,128)S(1)} %row_stats.1.refs_0_), channel_id=1, source_target_pairs={{0,3},{1,2},{2,1},{3,0},{4,7},{5,6},{6,5},{7,4},{8,11},{9,10},{10,... | collective-permute-start | bytes 98312 | tf_op jit(solution)/shard_map/ppermute | solution.py:415
  8.4 1.3 %collective-permute-start = (f32[16,512]{1,0:T(8,128)S(1)}, f32[16,512]{1,0:T(8,128)S(1)}, u32[]{:S(2)}, u32[]{:S(2)}) collective-permute-start(f32[16,512]{1,0:T(8,128)S(1)} %row_stats.1.refs_0_), channel_id=1, source_target_pairs={{0,2},{1,3},{2,0},{3,1},{4,6},{5,7},{6,4},{7,5},{8,10},{9,11},{10,... | collective-permute-start | bytes 98312 | tf_op jit(solution)/shard_map/ppermute | solution.py:415
  9.7 2.1 %turn_inputs.1 = (bf16[128,4096]{1,0:T(8,128)(2,1)S(1)}, bf16[128,4096]{1,0:T(8,128)(2,1)S(1)}, bf16[1024,128]{1,0:T(8,128)(2,1)S(1)}, bf16[1024,128]{1,0:T(8,128)(2,1)S(1)}, bf16[128,1024]{1,0:T(8,128)(2,1)S(1)}) custom-call(bf16[512,1024]{1,0:T(8,128)(2,1)} %q_hbm.3, bf16[512,1024]{1,0:T(8,128)(2,1)} %g_hbm.3, bf16[8,1024,128]{2,1,0:T(8,128)(2,1)} %k_hbm.3, ...), custom_call_target="tpu_custom_call" | custom-call | flops 3449999872 | tf_op jit(solution)/shard_map/turn_inputs/pallas_call | solution.py:360
  11.8 0.0 collective-permute-done.2.refs_3_
  11.8 0.0 collective-permute-done.1.refs_2_
  11.8 0.5 collective-permute-done.refs_1_
  12.3 7.8 %key_grads.1 = (bf16[5,256,2048]{2,1,0:T(8,128)(2,1)S(1)}, f32[256,128]{1,0:T(8,128)S(1)}, f32[256,128]{1,0:T(8,128)S(1)}, f32[256,128]{1,0:T(8,128)S(1)}, f32[2...) custom-call(s32[2]{0:T(128)} %blocks.5, ...), custom_call_target="tpu_custom_call" | custom-call | tf_op jit(solution)/shard_map/key_grads/pallas_call | solution.py:378
  20.1 0.9 %collective-permute-start.7 = (f32[256,128]{1,0:T(8,128)S(1)}, f32[256,128]{1,0:T(8,128)S(1)}, u32[]{:S(2)}, u32[]{:S(2)}) collective-permute-start(f32[256,128]{1,0:T(8,128)S(1)} %get-tuple-element.48), channel_id=1, source_target_pairs={{0,4},{4,8},{8,12},{12,16},{16,20},{20,24},{24,28},{28,0},{32,36},... | collective-permute-start | bytes 393224 | tf_op jit(solution)/shard_map/ppermute | solution.py:430
  21.0 4.0 %collective-permute-start.8 = (f32[256,128]{1,0:T(8,128)S(1)}, f32[256,128]{1,0:T(8,128)S(1)}, u32[]{:S(2)}, u32[]{:S(2)}) collective-permute-start(f32[256,128]{1,0:T(8,128)S(1)} %get-tuple-element.50), channel_id=1, source_target_pairs={{0,28},{4,0},{8,4},{12,8},{16,12},{20,16},{24,20},{28,24},{32,60},... | collective-permute-start | bytes 393224 | tf_op jit(solution)/shard_map/ppermute | solution.py:430
  25.0 0.0 collective-permute-start.9
  25.0 2.8 %query_grads.1 = (f32[128,1024]{1,0:T(8,128)S(1)}, f32[128,1024]{1,0:T(8,128)S(1)}, f32[256,1024]{1,0:T(8,128)S(1)}, f32[256,128]{1,0:T(8,128)S(1)}, f32[256,128]{1,0:T(8,128)S(1)}) custom-call(s32[2]{0:T(128)} %blocks.5, bf16[128,1024]{1,0:T(8,128)(2,1)S(1)} %get-tuple-element.32.kt_ref, bf16[5,256,2048]{2,1,0:T(8,128)(2,1)S(1)} %get-tuple-element.37.stash, ...), custom_call_target="tpu_custom_call" | custom-call | flops 2875000064 | tf_op jit(solution)/shard_map/query_grads/pallas_call | solution.py:394
  27.8 2.2 %collective-permute-start.5 = (f32[256,128]{1,0:T(8,128)S(1)}, f32[256,128]{1,0:T(8,128)S(1)}, u32[]{:S(2)}, u32[]{:S(2)}) collective-permute-start(f32[256,128]{1,0:T(8,128)S(1)} %get-tuple-element.45), channel_id=1, source_target_pairs={{0,4},{4,8},{8,12},{12,16},{16,20},{20,24},{24,28},{28,0},{32,36},... | collective-permute-start | bytes 393224 | tf_op jit(solution)/shard_map/ppermute | solution.py:430
  30.0 1.1 %collective-permute-start.6 = (f32[256,128]{1,0:T(8,128)S(1)}, f32[256,128]{1,0:T(8,128)S(1)}, u32[]{:S(2)}, u32[]{:S(2)}) collective-permute-start(f32[256,128]{1,0:T(8,128)S(1)} %get-tuple-element.46), channel_id=1, source_target_pairs={{0,28},{4,0},{8,4},{12,8},{16,12},{20,16},{24,20},{28,24},{32,60},... | collective-permute-start | bytes 393224 | tf_op jit(solution)/shard_map/ppermute | solution.py:430
  31.1 0.0 collective-permute-start.3
  31.2 2.7 %collective-permute-done.9.got_across = f32[256,128]{1,0:T(8,128)S(1)} collective-permute-done((f32[256,128]{1,0:T(8,128)S(1)}, f32[256,128]{1,0:T(8,128)S(1)}, u32[]{:S(2)}, u32[]{:S(2)}) %collective-permute-start.9) | collective-permute-done | bytes 131104 | tf_op jit(solution)/shard_map/ppermute | solution.py:437
  33.9 0.9 %collective-permute-start.10 = (f32[256,128]{1,0:T(8,128)S(1)}, f32[256,128]{1,0:T(8,128)S(1)}, u32[]{:S(2)}, u32[]{:S(2)}) collective-permute-start(f32[256,128]{1,0:T(8,128)S(1)} %get-tuple-element.52), channel_id=1, source_target_pairs={{0,8},{4,12},{8,16},{12,20},{16,24},{20,28},{24,0},{28,4},{32,40},... | collective-permute-start | bytes 393224 | tf_op jit(solution)/shard_map/ppermute | solution.py:430
  34.9 3.3 %collective-permute-start.11 = (f32[256,128]{1,0:T(8,128)S(1)}, f32[256,128]{1,0:T(8,128)S(1)}, u32[]{:S(2)}, u32[]{:S(2)}) collective-permute-start(f32[256,128]{1,0:T(8,128)S(1)} %get-tuple-element.53), channel_id=1, source_target_pairs={{0,24},{4,28},{8,0},{12,4},{16,8},{20,12},{24,16},{28,20},{32,56},... | collective-permute-start | bytes 393224 | tf_op jit(solution)/shard_map/ppermute | solution.py:430
  38.2 0.1 add_queries.1
  38.2 1.1 %collective-permute-start.4 = (f32[128,1024]{1,0:T(8,128)S(1)}, f32[128,1024]{1,0:T(8,128)S(1)}, u32[]{:S(2)}, u32[]{:S(2)}) collective-permute-start(f32[128,1024]{1,0:T(8,128)S(1)} %add_queries.1), channel_id=1, source_target_pairs={{0,2},{1,3},{2,0},{3,1},{4,6},{5,7},{6,4},{7,5},{8,10},{9,11},{10,... | collective-permute-start | bytes 1572872 | tf_op jit(solution)/shard_map/ppermute | solution.py:415
  39.3 3.1 %collective-permute-done.10.far_p = f32[256,128]{1,0:T(8,128)S(1)} collective-permute-done((f32[256,128]{1,0:T(8,128)S(1)}, f32[256,128]{1,0:T(8,128)S(1)}, u32[]{:S(2)}, u32[]{:S(2)}) %collective-permute-start.10) | collective-permute-done | bytes 131104 | tf_op jit(solution)/shard_map/ppermute | solution.py:430
  42.5 1.5 %collective-permute-done.11.far_m = f32[256,128]{1,0:T(8,128)S(1)} collective-permute-done((f32[256,128]{1,0:T(8,128)S(1)}, f32[256,128]{1,0:T(8,128)S(1)}, u32[]{:S(2)}, u32[]{:S(2)}) %collective-permute-start.11) | collective-permute-done | bytes 131104 | tf_op jit(solution)/shard_map/ppermute | solution.py:430
  44.0 0.3 collective-permute-start.12
  44.4 3.5 %collective-permute-start.13 = (f32[2,32,128]{2,1,0:T(8,128)S(1)}, f32[2,32,128]{2,1,0:T(8,128)S(1)}, u32[]{:S(2)}, u32[]{:S(2)}) collective-permute-start(f32[2,32,128]{2,1,0:T(8,128)S(1)} %get-tuple-element.56), channel_id=1, source_target_pairs={{0,64},{4,68},{8,72},{12,76},{16,80},{20,84},{24,88},{28,92},{32,9... | collective-permute-start | bytes 98312 | tf_op jit(solution)/shard_map/ppermute | solution.py:425
  47.8 0.2 collective-permute-done.12.from1
  48.0 1.8 %collective-permute-done.13.from2 = f32[2,32,128]{2,1,0:T(8,128)S(1)} collective-permute-done((f32[2,32,128]{2,1,0:T(8,128)S(1)}, f32[2,32,128]{2,1,0:T(8,128)S(1)}, u32[]{:S(2)}, u32[]{:S(2)}) %collective-permute-start.13) | collective-permute-done | bytes 32800 | tf_op jit(solution)/shard_map/ppermute | solution.py:425
  49.8 3.2 %collective-permute-done.14.from3 = f32[2,32,128]{2,1,0:T(8,128)S(1)} collective-permute-done((f32[2,32,128]{2,1,0:T(8,128)S(1)}, f32[2,32,128]{2,1,0:T(8,128)S(1)}, u32[]{:S(2)}, u32[]{:S(2)}) %collective-permute-start.14) | collective-permute-done | bytes 32800 | tf_op jit(solution)/shard_map/ppermute | solution.py:425
  53.0 1.9 %collective-permute-start.15 = (f32[4,32,128]{2,1,0:T(8,128)S(1)}, f32[4,32,128]{2,1,0:T(8,128)S(1)}, u32[]{:S(2)}, u32[]{:S(2)}) collective-permute-start(f32[4,32,128]{2,1,0:T(8,128)S(1)} %cross_parts.1), channel_id=1, source_target_pairs={{0,128},{4,132},{8,136},{12,140},{16,144},{20,148},{24,152},{28,15... | collective-permute-start | bytes 196616 | tf_op jit(solution)/shard_map/ppermute | solution.py:483
  54.9 0.8 %finish_queries.1 = (bf16[128,1024]{1,0:T(8,128)(2,1)}, f32[8,128]{1,0:T(8,128)S(1)}) custom-call(f32[128,1024]{1,0:T(8,128)S(1)} %get-tuple-element.40.a_ref, f32[256,1024]{1,0:T(8,128)S(1)} %collective-permute-done.3.b_ref, f32[128,1024]{1,0:T(8,128)S(1)} %collective-permute-done.4.c_ref), custom_call_target="tpu_custom_call" | custom-call | tf_op jit(solution)/shard_map/finish_queries/pallas_call | solution.py:484
  55.7 3.0 %collective-permute-done.15.crossed = f32[4,32,128]{2,1,0:T(8,128)S(1)} collective-permute-done((f32[4,32,128]{2,1,0:T(8,128)S(1)}, f32[4,32,128]{2,1,0:T(8,128)S(1)}, u32[]{:S(2)}, u32[]{:S(2)}) %collective-permute-start.15) | collective-permute-done | bytes 65568 | tf_op jit(solution)/shard_map/ppermute | solution.py:483
  58.7 0.7 %place_rows.1 = (bf16[2,64,128]{2,1,0:T(8,128)(2,1)}, bf16[2,64,128]{2,1,0:T(8,128)(2,1)}) custom-call(f32[2,32,128]{2,1,0:T(8,128)S(1)} %get-tuple-element.54.own, f32[2,32,128]{2,1,0:T(8,128)S(1)} %collective-permute-done.12.from1, f32[2,32,128]{2,1,0:T(8,128)S(1)} %collective-permute-done.13.from2, f32[2,32,128]{2,1,0:T(8,128)S(1)} %collective-permute-done.14.from3, ...), custom_call_target="tpu_custom_call" | custom-call | flops 3449999872 | tf_op jit(solution)/shard_map/place_rows/pallas_call | solution.py:492
  (10 shorter events, 0.1 us)
Async XLA Ops:
  7.4 4.3 %collective-permute-start.2 = (f32[16,512]{1,0:T(8,128)S(1)}, f32[16,512]{1,0:T(8,128)S(1)}, u32[]{:S(2)}, u32[]{:S(2)}) collective-permute-start(f32[16,512]{1,0:T(8,128)S(1)} %row_stats.1.refs_0_), channel_id=1, source_target_pairs={{0,1},{1,0},{2,3},{3,2},{4,5},{5,4},{6,7},{7,6},{8,9},{9,8},{10,11... | collective-permute-start | bytes 98312 | tf_op jit(solution)/shard_map/ppermute | solution.py:415
  7.5 4.2 %collective-permute-start.1 = (f32[16,512]{1,0:T(8,128)S(1)}, f32[16,512]{1,0:T(8,128)S(1)}, u32[]{:S(2)}, u32[]{:S(2)}) collective-permute-start(f32[16,512]{1,0:T(8,128)S(1)} %row_stats.1.refs_0_), channel_id=1, source_target_pairs={{0,3},{1,2},{2,1},{3,0},{4,7},{5,6},{6,5},{7,4},{8,11},{9,10},{10,... | collective-permute-start | bytes 98312 | tf_op jit(solution)/shard_map/ppermute | solution.py:415
  8.4 3.9 %collective-permute-start = (f32[16,512]{1,0:T(8,128)S(1)}, f32[16,512]{1,0:T(8,128)S(1)}, u32[]{:S(2)}, u32[]{:S(2)}) collective-permute-start(f32[16,512]{1,0:T(8,128)S(1)} %row_stats.1.refs_0_), channel_id=1, source_target_pairs={{0,2},{1,3},{2,0},{3,1},{4,6},{5,7},{6,4},{7,5},{8,10},{9,11},{10,... | collective-permute-start | bytes 98312 | tf_op jit(solution)/shard_map/ppermute | solution.py:415
  20.1 11.0 %collective-permute-start.7 = (f32[256,128]{1,0:T(8,128)S(1)}, f32[256,128]{1,0:T(8,128)S(1)}, u32[]{:S(2)}, u32[]{:S(2)}) collective-permute-start(f32[256,128]{1,0:T(8,128)S(1)} %get-tuple-element.48), channel_id=1, source_target_pairs={{0,4},{4,8},{8,12},{12,16},{16,20},{20,24},{24,28},{28,0},{32,36},... | collective-permute-start | bytes 393224 | tf_op jit(solution)/shard_map/ppermute | solution.py:430
  21.0 10.2 %collective-permute-start.8 = (f32[256,128]{1,0:T(8,128)S(1)}, f32[256,128]{1,0:T(8,128)S(1)}, u32[]{:S(2)}, u32[]{:S(2)}) collective-permute-start(f32[256,128]{1,0:T(8,128)S(1)} %get-tuple-element.50), channel_id=1, source_target_pairs={{0,28},{4,0},{8,4},{12,8},{16,12},{20,16},{24,20},{28,24},{32,60},... | collective-permute-start | bytes 393224 | tf_op jit(solution)/shard_map/ppermute | solution.py:430
  25.0 8.9 %collective-permute-start.9 = (f32[256,128]{1,0:T(8,128)S(1)}, f32[256,128]{1,0:T(8,128)S(1)}, u32[]{:S(2)}, u32[]{:S(2)}) collective-permute-start(f32[256,128]{1,0:T(8,128)S(1)} %get-tuple-element.51), channel_id=1, source_target_pairs={{0,8},{1,25},{2,10},{3,27},{4,12},{5,29},{6,14},{7,31},{8,16},{9,1... | collective-permute-start | bytes 393224 | tf_op jit(solution)/shard_map/ppermute | solution.py:437
  27.8 11.5 %collective-permute-start.5 = (f32[256,128]{1,0:T(8,128)S(1)}, f32[256,128]{1,0:T(8,128)S(1)}, u32[]{:S(2)}, u32[]{:S(2)}) collective-permute-start(f32[256,128]{1,0:T(8,128)S(1)} %get-tuple-element.45), channel_id=1, source_target_pairs={{0,4},{4,8},{8,12},{12,16},{16,20},{20,24},{24,28},{28,0},{32,36},... | collective-permute-start | bytes 393224 | tf_op jit(solution)/shard_map/ppermute | solution.py:430
  30.0 9.3 %collective-permute-start.6 = (f32[256,128]{1,0:T(8,128)S(1)}, f32[256,128]{1,0:T(8,128)S(1)}, u32[]{:S(2)}, u32[]{:S(2)}) collective-permute-start(f32[256,128]{1,0:T(8,128)S(1)} %get-tuple-element.46), channel_id=1, source_target_pairs={{0,28},{4,0},{8,4},{12,8},{16,12},{20,16},{24,20},{28,24},{32,60},... | collective-permute-start | bytes 393224 | tf_op jit(solution)/shard_map/ppermute | solution.py:430
  31.1 7.0 %collective-permute-start.3 = (f32[256,1024]{1,0:T(8,128)S(1)}, f32[256,1024]{1,0:T(8,128)S(1)}, u32[]{:S(2)}, u32[]{:S(2)}) collective-permute-start(f32[256,1024]{1,0:T(8,128)S(1)} %get-tuple-element.41), channel_id=1, source_target_pairs={{0,1},{1,0},{2,3},{3,2},{4,5},{5,4},{6,7},{7,6},{8,9},{9,8},{10,11... | collective-permute-start | bytes 3145736 | tf_op jit(solution)/shard_map/ppermute | solution.py:415
  33.9 8.5 %collective-permute-start.10 = (f32[256,128]{1,0:T(8,128)S(1)}, f32[256,128]{1,0:T(8,128)S(1)}, u32[]{:S(2)}, u32[]{:S(2)}) collective-permute-start(f32[256,128]{1,0:T(8,128)S(1)} %get-tuple-element.52), channel_id=1, source_target_pairs={{0,8},{4,12},{8,16},{12,20},{16,24},{20,28},{24,0},{28,4},{32,40},... | collective-permute-start | bytes 393224 | tf_op jit(solution)/shard_map/ppermute | solution.py:430
  34.9 9.1 %collective-permute-start.11 = (f32[256,128]{1,0:T(8,128)S(1)}, f32[256,128]{1,0:T(8,128)S(1)}, u32[]{:S(2)}, u32[]{:S(2)}) collective-permute-start(f32[256,128]{1,0:T(8,128)S(1)} %get-tuple-element.53), channel_id=1, source_target_pairs={{0,24},{4,28},{8,0},{12,4},{16,8},{20,12},{24,16},{28,20},{32,56},... | collective-permute-start | bytes 393224 | tf_op jit(solution)/shard_map/ppermute | solution.py:430
  38.2 16.6 %collective-permute-start.4 = (f32[128,1024]{1,0:T(8,128)S(1)}, f32[128,1024]{1,0:T(8,128)S(1)}, u32[]{:S(2)}, u32[]{:S(2)}) collective-permute-start(f32[128,1024]{1,0:T(8,128)S(1)} %add_queries.1), channel_id=1, source_target_pairs={{0,2},{1,3},{2,0},{3,1},{4,6},{5,7},{6,4},{7,5},{8,10},{9,11},{10,... | collective-permute-start | bytes 1572872 | tf_op jit(solution)/shard_map/ppermute | solution.py:415
  44.0 4.0 %collective-permute-start.12 = (f32[2,32,128]{2,1,0:T(8,128)S(1)}, f32[2,32,128]{2,1,0:T(8,128)S(1)}, u32[]{:S(2)}, u32[]{:S(2)}) collective-permute-start(f32[2,32,128]{2,1,0:T(8,128)S(1)} %get-tuple-element.55), channel_id=1, source_target_pairs={{0,32},{4,36},{8,40},{12,44},{16,48},{20,52},{24,56},{28,60},{32,6... | collective-permute-start | bytes 98312 | tf_op jit(solution)/shard_map/ppermute | solution.py:425
  44.4 5.4 %collective-permute-start.13 = (f32[2,32,128]{2,1,0:T(8,128)S(1)}, f32[2,32,128]{2,1,0:T(8,128)S(1)}, u32[]{:S(2)}, u32[]{:S(2)}) collective-permute-start(f32[2,32,128]{2,1,0:T(8,128)S(1)} %get-tuple-element.56), channel_id=1, source_target_pairs={{0,64},{4,68},{8,72},{12,76},{16,80},{20,84},{24,88},{28,92},{32,9... | collective-permute-start | bytes 98312 | tf_op jit(solution)/shard_map/ppermute | solution.py:425
  47.8 5.1 %collective-permute-start.14 = (f32[2,32,128]{2,1,0:T(8,128)S(1)}, f32[2,32,128]{2,1,0:T(8,128)S(1)}, u32[]{:S(2)}, u32[]{:S(2)}) collective-permute-start(f32[2,32,128]{2,1,0:T(8,128)S(1)} %get-tuple-element.57), channel_id=1, source_target_pairs={{0,96},{4,100},{8,104},{12,108},{16,112},{20,116},{24,120},{28,124... | collective-permute-start | bytes 98312 | tf_op jit(solution)/shard_map/ppermute | solution.py:425
  53.0 5.8 %collective-permute-start.15 = (f32[4,32,128]{2,1,0:T(8,128)S(1)}, f32[4,32,128]{2,1,0:T(8,128)S(1)}, u32[]{:S(2)}, u32[]{:S(2)}) collective-permute-start(f32[4,32,128]{2,1,0:T(8,128)S(1)} %cross_parts.1), channel_id=1, source_target_pairs={{0,128},{4,132},{8,136},{12,140},{16,144},{20,148},{24,152},{28,15... | collective-permute-start | bytes 196616 | tf_op jit(solution)/shard_map/ppermute | solution.py:483

commit v7 on v6

--- a/solution.py
+++ b/solution.py
@@ -130,20 +130,11 @@
             out_ref[heads + h : heads + h + 1, cols] = jnp.where(total > 0, dotted / total, 0.0)
 
 
-def turn_kernel(
-    q_hbm, g_hbm, k_hbm, v_hbm, qt_ref, gt_ref, k_ref, v_ref, kt_ref, q_ref, g_ref, sems
-):
-    copies = copies_in(q_hbm, g_hbm, k_hbm, v_hbm, q_ref, g_ref, k_ref, v_ref, sems)
+def turn_kernel(q_ref, g_ref, k_ref, qt_ref, gt_ref, kt_ref):
     width = k_ref.shape[1]
     heads = q_ref.shape[1] // width
-    for copy in copies:
-        copy.start()
-    for copy in copies[:2]:
-        copy.wait()
     kt_ref[...] = k_ref[...].T
     for slot in range(2):
-        for copy in copies[2 + 2 * slot : 4 + 2 * slot]:
-            copy.wait()
         for h in range(heads):
             cols = slice(h * width, (h + 1) * width)
             at = (slot * heads + h) * TILE
@@ -339,34 +330,31 @@
     _, key_count, width = keys.shape
     query_count = queries.shape[0]
     heads = queries.shape[1] // width
+    own = array((key_count, width), BF16)
+    rows = array(queries.shape, BF16)
     return pl.pallas_call(
         functools.partial(stat_kernel, width),
-        out_shape=array((2 * heads, query_count)),
+        out_shape=[array((2 * heads, query_count)), rows, rows, own, own],
         in_specs=[SCALARS] + [LARGE] * 4,
-        out_specs=SMALL,
-        scratch_shapes=[pltpu.VMEM(queries.shape, BF16)] * 2
-        + [pltpu.VMEM((key_count, width), BF16)] * 2
-        + [pltpu.VMEM((heads, 2, 8, TILE), F32)] * 3
-        + [pltpu.SemaphoreType.DMA((6,))],
+        out_specs=[SMALL] * 5,
+        scratch_shapes=[pltpu.VMEM((heads, 2, 8, TILE), F32)] * 3 + [pltpu.SemaphoreType.DMA((6,))],
         compiler_params=vmem(24),
         name="row_stats",
     )(blocks, queries, grad_out, keys, values)
 
 
-def turned_inputs(queries, grad_out, keys, values):
-    _, key_count, width = keys.shape
+def turned_inputs(queries, grad_out, keys):
+    key_count, width = keys.shape
     turned = array((width, queries.size // width), BF16)
-    own = array((key_count, width), BF16)
     return pl.pallas_call(
         turn_kernel,
-        out_shape=[turned, turned, own, own, array((width, key_count), BF16)],
-        in_specs=[LARGE] * 4,
-        out_specs=[SMALL] * 5,
-        scratch_shapes=[pltpu.VMEM(queries.shape, BF16)] * 2 + [pltpu.SemaphoreType.DMA((6,))],
+        out_shape=[turned, turned, array((width, key_count), BF16)],
+        in_specs=[SMALL] * 3,
+        out_specs=[SMALL] * 3,
         compiler_params=vmem(16),
         cost_estimate=cost(3),
         name="turn_inputs",
-    )(queries, grad_out, keys, values)
+    )(queries, grad_out, keys)
 
 
 def key_gradients(blocks, turned_q, turned_g, keys, values, stats):
@@ -414,9 +402,9 @@
     def across_ka(x, by):
         return lax.ppermute(x, "ka", [(a, a ^ by) for a in range(4)])
 
-    own_stats = row_stats(blocks, queries, grad_out, keys, values)
+    own_stats, own_q, own_g, own_k, own_v = row_stats(blocks, queries, grad_out, keys, values)
     stats = [own_stats] + [across_ka(own_stats, by) for by in (2, 3, 1)]
-    turned_q, turned_g, own_k, own_v, turned_k = turned_inputs(queries, grad_out, keys, values)
+    turned_q, turned_g, turned_k = turned_inputs(own_q, own_g, own_k)
     stash, own, near_p, near_m, next_p, next_m, far_p, far_m, across = key_gradients(
         blocks, turned_q, turned_g, own_k, own_v, stats
     )

time: 59.8 us -> 59.9 us (level)
  the two profiles are of different devices: /device:TPU:24 before, /device:TPU:64 now
where the time goes in v7:
time: 59.9 us; the launch traced here: 59 us
  starting transfers between devices  25.1 us (42%)
  Pallas kernels  17.5 us (29%)
  waiting for transfers between devices  15.6 us (26%)
  between operations  0.72 us (1%)
    ppermute x6, starting transfers between devices, along_z(): lax.ppermute(x, 'pb', [(p, p // ZS * ZS + (p + by) % ZS) for p in range(p...  8.45 us
    ppermute x6, waiting for transfers between devices, along_z(): lax.ppermute(x, 'pb', [(p, p // ZS * ZS + (p + by) % ZS) for p in range(p...  7.68 us
    pallas_call x1, Pallas kernels, key_gradients(): pl.pallas_call(functools.partial(grad_kernel, width), out_shape=[array((5...  6.5 us
    ppermute x1, starting transfers between devices, on_device(): got_across = lax.ppermute(across, ('pb', 'ka'), pairs)  6.32 us
    pallas_call x1, Pallas kernels, row_stats(): pl.pallas_call(functools.partial(stat_kernel, width), out_shape=[array((2...  6.08 us
    ppermute x3, starting transfers between devices, along_y(): lax.ppermute(x, 'pb', [(p, (p // (ZS * YS) * YS + (p // ZS + by) % YS) *...  5.4 us
    ppermute x5, waiting for transfers between devices, across_ka(): return lax.ppermute(x, 'ka', [(a, a ^ by) for a in range(4)])  2.75 us
    ppermute x1, waiting for transfers between devices, on_device(): lax.ppermute(crossed, 'pb', [(p, (p + pb_size // 2) % pb_size) for p in r...  2.65 us
  transfers between devices with their start and end apart: 16, of which 7 were waited for; matrix products, arithmetic and copies ran while one was open for 0% of the time, Pallas kernels for 7%

profile of v7, /device:TPU:64, one launch (start us, length us, event | category | flops | bytes accessed | tf_op | source)
XLA Modules:
  0.0 59.0 jit_solution(4037731213563172731)
XLA Ops:
  0.6 6.1 %row_stats.1 = (f32[16,512]{1,0:T(8,128)S(1)}, bf16[512,1024]{1,0:T(8,128)(2,1)S(1)}, bf16[512,1024]{1,0:T(8,128)(2,1)S(1)}, bf16[1024,128]{1,0:T(8,128)(2,1)S(1)}, bf16[1024,128]{1,0:T(8,128)(2,1)S(1)}) custom-call(s32[2]{0:T(128)} %blocks.5, bf16[512,1024]{1,0:T(8,128)(2,1)} %q_hbm.1, bf16[512,1024]{1,0:T(8,128)(2,1)} %g_hbm.1, ...), custom_call_target="tpu_custom_call" | custom-call | tf_op jit(solution)/shard_map/row_stats/pallas_call | solution.py:335
  6.7 0.7 %collective-permute-start.2 = (f32[16,512]{1,0:T(8,128)S(1)}, f32[16,512]{1,0:T(8,128)S(1)}, u32[]{:S(2)}, u32[]{:S(2)}) collective-permute-start(f32[16,512]{1,0:T(8,128)S(1)} %get-tuple-element.42.refs_0_), channel_id=1, source_target_pairs={{0,1},{1,0},{2,3},{3,2},{4,5},{5,4},{6,7},{7,6},{8,9},{9,8},{10,11... | collective-permute-start | bytes 98312 | tf_op jit(solution)/shard_map/ppermute | solution.py:403
  7.4 1.2 %collective-permute-start.1 = (f32[16,512]{1,0:T(8,128)S(1)}, f32[16,512]{1,0:T(8,128)S(1)}, u32[]{:S(2)}, u32[]{:S(2)}) collective-permute-start(f32[16,512]{1,0:T(8,128)S(1)} %get-tuple-element.42.refs_0_), channel_id=1, source_target_pairs={{0,3},{1,2},{2,1},{3,0},{4,7},{5,6},{6,5},{7,4},{8,11},{9,10},{10,... | collective-permute-start | bytes 98312 | tf_op jit(solution)/shard_map/ppermute | solution.py:403
  8.7 0.5 collective-permute-start
  9.2 0.7 %turn_inputs.1 = (bf16[128,4096]{1,0:T(8,128)(2,1)S(1)}, bf16[128,4096]{1,0:T(8,128)(2,1)S(1)}, bf16[128,1024]{1,0:T(8,128)(2,1)S(1)}) custom-call(bf16[512,1024]{1,0:T(8,128)(2,1)S(1)} %get-tuple-element.35.q_ref, bf16[512,1024]{1,0:T(8,128)(2,1)S(1)} %get-tuple-element.36.g_ref, bf16[1024,128]{1,0:T(8,128)(2,1)S(1)} %get-tuple-element.37.k_ref), custom_call_target="tpu_custom_call" | custom-call | flops 3449999872 | tf_op jit(solution)/shard_map/turn_inputs/pallas_call | solution.py:349
  9.8 1.0 %collective-permute-done.1.refs_2_ = f32[16,512]{1,0:T(8,128)S(1)} collective-permute-done((f32[16,512]{1,0:T(8,128)S(1)}, f32[16,512]{1,0:T(8,128)S(1)}, u32[]{:S(2)}, u32[]{:S(2)}) %collective-permute-start.1) | collective-permute-done | bytes 32800 | tf_op jit(solution)/shard_map/ppermute | solution.py:403
  10.8 1.7 %collective-permute-done.refs_1_ = f32[16,512]{1,0:T(8,128)S(1)} collective-permute-done((f32[16,512]{1,0:T(8,128)S(1)}, f32[16,512]{1,0:T(8,128)S(1)}, u32[]{:S(2)}, u32[]{:S(2)}) %collective-permute-start) | collective-permute-done | bytes 32800 | tf_op jit(solution)/shard_map/ppermute | solution.py:403
  12.6 6.5 %key_grads.1 = (bf16[5,256,2048]{2,1,0:T(8,128)(2,1)S(1)}, f32[256,128]{1,0:T(8,128)S(1)}, f32[256,128]{1,0:T(8,128)S(1)}, f32[256,128]{1,0:T(8,128)S(1)}, f32[2...) custom-call(s32[2]{0:T(128)} %blocks.5, ...), custom_call_target="tpu_custom_call" | custom-call | tf_op jit(solution)/shard_map/key_grads/pallas_call | solution.py:366
  19.1 2.6 %collective-permute-start.7 = (f32[256,128]{1,0:T(8,128)S(1)}, f32[256,128]{1,0:T(8,128)S(1)}, u32[]{:S(2)}, u32[]{:S(2)}) collective-permute-start(f32[256,128]{1,0:T(8,128)S(1)} %get-tuple-element.54), channel_id=1, source_target_pairs={{0,4},{4,8},{8,12},{12,16},{16,20},{20,24},{24,28},{28,0},{32,36},... | collective-permute-start | bytes 393224 | tf_op jit(solution)/shard_map/ppermute | solution.py:418
  21.6 0.0 collective-permute-start.8
  21.6 6.3 %collective-permute-start.9 = (f32[256,128]{1,0:T(8,128)S(1)}, f32[256,128]{1,0:T(8,128)S(1)}, u32[]{:S(2)}, u32[]{:S(2)}) collective-permute-start(f32[256,128]{1,0:T(8,128)S(1)} %get-tuple-element.57), channel_id=1, source_target_pairs={{0,8},{1,25},{2,10},{3,27},{4,12},{5,29},{6,14},{7,31},{8,16},{9,1... | collective-permute-start | bytes 393224 | tf_op jit(solution)/shard_map/ppermute | solution.py:425
  28.0 2.5 %query_grads.1 = (f32[128,1024]{1,0:T(8,128)S(1)}, f32[128,1024]{1,0:T(8,128)S(1)}, f32[256,1024]{1,0:T(8,128)S(1)}, f32[256,128]{1,0:T(8,128)S(1)}, f32[256,128]{1,0:T(8,128)S(1)}) custom-call(s32[2]{0:T(128)} %blocks.5, bf16[128,1024]{1,0:T(8,128)(2,1)S(1)} %get-tuple-element.38.kt_ref, bf16[5,256,2048]{2,1,0:T(8,128)(2,1)S(1)} %get-tuple-element.43.stash, ...), custom_call_target="tpu_custom_call" | custom-call | flops 2875000064 | tf_op jit(solution)/shard_map/query_grads/pallas_call | solution.py:382
  30.5 0.1 collective-permute-start.5
  30.6 2.0 %collective-permute-start.6 = (f32[256,128]{1,0:T(8,128)S(1)}, f32[256,128]{1,0:T(8,128)S(1)}, u32[]{:S(2)}, u32[]{:S(2)}) collective-permute-start(f32[256,128]{1,0:T(8,128)S(1)} %get-tuple-element.52), channel_id=1, source_target_pairs={{0,28},{4,0},{8,4},{12,8},{16,12},{20,16},{24,20},{28,24},{32,60},... | collective-permute-start | bytes 393224 | tf_op jit(solution)/shard_map/ppermute | solution.py:418
  32.6 0.0 collective-permute-done.9.got_across
  32.7 3.6 %collective-permute-start.10 = (f32[256,128]{1,0:T(8,128)S(1)}, f32[256,128]{1,0:T(8,128)S(1)}, u32[]{:S(2)}, u32[]{:S(2)}) collective-permute-start(f32[256,128]{1,0:T(8,128)S(1)} %get-tuple-element.58), channel_id=1, source_target_pairs={{0,8},{4,12},{8,16},{12,20},{16,24},{20,28},{24,0},{28,4},{32,40},... | collective-permute-start | bytes 393224 | tf_op jit(solution)/shard_map/ppermute | solution.py:418
  36.2 0.2 collective-permute-start.11
  36.5 0.0 collective-permute-done.3.b_ref
  36.5 0.1 add_queries.1
  36.5 0.2 collective-permute-start.4
  36.8 5.8 %collective-permute-done.10.far_p = f32[256,128]{1,0:T(8,128)S(1)} collective-permute-done((f32[256,128]{1,0:T(8,128)S(1)}, f32[256,128]{1,0:T(8,128)S(1)}, u32[]{:S(2)}, u32[]{:S(2)}) %collective-permute-start.10) | collective-permute-done | bytes 131104 | tf_op jit(solution)/shard_map/ppermute | solution.py:418
  42.6 1.9 %collective-permute-done.11.far_m = f32[256,128]{1,0:T(8,128)S(1)} collective-permute-done((f32[256,128]{1,0:T(8,128)S(1)}, f32[256,128]{1,0:T(8,128)S(1)}, u32[]{:S(2)}, u32[]{:S(2)}) %collective-permute-start.11) | collective-permute-done | bytes 131104 | tf_op jit(solution)/shard_map/ppermute | solution.py:418
  44.5 1.7 %collective-permute-start.12 = (f32[2,32,128]{2,1,0:T(8,128)S(1)}, f32[2,32,128]{2,1,0:T(8,128)S(1)}, u32[]{:S(2)}, u32[]{:S(2)}) collective-permute-start(f32[2,32,128]{2,1,0:T(8,128)S(1)} %get-tuple-element.61), channel_id=1, source_target_pairs={{0,32},{4,36},{8,40},{12,44},{16,48},{20,52},{24,56},{28,60},{32,6... | collective-permute-start | bytes 98312 | tf_op jit(solution)/shard_map/ppermute | solution.py:413
  46.2 2.3 %collective-permute-start.13 = (f32[2,32,128]{2,1,0:T(8,128)S(1)}, f32[2,32,128]{2,1,0:T(8,128)S(1)}, u32[]{:S(2)}, u32[]{:S(2)}) collective-permute-start(f32[2,32,128]{2,1,0:T(8,128)S(1)} %get-tuple-element.62), channel_id=1, source_target_pairs={{0,64},{4,68},{8,72},{12,76},{16,80},{20,84},{24,88},{28,92},{32,9... | collective-permute-start | bytes 98312 | tf_op jit(solution)/shard_map/ppermute | solution.py:413
  48.5 1.3 %collective-permute-start.14 = (f32[2,32,128]{2,1,0:T(8,128)S(1)}, f32[2,32,128]{2,1,0:T(8,128)S(1)}, u32[]{:S(2)}, u32[]{:S(2)}) collective-permute-start(f32[2,32,128]{2,1,0:T(8,128)S(1)} %get-tuple-element.63), channel_id=1, source_target_pairs={{0,96},{4,100},{8,104},{12,108},{16,112},{20,116},{24,120},{28,124... | collective-permute-start | bytes 98312 | tf_op jit(solution)/shard_map/ppermute | solution.py:413
  49.9 0.0 collective-permute-done.12.from1
  49.9 1.7 %collective-permute-done.13.from2 = f32[2,32,128]{2,1,0:T(8,128)S(1)} collective-permute-done((f32[2,32,128]{2,1,0:T(8,128)S(1)}, f32[2,32,128]{2,1,0:T(8,128)S(1)}, u32[]{:S(2)}, u32[]{:S(2)}) %collective-permute-start.13) | collective-permute-done | bytes 32800 | tf_op jit(solution)/shard_map/ppermute | solution.py:413
  51.6 0.8 %collective-permute-done.14.from3 = f32[2,32,128]{2,1,0:T(8,128)S(1)} collective-permute-done((f32[2,32,128]{2,1,0:T(8,128)S(1)}, f32[2,32,128]{2,1,0:T(8,128)S(1)}, u32[]{:S(2)}, u32[]{:S(2)}) %collective-permute-start.14) | collective-permute-done | bytes 32800 | tf_op jit(solution)/shard_map/ppermute | solution.py:413
  52.4 2.3 %collective-permute-start.15 = (f32[4,32,128]{2,1,0:T(8,128)S(1)}, f32[4,32,128]{2,1,0:T(8,128)S(1)}, u32[]{:S(2)}, u32[]{:S(2)}) collective-permute-start(f32[4,32,128]{2,1,0:T(8,128)S(1)} %cross_parts.1), channel_id=1, source_target_pairs={{0,128},{4,132},{8,136},{12,140},{16,144},{20,148},{24,152},{28,15... | collective-permute-start | bytes 196616 | tf_op jit(solution)/shard_map/ppermute | solution.py:471
  54.7 0.8 %finish_queries.1 = (bf16[128,1024]{1,0:T(8,128)(2,1)}, f32[8,128]{1,0:T(8,128)S(1)}) custom-call(f32[128,1024]{1,0:T(8,128)S(1)} %get-tuple-element.46.a_ref, f32[256,1024]{1,0:T(8,128)S(1)} %collective-permute-done.3.b_ref, f32[128,1024]{1,0:T(8,128)S(1)} %collective-permute-done.4.c_ref), custom_call_target="tpu_custom_call" | custom-call | tf_op jit(solution)/shard_map/finish_queries/pallas_call | solution.py:472
  55.6 2.6 %collective-permute-done.15.crossed = f32[4,32,128]{2,1,0:T(8,128)S(1)} collective-permute-done((f32[4,32,128]{2,1,0:T(8,128)S(1)}, f32[4,32,128]{2,1,0:T(8,128)S(1)}, u32[]{:S(2)}, u32[]{:S(2)}) %collective-permute-start.15) | collective-permute-done | bytes 65568 | tf_op jit(solution)/shard_map/ppermute | solution.py:471
  58.2 0.7 %place_rows.1 = (bf16[2,64,128]{2,1,0:T(8,128)(2,1)}, bf16[2,64,128]{2,1,0:T(8,128)(2,1)}) custom-call(f32[2,32,128]{2,1,0:T(8,128)S(1)} %get-tuple-element.60.own, f32[2,32,128]{2,1,0:T(8,128)S(1)} %collective-permute-done.12.from1, f32[2,32,128]{2,1,0:T(8,128)S(1)} %collective-permute-done.13.from2, f32[2,32,128]{2,1,0:T(8,128)S(1)} %collective-permute-done.14.from3, ...), custom_call_target="tpu_custom_call" | custom-call | flops 3449999872 | tf_op jit(solution)/shard_map/place_rows/pallas_call | solution.py:480
  (10 shorter events, 0.1 us)
Async XLA Ops:
  6.7 3.1 %collective-permute-start.2 = (f32[16,512]{1,0:T(8,128)S(1)}, f32[16,512]{1,0:T(8,128)S(1)}, u32[]{:S(2)}, u32[]{:S(2)}) collective-permute-start(f32[16,512]{1,0:T(8,128)S(1)} %get-tuple-element.42.refs_0_), channel_id=1, source_target_pairs={{0,1},{1,0},{2,3},{3,2},{4,5},{5,4},{6,7},{7,6},{8,9},{9,8},{10,11... | collective-permute-start | bytes 98312 | tf_op jit(solution)/shard_map/ppermute | solution.py:403
  7.4 3.4 %collective-permute-start.1 = (f32[16,512]{1,0:T(8,128)S(1)}, f32[16,512]{1,0:T(8,128)S(1)}, u32[]{:S(2)}, u32[]{:S(2)}) collective-permute-start(f32[16,512]{1,0:T(8,128)S(1)} %get-tuple-element.42.refs_0_), channel_id=1, source_target_pairs={{0,3},{1,2},{2,1},{3,0},{4,7},{5,6},{6,5},{7,4},{8,11},{9,10},{10,... | collective-permute-start | bytes 98312 | tf_op jit(solution)/shard_map/ppermute | solution.py:403
  8.7 3.9 %collective-permute-start = (f32[16,512]{1,0:T(8,128)S(1)}, f32[16,512]{1,0:T(8,128)S(1)}, u32[]{:S(2)}, u32[]{:S(2)}) collective-permute-start(f32[16,512]{1,0:T(8,128)S(1)} %get-tuple-element.42.refs_0_), channel_id=1, source_target_pairs={{0,2},{1,3},{2,0},{3,1},{4,6},{5,7},{6,4},{7,5},{8,10},{9,11},{10,... | collective-permute-start | bytes 98312 | tf_op jit(solution)/shard_map/ppermute | solution.py:403
  19.1 13.5 %collective-permute-start.7 = (f32[256,128]{1,0:T(8,128)S(1)}, f32[256,128]{1,0:T(8,128)S(1)}, u32[]{:S(2)}, u32[]{:S(2)}) collective-permute-start(f32[256,128]{1,0:T(8,128)S(1)} %get-tuple-element.54), channel_id=1, source_target_pairs={{0,4},{4,8},{8,12},{12,16},{16,20},{20,24},{24,28},{28,0},{32,36},... | collective-permute-start | bytes 393224 | tf_op jit(solution)/shard_map/ppermute | solution.py:418
  21.6 11.0 %collective-permute-start.8 = (f32[256,128]{1,0:T(8,128)S(1)}, f32[256,128]{1,0:T(8,128)S(1)}, u32[]{:S(2)}, u32[]{:S(2)}) collective-permute-start(f32[256,128]{1,0:T(8,128)S(1)} %get-tuple-element.56), channel_id=1, source_target_pairs={{0,28},{4,0},{8,4},{12,8},{16,12},{20,16},{24,20},{28,24},{32,60},... | collective-permute-start | bytes 393224 | tf_op jit(solution)/shard_map/ppermute | solution.py:418
  21.6 11.0 %collective-permute-start.9 = (f32[256,128]{1,0:T(8,128)S(1)}, f32[256,128]{1,0:T(8,128)S(1)}, u32[]{:S(2)}, u32[]{:S(2)}) collective-permute-start(f32[256,128]{1,0:T(8,128)S(1)} %get-tuple-element.57), channel_id=1, source_target_pairs={{0,8},{1,25},{2,10},{3,27},{4,12},{5,29},{6,14},{7,31},{8,16},{9,1... | collective-permute-start | bytes 393224 | tf_op jit(solution)/shard_map/ppermute | solution.py:425
  30.5 6.3 %collective-permute-start.5 = (f32[256,128]{1,0:T(8,128)S(1)}, f32[256,128]{1,0:T(8,128)S(1)}, u32[]{:S(2)}, u32[]{:S(2)}) collective-permute-start(f32[256,128]{1,0:T(8,128)S(1)} %get-tuple-element.51), channel_id=1, source_target_pairs={{0,4},{4,8},{8,12},{12,16},{16,20},{20,24},{24,28},{28,0},{32,36},... | collective-permute-start | bytes 393224 | tf_op jit(solution)/shard_map/ppermute | solution.py:418
  30.6 6.2 %collective-permute-start.6 = (f32[256,128]{1,0:T(8,128)S(1)}, f32[256,128]{1,0:T(8,128)S(1)}, u32[]{:S(2)}, u32[]{:S(2)}) collective-permute-start(f32[256,128]{1,0:T(8,128)S(1)} %get-tuple-element.52), channel_id=1, source_target_pairs={{0,28},{4,0},{8,4},{12,8},{16,12},{20,16},{24,20},{28,24},{32,60},... | collective-permute-start | bytes 393224 | tf_op jit(solution)/shard_map/ppermute | solution.py:418
  32.6 3.9 %collective-permute-start.3 = (f32[256,1024]{1,0:T(8,128)S(1)}, f32[256,1024]{1,0:T(8,128)S(1)}, u32[]{:S(2)}, u32[]{:S(2)}) collective-permute-start(f32[256,1024]{1,0:T(8,128)S(1)} %get-tuple-element.47), channel_id=1, source_target_pairs={{0,1},{1,0},{2,3},{3,2},{4,5},{5,4},{6,7},{7,6},{8,9},{9,8},{10,11... | collective-permute-start | bytes 3145736 | tf_op jit(solution)/shard_map/ppermute | solution.py:403
  32.7 9.9 %collective-permute-start.10 = (f32[256,128]{1,0:T(8,128)S(1)}, f32[256,128]{1,0:T(8,128)S(1)}, u32[]{:S(2)}, u32[]{:S(2)}) collective-permute-start(f32[256,128]{1,0:T(8,128)S(1)} %get-tuple-element.58), channel_id=1, source_target_pairs={{0,8},{4,12},{8,16},{12,20},{16,24},{20,28},{24,0},{28,4},{32,40},... | collective-permute-start | bytes 393224 | tf_op jit(solution)/shard_map/ppermute | solution.py:418
  36.2 8.2 %collective-permute-start.11 = (f32[256,128]{1,0:T(8,128)S(1)}, f32[256,128]{1,0:T(8,128)S(1)}, u32[]{:S(2)}, u32[]{:S(2)}) collective-permute-start(f32[256,128]{1,0:T(8,128)S(1)} %get-tuple-element.59), channel_id=1, source_target_pairs={{0,24},{4,28},{8,0},{12,4},{16,8},{20,12},{24,16},{28,20},{32,56},... | collective-permute-start | bytes 393224 | tf_op jit(solution)/shard_map/ppermute | solution.py:418
  36.5 18.2 %collective-permute-start.4 = (f32[128,1024]{1,0:T(8,128)S(1)}, f32[128,1024]{1,0:T(8,128)S(1)}, u32[]{:S(2)}, u32[]{:S(2)}) collective-permute-start(f32[128,1024]{1,0:T(8,128)S(1)} %add_queries.1), channel_id=1, source_target_pairs={{0,2},{1,3},{2,0},{3,1},{4,6},{5,7},{6,4},{7,5},{8,10},{9,11},{10,... | collective-permute-start | bytes 1572872 | tf_op jit(solution)/shard_map/ppermute | solution.py:403
  44.5 5.4 %collective-permute-start.12 = (f32[2,32,128]{2,1,0:T(8,128)S(1)}, f32[2,32,128]{2,1,0:T(8,128)S(1)}, u32[]{:S(2)}, u32[]{:S(2)}) collective-permute-start(f32[2,32,128]{2,1,0:T(8,128)S(1)} %get-tuple-element.61), channel_id=1, source_target_pairs={{0,32},{4,36},{8,40},{12,44},{16,48},{20,52},{24,56},{28,60},{32,6... | collective-permute-start | bytes 98312 | tf_op jit(solution)/shard_map/ppermute | solution.py:413
  46.2 5.4 %collective-permute-start.13 = (f32[2,32,128]{2,1,0:T(8,128)S(1)}, f32[2,32,128]{2,1,0:T(8,128)S(1)}, u32[]{:S(2)}, u32[]{:S(2)}) collective-permute-start(f32[2,32,128]{2,1,0:T(8,128)S(1)} %get-tuple-element.62), channel_id=1, source_target_pairs={{0,64},{4,68},{8,72},{12,76},{16,80},{20,84},{24,88},{28,92},{32,9... | collective-permute-start | bytes 98312 | tf_op jit(solution)/shard_map/ppermute | solution.py:413
  48.5 3.9 %collective-permute-start.14 = (f32[2,32,128]{2,1,0:T(8,128)S(1)}, f32[2,32,128]{2,1,0:T(8,128)S(1)}, u32[]{:S(2)}, u32[]{:S(2)}) collective-permute-start(f32[2,32,128]{2,1,0:T(8,128)S(1)} %get-tuple-element.63), channel_id=1, source_target_pairs={{0,96},{4,100},{8,104},{12,108},{16,112},{20,116},{24,120},{28,124... | collective-permute-start | bytes 98312 | tf_op jit(solution)/shard_map/ppermute | solution.py:413
  52.4 5.8 %collective-permute-start.15 = (f32[4,32,128]{2,1,0:T(8,128)S(1)}, f32[4,32,128]{2,1,0:T(8,128)S(1)}, u32[]{:S(2)}, u32[]{:S(2)}) collective-permute-start(f32[4,32,128]{2,1,0:T(8,128)S(1)} %cross_parts.1), channel_id=1, source_target_pairs={{0,128},{4,132},{8,136},{12,140},{16,144},{20,148},{24,152},{28,15... | collective-permute-start | bytes 196616 | tf_op jit(solution)/shard_map/ppermute | solution.py:471
